TPU v7x, 32 devices: a whole 2x2x4 slice. The times are simulated.
32 devices in a mesh: fsdp: 16 (over z, y, core), ctx: 2 (over x).
Axes of the slice: x: 2, y: 2, z: 4, core: 2. Of those that a mesh axis runs over, the one named last changes fastest.
Arguments:
- tokens: bfloat16 [32, 1024, 640], P('fsdp', 'ctx'), may hold values from -6 to 6
- cotangent: bfloat16 [32, 1024, 640], P('fsdp', 'ctx'), may hold values from -6 to 6
- norm_gain: bfloat16 [640], P('fsdp'), may hold values from 0.099609375 to 1.8984375
- query_weight: bfloat16 [640, 1024], P('fsdp'), may hold values from -0.25 to 0.25
- key_weight: bfloat16 [640, 256], P('fsdp'), may hold values from -0.25 to 0.25
- value_weight: bfloat16 [640, 256], P('fsdp'), may hold values from -0.25 to 0.25
- query_norm: bfloat16 [256], P('fsdp'), may hold values from 0.099609375 to 1.8984375
- key_norm: bfloat16 [256], P('fsdp'), may hold values from 0.099609375 to 1.8984375
- output_weight: bfloat16 [1024, 640], P('fsdp'), may hold values from -0.1875 to 0.1875
- attn_post_gain: bfloat16 [640], P('fsdp'), may hold values from 0.099609375 to 1.8984375
- mlp_pre_gain: bfloat16 [640], P('fsdp'), may hold values from 0.099609375 to 1.8984375
- gate_weight: bfloat16 [640, 2048], P('fsdp'), may hold values from -0.25 to 0.25
- up_weight: bfloat16 [640, 2048], P('fsdp'), may hold values from -0.25 to 0.25
- down_weight: bfloat16 [2048, 640], P('fsdp'), may hold values from -0.125 to 0.125
- mlp_post_gain: bfloat16 [640], P('fsdp'), may hold values from 0.099609375 to 1.8984375
Outputs:
- block_output: bfloat16 [32, 1024, 640], P('fsdp', 'ctx')
- token_grad: bfloat16 [32, 1024, 640], P('fsdp', 'ctx')
- grad_norm_gain: float32 [640], P('fsdp')
- grad_query_weight: float32 [640, 1024], P('fsdp')
- grad_key_weight: float32 [640, 256], P('fsdp')
- grad_value_weight: float32 [640, 256], P('fsdp')
- grad_query_norm: float32 [256], P('fsdp')
- grad_key_norm: float32 [256], P('fsdp')
- grad_output_weight: float32 [1024, 640], P('fsdp')
- grad_attn_post_gain: float32 [640], P('fsdp')
- grad_mlp_pre_gain: float32 [640], P('fsdp')
- grad_gate_weight: float32 [640, 2048], P('fsdp')
- grad_up_weight: float32 [640, 2048], P('fsdp')
- grad_down_weight: float32 [2048, 640], P('fsdp')
- grad_mlp_post_gain: float32 [640], P('fsdp')
All inputs are finite; a program needn't handle non-finite values.
Results may differ from a plain program's by a relative error of at most 0.018.
Values may be sent and summed in bfloat16 or wider, within the bound.
No kernel may reach another device: no remote copies, remote signals or barrier semaphores. Data moves between devices by JAX's collectives and lax.ppermute only.
A program may use at most 192 MiB of HBM per device.

v0:
```python
import functools

import jax
import jax.numpy as jnp
from jax import lax
from jax.experimental import pallas as pl
from jax.experimental.pallas import tpu as pltpu
from jax.sharding import PartitionSpec as P

WINDOW = 512


EPSILON = 1e-06
MASKED = -1e30
ROOT = (2.0 / jnp.pi) ** 0.5
ROWS = 256
VMEM_BYTES = 60 * 1024 * 1024


LANES = 128


def swap(value, axis, mask):
    count = lax.axis_size(axis)
    return lax.ppermute(value, axis, [(source, source ^ mask) for source in range(count)])


def gather_pairs(shard, axis):
    count = lax.axis_size(axis)
    index = lax.axis_index(axis)
    held = shard[None]
    mask = count // 2
    while mask:
        other = swap(held, axis, mask)
        upper = (index & mask) != 0
        held = jnp.stack(
            [jnp.where(upper, other, held), jnp.where(upper, held, other)], axis=1
        ).reshape((-1,) + shard.shape)
        mask //= 2
    return held.reshape((-1,) + shard.shape[1:])


def halve(value, axis, mask, bit):
    half = value.shape[0] // 2
    parts = value.reshape((2, half) + value.shape[1:])
    kept = lax.dynamic_index_in_dim(parts, bit, 0, keepdims=False)
    sent = lax.dynamic_index_in_dim(parts, 1 - bit, 0, keepdims=False)
    return kept.astype(jnp.float32) + swap(sent, axis, mask).astype(jnp.float32)


def shared_sum(value, axis):
    count = lax.axis_size(axis)
    total = 0.0
    for step in range(1, count):
        total = total + swap(value, axis, step).astype(jnp.float32)
    return total


def scatter_pairs(shards, axis, summed):
    count = lax.axis_size(axis)
    index = lax.axis_index(axis)
    value = shards
    value = jnp.moveaxis(value.reshape((count // 2, 2) + value.shape[1:]), 1, 0).reshape(value.shape)
    value = halve(value, axis, 1, index & 1).astype(jnp.bfloat16)
    mask = count // 2
    while mask > 1:
        value = halve(value, axis, mask, (index & mask) // mask).astype(jnp.bfloat16)
        mask //= 2
    value = value[0]
    total = value.astype(jnp.float32)
    for other in summed:
        total = total + shared_sum(value, other)
    return total


def shifted(value, axis, steps):
    count = lax.axis_size(axis)
    leading, last = (max(0, -steps), min(count, count - steps))
    return lax.ppermute(value, axis, [(source, source + steps) for source in range(leading, last)])


def dot(left, right):
    return jnp.dot(left, right, preferred_element_type=jnp.float32)


def dot_nt(left, right):
    return lax.dot_general(left, right, (((1,), (1,)), ((), ())), preferred_element_type=jnp.float32)


def dot_tn(left, right):
    return lax.dot_general(left, right, (((0,), (0,)), ((), ())), preferred_element_type=jnp.float32)


def inverse_rms(rows):
    return lax.rsqrt(jnp.mean(rows * rows, axis=-1, keepdims=True) + EPSILON)


def rms_back(rows, scale, gain, grad):
    weighted = gain * grad
    inner = jnp.mean(rows * weighted, axis=-1, keepdims=True)
    return scale * weighted - rows * (scale * scale * scale * inner), grad * rows * scale


def turn(rows, cosine, sine):
    half = rows.shape[-1] // 2
    front, back = rows[:, :half], rows[:, half:]
    return jnp.concatenate([front * cosine - back * sine, back * cosine + front * sine], axis=-1)


def turn_back(rows, cosine, sine):
    return turn(rows, cosine, -sine)


def projection_kernel(head_dim, x_ref, w_ref, gain_ref, head_gain_ref, cos_ref, sin_ref, q_ref, k_ref, v_ref):
    x = x_ref[...].astype(jnp.float32)
    normed = (x * inverse_rms(x) * gain_ref[0:1, :]).astype(jnp.bfloat16)
    cosine, sine = cos_ref[...], sin_ref[...]
    queries = q_ref.shape[1]
    for start in range(0, queries + head_dim, head_dim):
        raw = dot(normed, w_ref[:, start : start + head_dim])
        gain = head_gain_ref[0:1, :] if start < queries else head_gain_ref[1:2, :]
        turned = turn(raw * inverse_rms(raw) * gain, cosine, sine).astype(jnp.bfloat16)
        if start < queries:
            q_ref[:, start : start + head_dim] = turned
        else:
            k_ref[...] = turned
    v_ref[...] = dot(normed, w_ref[:, queries + head_dim : queries + 2 * head_dim]).astype(jnp.bfloat16)


def window_parts(rows, now, before, has_before, product):
    half = rows.shape[0] // 2
    low = lax.broadcasted_iota(jnp.int32, (half, half), 1) <= lax.broadcasted_iota(
        jnp.int32, (half, half), 0
    )
    top, bottom = rows[:half], rows[half:]
    before_left = product(top, before[:half])
    before_right = product(top, before[half:])
    before_low = product(bottom, before[half:])
    if has_before is not None:
        before_left = jnp.where(has_before, before_left, MASKED)
        before_right = jnp.where(has_before, before_right, MASKED)
        before_low = jnp.where(has_before, before_low, MASKED)
    upper = jnp.concatenate([jnp.where(low, product(top, now[:half]), before_left), before_right], axis=1)
    lower = jnp.concatenate(
        [product(bottom, now[:half]), jnp.where(low, product(bottom, now[half:]), before_low)], axis=1
    )
    return jnp.concatenate([upper, lower], axis=0)


def window_split(matrix):
    half = matrix.shape[0] // 2
    low = lax.broadcasted_iota(jnp.int32, (half, half), 1) <= lax.broadcasted_iota(
        jnp.int32, (half, half), 0
    )
    first, last = matrix[:half, :half], matrix[half:, half:]
    zero = jnp.zeros_like(first)
    return (
        jnp.where(low, first, zero),
        jnp.where(low, zero, first),
        jnp.where(low, last, zero),
        jnp.where(low, zero, last),
        matrix[:half, half:],
        matrix[half:, :half],
    )


def window_apply(matrix, now, before):
    half = matrix.shape[0] // 2
    first_now, first_before, last_now, last_before, right, left = window_split(matrix)
    top = dot(first_now, now[:half]) + dot(first_before, before[:half]) + dot(right, before[half:])
    bottom = dot(left, now[:half]) + dot(last_now, now[half:]) + dot(last_before, before[half:])
    return jnp.concatenate([top, bottom], axis=0)


def window_apply_back(matrix, rows):
    half = matrix.shape[0] // 2
    first_now, first_before, last_now, last_before, right, left = window_split(matrix)
    top, bottom = rows[:half], rows[half:]
    now = jnp.concatenate([dot_tn(first_now, top) + dot_tn(left, bottom), dot_tn(last_now, bottom)], axis=0)
    before = jnp.concatenate(
        [dot_tn(first_before, top), dot_tn(right, top) + dot_tn(last_before, bottom)], axis=0
    )
    return now, before


def window_probs(query, key, key_before, has_before, scale):
    scores = window_parts(query, key, key_before, has_before, dot_nt) * scale
    terms = jnp.exp(scores - jnp.max(scores, axis=-1, keepdims=True))
    return terms * (1.0 / jnp.sum(terms, axis=-1, keepdims=True))


def attention_kernel(scale, flag_ref, q_ref, k_ref, v_ref, kb_ref, vb_ref, o_ref):
    has_before = flag_ref[0] > 0
    probs = window_probs(q_ref[...], k_ref[...], kb_ref[...], has_before, scale)
    o_ref[...] = window_apply(probs.astype(jnp.bfloat16), v_ref[...], vb_ref[...]).astype(jnp.bfloat16)


def attention_back_kernel(
    scale, flag_ref, q_ref, k_ref, v_ref, kb_ref, vb_ref, do_ref, dq_ref, dk_ref, dv_ref, dkb_ref, dvb_ref
):
    has_before = flag_ref[0] > 0
    query, grad = q_ref[...], do_ref[...]
    probs = window_probs(query, k_ref[...], kb_ref[...], has_before, scale)
    grad_probs = window_parts(grad, v_ref[...], vb_ref[...], None, dot_nt)
    inner = jnp.sum(grad_probs * probs, axis=-1, keepdims=True)
    grad_scores = (probs * (grad_probs - inner)).astype(jnp.bfloat16)
    dq_ref[...] = window_apply(grad_scores, k_ref[...], kb_ref[...]) * scale
    key_now, key_before = window_apply_back(grad_scores, query)
    value_now, value_before = window_apply_back(probs.astype(jnp.bfloat16), grad)

    @pl.when(pl.program_id(1) == 0)
    def _():
        dk_ref[...] = key_now * scale
        dkb_ref[...] = key_before * scale
        dv_ref[...] = value_now
        dvb_ref[...] = value_before

    @pl.when(pl.program_id(1) > 0)
    def _():
        dk_ref[...] += key_now * scale
        dkb_ref[...] += key_before * scale
        dv_ref[...] += value_now
        dvb_ref[...] += value_before


def middle_kernel(
    chunk,
    x_ref,
    dy_ref,
    att_ref,
    wo_ref,
    wg_ref,
    wu_ref,
    wd_ref,
    gain_ref,
    out_ref,
    dmid_ref,
    datt_ref,
    gain_grad_ref,
    go_ref,
    gg_ref,
    gu_ref,
    gd_ref,
    mlp_all,
    hidden_all,
    dmlp_all,
    dgate_all,
    dup_all,
    dattn_all,
):
    step = pl.program_id(0)
    block = x_ref.shape[0]
    rows = pl.ds(pl.multiple_of(step * block, block), block)
    ff = wg_ref.shape[1]
    gain_attn, gain_mlp, gain_final = gain_ref[1:2, :], gain_ref[2:3, :], gain_ref[3:4, :]
    x = x_ref[...].astype(jnp.float32)
    raw = dot(att_ref[rows, :], wo_ref[...])
    raw_scale = inverse_rms(raw)
    middle = x + raw * raw_scale * gain_attn
    middle_scale = inverse_rms(middle)
    mlp_low = (middle * middle_scale * gain_mlp).astype(jnp.bfloat16)
    mlp_all[rows, :] = mlp_low
    kept = []
    mlp_raw = None
    for start in range(0, ff, chunk):
        part = slice(start, start + chunk)
        gate = dot(mlp_low, wg_ref[:, part])
        up = dot(mlp_low, wu_ref[:, part])
        square = gate * gate
        bend = jnp.tanh(ROOT * (gate + 0.044715 * (gate * square)))
        half = 0.5 * (1.0 + bend)
        gelu = gate * half
        slope = half + (0.5 * ROOT) * gate * (1.0 - bend * bend) * (1.0 + (3 * 0.044715) * square)
        hidden = (gelu * up).astype(jnp.bfloat16)
        hidden_all[rows, part] = hidden
        kept.append((up * slope, gelu))
        term = dot(hidden, wd_ref[part, :])
        mlp_raw = term if mlp_raw is None else mlp_raw + term
    mlp_scale = inverse_rms(mlp_raw)
    out_ref[...] = (middle + mlp_raw * mlp_scale * gain_final).astype(jnp.bfloat16)
    dy = dy_ref[...].astype(jnp.float32)
    grad_raw, final_rows = rms_back(mlp_raw, mlp_scale, gain_final, dy)
    dmlp_low = grad_raw.astype(jnp.bfloat16)
    dmlp_all[rows, :] = dmlp_low
    grad_in = None
    for index, start in enumerate(range(0, ff, chunk)):
        part = slice(start, start + chunk)
        grad_hidden = dot_nt(dmlp_low, wd_ref[part, :])
        up_slope, gelu = kept[index]
        dgate = (grad_hidden * up_slope).astype(jnp.bfloat16)
        dup = (grad_hidden * gelu).astype(jnp.bfloat16)
        dgate_all[rows, part] = dgate
        dup_all[rows, part] = dup
        term = dot_nt(dgate, wg_ref[:, part]) + dot_nt(dup, wu_ref[:, part])
        grad_in = term if grad_in is None else grad_in + term
    grad_middle, mlp_rows = rms_back(middle, middle_scale, gain_mlp, grad_in)
    grad_middle = dy + grad_middle
    dmid_ref[...] = grad_middle
    grad_attn, attn_rows = rms_back(raw, raw_scale, gain_attn, grad_middle)
    dattn_low = grad_attn.astype(jnp.bfloat16)
    dattn_all[rows, :] = dattn_low
    datt_ref[...] = dot_nt(dattn_low, wo_ref[...]).astype(jnp.bfloat16)
    sums = [jnp.sum(part, axis=0, keepdims=True) for part in (attn_rows, mlp_rows, final_rows)]
    gain_sums = jnp.concatenate(sums + [jnp.zeros((8 - len(sums), x.shape[1]), jnp.float32)], axis=0)

    @pl.when(step == 0)
    def _():
        gain_grad_ref[...] = gain_sums

    @pl.when(step > 0)
    def _():
        gain_grad_ref[...] += gain_sums

    @pl.when(step == pl.num_programs(0) - 1)
    def _():
        for start in range(0, ff, chunk):
            part = slice(start, start + chunk)
            gg_ref[:, part] = dot_tn(mlp_all[...], dgate_all[:, part]).astype(jnp.bfloat16)
            gu_ref[:, part] = dot_tn(mlp_all[...], dup_all[:, part]).astype(jnp.bfloat16)
            gd_ref[part, :] = dot_tn(hidden_all[:, part], dmlp_all[...]).astype(jnp.bfloat16)
        for start in range(0, go_ref.shape[0], chunk):
            part = slice(start, start + chunk)
            go_ref[part, :] = dot_tn(att_ref[:, part], dattn_all[...]).astype(jnp.bfloat16)


def head_back_kernel(
    head_dim,
    x_ref,
    w_ref,
    gain_ref,
    head_gain_ref,
    cos_ref,
    sin_ref,
    dq_ref,
    dk_ref,
    dv_ref,
    dkb_ref,
    dvb_ref,
    dmid_ref,
    token_ref,
    gw_ref,
    gain_grad_ref,
    head_grad_ref,
    normed_all,
    draw_all,
):
    step = pl.program_id(0)
    block = x_ref.shape[0]
    rows = pl.ds(pl.multiple_of(step * block, block), block)
    x = x_ref[...].astype(jnp.float32)
    x_scale = inverse_rms(x)
    normed = (x * x_scale * gain_ref[0:1, :]).astype(jnp.bfloat16)
    normed_all[rows, :] = normed
    cosine, sine = cos_ref[...], sin_ref[...]
    queries = dq_ref.shape[1]
    query_rows = None
    for start in range(0, queries + head_dim, head_dim):
        part = slice(start, start + head_dim)
        raw = dot(normed, w_ref[:, part])
        scale = inverse_rms(raw)
        if start < queries:
            grad = turn_back(dq_ref[:, part], cosine, sine)
            grad_raw, head_rows = rms_back(raw, scale, head_gain_ref[0:1, :], grad)
            query_rows = head_rows if query_rows is None else query_rows + head_rows
        else:
            grad = turn_back(dk_ref[...] + dkb_ref[...].astype(jnp.float32), cosine, sine)
            grad_raw, key_rows = rms_back(raw, scale, head_gain_ref[1:2, :], grad)
        draw_all[rows, part] = grad_raw.astype(jnp.bfloat16)
    draw_all[rows, queries + head_dim : queries + 2 * head_dim] = (
        dv_ref[...] + dvb_ref[...].astype(jnp.float32)
    ).astype(jnp.bfloat16)
    grad_normed = dot_nt(draw_all[rows, :], w_ref[:, : queries + 2 * head_dim])
    grad_x, norm_rows = rms_back(x, x_scale, gain_ref[0:1, :], grad_normed)
    token_ref[...] = (dmid_ref[...] + grad_x).astype(jnp.bfloat16)

    def padded(parts):
        sums = [jnp.sum(part, axis=0, keepdims=True) for part in parts]
        return jnp.concatenate(sums + [jnp.zeros((8 - len(sums), sums[0].shape[1]), jnp.float32)], axis=0)

    norm_sums, head_sums = padded([norm_rows]), padded([query_rows, key_rows])

    @pl.when(step == 0)
    def _():
        gain_grad_ref[...] = norm_sums
        head_grad_ref[...] = head_sums

    @pl.when(step > 0)
    def _():
        gain_grad_ref[...] += norm_sums
        head_grad_ref[...] += head_sums

    @pl.when(step == pl.num_programs(0) - 1)
    def _():
        for start in range(0, gw_ref.shape[1], 512):
            part = slice(start, start + 512)
            gw_ref[:, part] = dot_tn(normed_all[...], draw_all[:, part]).astype(jnp.bfloat16)


def angle_tables(offset, length_rows, head_dim):
    half_dim = head_dim // 2
    frequency = 10000.0 ** (-(jnp.arange(half_dim).astype(jnp.float32) * 2.0 / head_dim))
    positions = (offset + jnp.arange(length_rows)).astype(jnp.float32)
    angles = positions[:, None] * frequency[None, :]
    return (jnp.cos(angles), jnp.sin(angles))


def per_device(
    tokens,
    cotangent,
    norm_gain,
    query_weight,
    key_weight,
    value_weight,
    query_norm,
    key_norm,
    output_weight,
    attn_post_gain,
    mlp_pre_gain,
    gate_weight,
    up_weight,
    down_weight,
    mlp_post_gain,
):
    fsdp = lax.axis_size("fsdp")
    rows = norm_gain.shape[0]
    head_rows = query_norm.shape[0]
    gain_columns = jnp.stack(
        [
            norm_gain,
            attn_post_gain,
            mlp_pre_gain,
            mlp_post_gain,
            jnp.pad(query_norm, (0, rows - head_rows)),
            jnp.pad(key_norm, (0, rows - head_rows)),
        ],
        axis=1,
    )
    gain_columns = jnp.pad(gain_columns, ((0, 0), (0, LANES - gain_columns.shape[1])))
    query_columns = query_weight.shape[1]
    head_dim = key_weight.shape[1]
    ff = gate_weight.shape[1]
    first_shard = jnp.concatenate([query_weight, key_weight, value_weight, gain_columns], axis=1)
    rest_shard = jnp.concatenate(
        [
            gate_weight,
            up_weight,
            down_weight.reshape(rows, -1),
            output_weight.reshape(rows, -1),
        ],
        axis=1,
    )
    first_full = gather_pairs(first_shard, "fsdp")
    rest_full = lax.all_gather(rest_shard, "fsdp", axis=0, tiled=True)
    qkv_columns = query_columns + 2 * head_dim
    query_full = first_full[:, :query_columns]
    key_full = first_full[:, query_columns : query_columns + head_dim]
    value_full = first_full[:, query_columns + head_dim : qkv_columns]
    gains = first_full[:, qkv_columns : qkv_columns + 6].astype(jnp.float32).T
    gain_first, gain_attn, gain_mlp, gain_final = gains[0], gains[1], gains[2], gains[3]
    gain_query = gains[4].reshape(fsdp, rows)[:, :head_rows].reshape(-1)
    gain_key = gains[5].reshape(fsdp, rows)[:, :head_rows].reshape(-1)
    gate_full = rest_full[:, :ff]
    up_full = rest_full[:, ff : 2 * ff]
    down_full = rest_full[:, 2 * ff : 3 * ff].reshape(ff, -1)
    output_full = rest_full[:, 3 * ff :].reshape(query_columns, -1)
    sequences, span_len, model_width = tokens.shape
    head_count = query_columns // head_dim
    assert span_len == WINDOW
    offset = lax.axis_index("ctx") * span_len
    score_scale = head_dim ** (-0.5)
    cosine_table, sine_table = angle_tables(offset, span_len, head_dim)
    has_before = jnp.full((1,), lax.axis_index("ctx"), jnp.int32)
    total = sequences * span_len
    steps = total // ROWS
    span_steps = span_len // ROWS
    x = tokens.reshape(total, model_width)
    upstream = cotangent.reshape(total, model_width)
    gain_rows = jnp.stack([gain_first, gain_attn, gain_mlp, gain_final] + [gain_final] * 4)
    head_gain_rows = jnp.stack([gain_query, gain_key] + [gain_key] * 6)
    params = pltpu.CompilerParams(vmem_limit_bytes=VMEM_BYTES)
    whole = pl.BlockSpec(memory_space=pltpu.VMEM)

    def by_rows(columns):
        return pl.BlockSpec((ROWS, columns), lambda i: (i, 0))

    table = pl.BlockSpec((ROWS, head_dim // 2), lambda i: (i % span_steps, 0))

    def bf16(*shape):
        return jax.ShapeDtypeStruct(shape, jnp.bfloat16)

    def f32(*shape):
        return jax.ShapeDtypeStruct(shape, jnp.float32)

    query_low, key_low, value_low = pl.pallas_call(
        functools.partial(projection_kernel, head_dim),
        grid=(steps,),
        in_specs=[by_rows(model_width), whole, whole, whole, table, table],
        out_specs=[by_rows(query_columns), by_rows(head_dim), by_rows(head_dim)],
        out_shape=[bf16(total, query_columns), bf16(total, head_dim), bf16(total, head_dim)],
        compiler_params=params,
        name="projection",
    )(x, first_full, gain_rows, head_gain_rows, cosine_table, sine_table)
    key_prev, value_prev = shifted((key_low, value_low), "ctx", 1)
    flag = pl.BlockSpec(memory_space=pltpu.SMEM)
    head = pl.BlockSpec((span_len, head_dim), lambda s, h: (s, h))
    shared = pl.BlockSpec((span_len, head_dim), lambda s, h: (s, 0))
    attended_low = pl.pallas_call(
        functools.partial(attention_kernel, score_scale),
        grid=(sequences, head_count),
        in_specs=[flag, head, shared, shared, shared, shared],
        out_specs=head,
        out_shape=bf16(total, query_columns),
        compiler_params=params,
        name="attention",
    )(has_before, query_low, key_low, value_low, key_prev, value_prev)
    (
        block_output,
        grad_middle,
        grad_attended,
        middle_gains,
        grad_output_weight,
        grad_gate_weight,
        grad_up_weight,
        grad_down_weight,
    ) = pl.pallas_call(
        functools.partial(middle_kernel, 512),
        grid=(steps,),
        in_specs=[by_rows(model_width), by_rows(model_width), whole, whole, whole, whole, whole, whole],
        out_specs=[by_rows(model_width), by_rows(model_width), by_rows(query_columns)] + [whole] * 5,
        out_shape=[
            bf16(total, model_width),
            f32(total, model_width),
            bf16(total, query_columns),
            f32(8, model_width),
            bf16(query_columns, model_width),
            bf16(model_width, ff),
            bf16(model_width, ff),
            bf16(ff, model_width),
        ],
        scratch_shapes=[
            pltpu.VMEM((total, model_width), jnp.bfloat16),
            pltpu.VMEM((total, ff), jnp.bfloat16),
            pltpu.VMEM((total, model_width), jnp.bfloat16),
            pltpu.VMEM((total, ff), jnp.bfloat16),
            pltpu.VMEM((total, ff), jnp.bfloat16),
            pltpu.VMEM((total, model_width), jnp.bfloat16),
        ],
        compiler_params=params,
        name="middle",
    )(x, upstream, attended_low, output_full, gate_full, up_full, down_full, gain_rows)
    grad_query, grad_key, grad_value, key_send, value_send = pl.pallas_call(
        functools.partial(attention_back_kernel, score_scale),
        grid=(sequences, head_count),
        in_specs=[flag, head, shared, shared, shared, shared, head],
        out_specs=[head, shared, shared, shared, shared],
        out_shape=[f32(total, query_columns)] + [f32(total, head_dim)] * 4,
        compiler_params=params,
        name="attention_back",
    )(has_before, query_low, key_low, value_low, key_prev, value_prev, grad_attended)
    key_back, value_back = shifted(
        (key_send.astype(jnp.bfloat16), value_send.astype(jnp.bfloat16)), "ctx", -1
    )
    token_grad, grad_first_weight, norm_gains, head_gains = pl.pallas_call(
        functools.partial(head_back_kernel, head_dim),
        grid=(steps,),
        in_specs=[by_rows(model_width), whole, whole, whole, table, table, by_rows(query_columns)]
        + [by_rows(head_dim)] * 4
        + [by_rows(model_width)],
        out_specs=[by_rows(model_width), whole, whole, whole],
        out_shape=[
            bf16(total, model_width),
            bf16(model_width, qkv_columns),
            f32(8, model_width),
            f32(8, head_dim),
        ],
        scratch_shapes=[
            pltpu.VMEM((total, model_width), jnp.bfloat16),
            pltpu.VMEM((total, qkv_columns), jnp.bfloat16),
        ],
        compiler_params=params,
        name="head_back",
    )(
        x,
        first_full,
        gain_rows,
        head_gain_rows,
        cosine_table,
        sine_table,
        grad_query,
        grad_key,
        grad_value,
        key_back,
        value_back,
        grad_middle,
    )
    grad_norm_gain = norm_gains[0]
    grad_attn_gain, grad_mlp_gain, grad_final_gain = middle_gains[0], middle_gains[1], middle_gains[2]
    grad_query_gain, grad_key_gain = head_gains[0], head_gains[1]

    def to_shards(grad):
        return grad.astype(jnp.bfloat16).reshape(fsdp, rows, -1)

    rest_grads = jnp.concatenate(
        [
            to_shards(grad_gate_weight),
            to_shards(grad_up_weight),
            to_shards(grad_down_weight),
            to_shards(grad_output_weight),
        ],
        axis=2,
    ).reshape(fsdp * rows, -1)
    rest_sum = lax.psum_scatter(rest_grads, "fsdp", scatter_dimension=0, tiled=True)
    rest_sum = rest_sum.astype(jnp.float32) + shared_sum(rest_sum, "ctx")

    def head_gain(grad):
        return jnp.pad(grad.reshape(fsdp, head_rows), ((0, 0), (0, rows - head_rows))).reshape(-1)

    gain_grads = jnp.stack(
        [
            grad_norm_gain,
            grad_attn_gain,
            grad_mlp_gain,
            grad_final_gain,
            head_gain(grad_query_gain),
            head_gain(grad_key_gain),
        ],
        axis=1,
    )
    gain_grads = jnp.pad(gain_grads, ((0, 0), (0, LANES - gain_grads.shape[1])))
    first_grads = jnp.concatenate([grad_first_weight, gain_grads.astype(jnp.bfloat16)], axis=1)
    first_sum = scatter_pairs(first_grads.reshape(fsdp, rows, -1), "fsdp", ("ctx",))
    return (
        block_output.reshape(tokens.shape),
        token_grad.reshape(tokens.shape),
        first_sum[:, qkv_columns],
        first_sum[:, :query_columns],
        first_sum[:, query_columns : query_columns + head_dim],
        first_sum[:, query_columns + head_dim : qkv_columns],
        first_sum[:head_rows, qkv_columns + 4],
        first_sum[:head_rows, qkv_columns + 5],
        rest_sum[:, 3 * ff :].reshape(output_weight.shape),
        first_sum[:, qkv_columns + 1],
        first_sum[:, qkv_columns + 2],
        rest_sum[:, :ff],
        rest_sum[:, ff : 2 * ff],
        rest_sum[:, 2 * ff : 3 * ff].reshape(down_weight.shape),
        first_sum[:, qkv_columns + 3],
    )


def solution(mesh):
    return jax.shard_map(
        per_device,
        mesh=mesh,
        in_specs=(
            P("fsdp", "ctx", None),
            P("fsdp", "ctx", None),
            P("fsdp"),
            P("fsdp", None),
            P("fsdp", None),
            P("fsdp", None),
            P("fsdp"),
            P("fsdp"),
            P("fsdp", None),
            P("fsdp"),
            P("fsdp"),
            P("fsdp", None),
            P("fsdp", None),
            P("fsdp", None),
            P("fsdp"),
        ),
        out_specs=(
            P("fsdp", "ctx", None),
            P("fsdp", "ctx", None),
            P("fsdp"),
            P("fsdp", None),
            P("fsdp", None),
            P("fsdp", None),
            P("fsdp"),
            P("fsdp"),
            P("fsdp", None),
            P("fsdp"),
            P("fsdp"),
            P("fsdp", None),
            P("fsdp", None),
            P("fsdp", None),
            P("fsdp"),
        ),
        check_vma=False,
    )
```

profile of v0, /device:TPU:0, one launch (start us, length us, event | category | flops | bytes accessed | tf_op | source)
XLA Modules:
  0.0 344.9 jit_solution(11032184942852214280)
XLA Ops:
  7.3 1.2 reshape.122
  8.5 1.0 reshape.123
  9.5 1.8 pad_maximum_fusion.3
  11.7 4.1 %collective-permute-start = (bf16[1,40,1664]{2,1,0:T(8,128)(2,1)S(1)}, bf16[1,40,1664]{2,1,0:T(8,128)(2,1)S(1)}, u32[]{:S(2)}, u32[]{:S(2)}) collective-permute-start(bf16[1,40,1664]{2,1,0:T(8,128)(2,1)S(1)} %fusion.7), channel_id=1, source_target_pairs={{0,16},{2,18},{4,20},{6,22},{8,24},{10,26},{12,28},{14,30},{16,0},... | collective-permute-start | bytes 399368 | tf_op jit(solution)/shard_map/ppermute | solution.py:25
  15.8 6.4 %collective-permute-done = bf16[1,40,1664]{2,1,0:T(8,128)(2,1)S(1)} collective-permute-done((bf16[1,40,1664]{2,1,0:T(8,128)(2,1)S(1)}, bf16[1,40,1664]{2,1,0:T(8,128)(2,1)S(1)}, u32[]{:S(2)}, u32[]{:S(2)}) %collective-permute-start) | collective-permute-done | bytes 133152 | tf_op jit(solution)/shard_map/ppermute | solution.py:25
  22.2 0.8 collective-permute-start.1
  23.0 18.7 %collective-permute-done.1 = bf16[2,40,1664]{2,1,0:T(8,128)(2,1)S(1)} collective-permute-done((bf16[2,40,1664]{2,1,0:T(8,128)(2,1)S(1)}, bf16[2,40,1664]{2,1,0:T(8,128)(2,1)S(1)}, u32[]{:S(2)}, u32[]{:S(2)}) %collective-permute-start.1) | collective-permute-done | bytes 266272 | tf_op jit(solution)/shard_map/ppermute | solution.py:25
  42.5 8.7 %collective-permute-done.2 = bf16[4,40,1664]{2,1,0:T(8,128)(2,1)S(1)} collective-permute-done((bf16[4,40,1664]{2,1,0:T(8,128)(2,1)S(1)}, bf16[4,40,1664]{2,1,0:T(8,128)(2,1)S(1)}, u32[]{:S(2)}, u32[]{:S(2)}) %collective-permute-start.2) | collective-permute-done | bytes 532512 | tf_op jit(solution)/shard_map/ppermute | solution.py:25
  51.7 1.8 multiply_sine_fusion
  53.5 0.8 collective-permute-done.3
  56.9 7.2 %projection.1 = (bf16[1024,1024]{1,0:T(8,128)(2,1)}, bf16[1024,256]{1,0:T(8,128)(2,1)}, bf16[1024,256]{1,0:T(8,128)(2,1)}) custom-call(bf16[1024,640]{1,0:T(8,128)(2,1)} %bitcast.85, bf16[640,1664]{1,0:T(8,128)(2,1)} %bitcast.83, f32[8,640]{1,0:T(8,128)} %stack.86.gain_ref, f32[8,256]{1,0:T(8,128)} %stack.87.head_gain_ref, ...), custom_call_target="tpu_custom_call" | custom-call | tf_op jit(solution)/shard_map/projection/pallas_call | solution.py:494
  64.1 2.5 collective-permute-start.4
  66.6 1.3 collective-permute-start.5
  67.9 11.2 %collective-permute-done.4.kb_ref = bf16[1024,256]{1,0:T(8,128)(2,1)S(1)} collective-permute-done((bf16[1024,256]{1,0:T(8,128)(2,1)}, bf16[1024,256]{1,0:T(8,128)(2,1)S(1)}, u32[]{:S(2)}, u32[]{:S(2)}) %collective-permute-start.4) | collective-permute-done | bytes 524320 | tf_op jit(solution)/shard_map/ppermute | solution.py:79
  79.2 10.4 %collective-permute-done.5.vb_ref = bf16[1024,256]{1,0:T(8,128)(2,1)S(1)} collective-permute-done((bf16[1024,256]{1,0:T(8,128)(2,1)}, bf16[1024,256]{1,0:T(8,128)(2,1)S(1)}, u32[]{:S(2)}, u32[]{:S(2)}) %collective-permute-start.5) | collective-permute-done | bytes 524320 | tf_op jit(solution)/shard_map/ppermute | solution.py:79
  89.6 0.8 copy-done.2
  90.4 10.3 %attention.1.att_ref = bf16[1024,1024]{1,0:T(8,128)(2,1)} custom-call(s32[1]{0:T(128)} %bitcast.2.flag_ref, bf16[1024,1024]{1,0:T(8,128)(2,1)} %get-tuple-element.35.q_ref, bf16[1024,256]{1,0:T(8,128)(2,1)} %get-tuple-element.36.k_ref, bf16[1024,256]{1,0:T(8,128)(2,1)} %get-tuple-element.37.v_ref, bf16[1024,256]{1,0:T(8,128)(2,1)} %copy-done.1, ...), custom_call_target="tpu_custom_call" | custom-call | tf_op jit(solution)/shard_map/attention/pallas_call | solution.py:507
  100.7 5.3 %fusion.10 = (bf16[640,2048]{1,0:T(8,128)(2,1)S(1)}, bf16[640,2048]{1,0:T(8,128)(2,1)}, bf16[640,2048]{1,0:T(8,128)(2,1)}) fusion(bf16[640,7168]{1,0:T(8,128)(2,1)} %all-gather.2.cloned.1.call-done), kind=kLoop, calls=%fused_computation.57 | loop fusion | bytes 15728640 | tf_op jit(solution)/shard_map/slice | solution.py:464
  106.0 4.0 %reshape.125.wd_ref = bf16[2048,640]{1,0:T(8,128)(2,1)} reshape(bf16[640,2048]{1,0:T(8,128)(2,1)S(1)} %get-tuple-element.65) | data formatting | bytes 5242880 | tf_op jit(solution)/shard_map/reshape | solution.py:464
  110.0 1.3 slice-done
  111.3 2.3 reshape.124.wo_ref
  113.6 52.8 %middle.1 = (bf16[1024,640]{1,0:T(8,128)(2,1)}, f32[1024,640]{1,0:T(8,128)}, bf16[1024,1024]{1,0:T(8,128)(2,1)}, f32[8,640]{1,0:T(8,128)}, bf16[1024,640]{1,0:T(...) custom-call(bf16[1024,640]{1,0:T(8,128)(2,1)} %bitcast.86, ...), custom_call_target="tpu_custom_call" | custom-call | tf_op jit(solution)/shard_map/middle/pallas_call | solution.py:525
  166.4 4.5 %concatenate.20 = bf16[640,2048]{1,0:T(8,128)(2,1)S(1)} reshape(bf16[2048,640]{1,0:T(8,128)(2,1)} %get-tuple-element.53) | data formatting | bytes 5242880 | tf_op jit(solution)/shard_map/concatenate | solution.py:603
  170.9 3.7 %concatenate.21 = bf16[640,1024]{1,0:T(8,128)(2,1)} reshape(bf16[1024,640]{1,0:T(8,128)(2,1)} %get-tuple-element.54) | data formatting | bytes 2621440 | tf_op jit(solution)/shard_map/concatenate | solution.py:603
  174.6 7.6 %pad_maximum_fusion = bf16[640,7168]{1,0:T(8,128)(2,1)} fusion(bf16[640,1024]{1,0:T(8,128)(2,1)} %concatenate.21, bf16[640,2048]{1,0:T(8,128)(2,1)S(1)} %concatenate.20, bf16[640,2048]{1,0:T(8,128)(2,1)} %get-tuple-element.52, bf16[640,2048]{1,0:T(8,128)(2,1)} %get-tuple-element.51), kind=kLoop, calls=%fused_computation | loop fusion | flops 36700160 | bytes 18350080 | tf_op jit(solution)/shard_map/concatenate | solution.py:603
  182.2 18.1 %attention_back.1 = (f32[1024,1024]{1,0:T(8,128)}, f32[1024,256]{1,0:T(8,128)}, f32[1024,256]{1,0:T(8,128)}, f32[1024,256]{1,0:T(8,128)}, f32[1024,256]{1,0:T(8,128)}) custom-call(s32[1]{0:T(128)} %bitcast.2.flag_ref, bf16[1024,1024]{1,0:T(8,128)(2,1)} %get-tuple-element.35.q_ref, bf16[1024,256]{1,0:T(8,128)(2,1)} %get-tuple-element.36.k_ref, ...), custom_call_target="tpu_custom_call" | custom-call | tf_op jit(solution)/shard_map/attention_back/pallas_call | solution.py:551
  200.4 1.4 convert_element_type.93
  201.8 1.3 collective-permute-start.6
  203.1 1.3 collective-permute-start.7
  204.5 14.0 %collective-permute-done.6.dkb_ref = bf16[1024,256]{1,0:T(8,128)(2,1)S(1)} collective-permute-done((bf16[1024,256]{1,0:T(8,128)(2,1)S(1)}, bf16[1024,256]{1,0:T(8,128)(2,1)S(1)}, u32[]{:S(2)}, u32[]{:S(2)}) %collective-permute-start.6) | collective-permute-done | bytes 524320 | tf_op jit(solution)/shard_map/ppermute | solution.py:79
  218.5 9.9 %collective-permute-done.7.dvb_ref = bf16[1024,256]{1,0:T(8,128)(2,1)S(1)} collective-permute-done((bf16[1024,256]{1,0:T(8,128)(2,1)S(1)}, bf16[1024,256]{1,0:T(8,128)(2,1)S(1)}, u32[]{:S(2)}, u32[]{:S(2)}) %collective-permute-start.7) | collective-permute-done | bytes 524320 | tf_op jit(solution)/shard_map/ppermute | solution.py:79
  228.4 0.8 copy-done.5
  229.2 14.8 %head_back.1 = (bf16[1024,640]{1,0:T(8,128)(2,1)}, bf16[640,1536]{1,0:T(8,128)(2,1)}, f32[8,640]{1,0:T(8,128)}, f32[8,256]{1,0:T(8,128)}) custom-call(bf16[1024,640]{1,0:T(8,128)(2,1)} %bitcast.87, bf16[640,1664]{1,0:T(8,128)(2,1)} %bitcast.84, f32[8,640]{1,0:T(8,128)} %stack.86.gain_ref, f32[8,256]{1,0:T(8,128)} %stack.87.head_gain_ref, ...), custom_call_target="tpu_custom_call" | custom-call | tf_op jit(solution)/shard_map/head_back/pallas_call | solution.py:563
  246.1 1.7 fusion.1
  248.0 2.8 collective-permute-done.8
  250.8 1.5 fusion.2
  252.3 8.8 %collective-permute-start.9 = (bf16[4,40,1664]{2,1,0:T(8,128)(2,1)S(1)}, bf16[4,40,1664]{2,1,0:T(8,128)(2,1)S(1)}, u32[]{:S(2)}, u32[]{:S(2)}) collective-permute-start(bf16[4,40,1664]{2,1,0:T(8,128)(2,1)S(1)} %dynamic-slice_bitcast_fusion.1), channel_id=1, source_target_pairs={{0,16},{2,18},{4,20},{6,22},{8,24},{10,26},{12,28},{14,30},{16,0},... | collective-permute-start | bytes 1597448 | tf_op jit(solution)/shard_map/ppermute | solution.py:25
  261.1 29.4 %collective-permute-done.9 = bf16[4,40,1664]{2,1,0:T(8,128)(2,1)S(1)} collective-permute-done((bf16[4,40,1664]{2,1,0:T(8,128)(2,1)S(1)}, bf16[4,40,1664]{2,1,0:T(8,128)(2,1)S(1)}, u32[]{:S(2)}, u32[]{:S(2)}) %collective-permute-start.9) | collective-permute-done | bytes 532512 | tf_op jit(solution)/shard_map/ppermute | solution.py:25
  290.8 11.4 %collective-permute-done.10 = bf16[2,40,1664]{2,1,0:T(8,128)(2,1)S(1)} collective-permute-done((bf16[2,40,1664]{2,1,0:T(8,128)(2,1)S(1)}, bf16[2,40,1664]{2,1,0:T(8,128)(2,1)S(1)}, u32[]{:S(2)}, u32[]{:S(2)}) %collective-permute-start.10) | collective-permute-done | bytes 266272 | tf_op jit(solution)/shard_map/ppermute | solution.py:25
  302.3 1.5 collective-permute-start.11
  303.8 3.6 %collective-permute-done.11 = bf16[1,40,1664]{2,1,0:T(8,128)(2,1)S(1)} collective-permute-done((bf16[1,40,1664]{2,1,0:T(8,128)(2,1)S(1)}, bf16[1,40,1664]{2,1,0:T(8,128)(2,1)S(1)}, u32[]{:S(2)}, u32[]{:S(2)}) %collective-permute-start.11) | collective-permute-done | bytes 133152 | tf_op jit(solution)/shard_map/ppermute | solution.py:25
  307.4 1.5 collective-permute-start.12
  308.9 10.9 %reduce-scatter.2.cloned.1.call-done = bf16[40,7168]{1,0:T(8,128)(2,1)} async-done(((bf16[640,7168]{1,0:T(8,128)(2,1)}), bf16[40,7168]{1,0:T(8,128)(2,1)}) %reduce-scatter.2.cloned.1.call-update) | async-done | bytes 573456 | tf_op jit(solution)/shard_map/reduce_scatter | solution.py:612
  319.8 1.4 collective-permute-start.13
  324.0 10.5 %collective-permute-done.13 = bf16[40,7168]{1,0:T(8,128)(2,1)S(1)} collective-permute-done((bf16[40,7168]{1,0:T(8,128)(2,1)}, bf16[40,7168]{1,0:T(8,128)(2,1)S(1)}, u32[]{:S(2)}, u32[]{:S(2)}) %collective-permute-start.13) | collective-permute-done | bytes 573472 | tf_op jit(solution)/shard_map/ppermute | solution.py:25
  334.4 1.2 convert_add_fusion.1
  335.6 0.9 fusion.11
  336.5 0.8 reshape.131
  (96 shorter events, 10.3 us)
Async XLA Ops:
  7.2 4.2 %copy-start.15 = (bf16[16]{0:T(256)(128)(2,1)S(1)}, bf16[16]{0:T(256)(128)(2,1)}, u32[]{:S(2)}) copy-start(bf16[16]{0:T(256)(128)(2,1)} %param.21) | copy-start | bytes 100
  7.2 4.2 %copy-start.14 = (bf16[16]{0:T(256)(128)(2,1)S(1)}, bf16[16]{0:T(256)(128)(2,1)}, u32[]{:S(2)}) copy-start(bf16[16]{0:T(256)(128)(2,1)} %param.22) | copy-start | bytes 100
  7.2 4.2 %copy-start.10 = (bf16[40]{0:T(256)(128)(2,1)S(1)}, bf16[40]{0:T(256)(128)(2,1)}, u32[]{:S(2)}) copy-start(bf16[40]{0:T(256)(128)(2,1)} %param.17) | copy-start | bytes 244
  7.2 4.2 %copy-start.11 = (bf16[40]{0:T(256)(128)(2,1)S(1)}, bf16[40]{0:T(256)(128)(2,1)}, u32[]{:S(2)}) copy-start(bf16[40]{0:T(256)(128)(2,1)} %param.24) | copy-start | bytes 244
  7.2 4.2 %copy-start.12 = (bf16[40]{0:T(256)(128)(2,1)S(1)}, bf16[40]{0:T(256)(128)(2,1)}, u32[]{:S(2)}) copy-start(bf16[40]{0:T(256)(128)(2,1)} %param.25) | copy-start | bytes 244
  7.2 4.2 %copy-start.13 = (bf16[40]{0:T(256)(128)(2,1)S(1)}, bf16[40]{0:T(256)(128)(2,1)}, u32[]{:S(2)}) copy-start(bf16[40]{0:T(256)(128)(2,1)} %param.29) | copy-start | bytes 244
  7.2 4.4 %copy-start.6 = (bf16[40,1024]{1,0:T(8,128)(2,1)S(1)}, bf16[40,1024]{1,0:T(8,128)(2,1)}, u32[]{:S(2)}) copy-start(bf16[40,1024]{1,0:T(8,128)(2,1)} %param.18) | copy-start | bytes 245764
  7.3 4.4 %copy-start.8 = (bf16[40,256]{1,0:T(8,128)(2,1)S(1)}, bf16[40,256]{1,0:T(8,128)(2,1)}, u32[]{:S(2)}) copy-start(bf16[40,256]{1,0:T(8,128)(2,1)} %param.19) | copy-start | bytes 61444
  7.3 4.4 %copy-start.7 = (bf16[40,256]{1,0:T(8,128)(2,1)S(1)}, bf16[40,256]{1,0:T(8,128)(2,1)}, u32[]{:S(2)}) copy-start(bf16[40,256]{1,0:T(8,128)(2,1)} %param.20) | copy-start | bytes 61444
  7.3 93.4 %all-gather.2.cloned.1.call-start = ((), (), s32[]{:S(2)}) async-start(), calls=%async_computation.1 | async-start | bytes 9748480 | tf_op jit(solution)/shard_map/all_gather | solution.py:453
  11.4 308.5 %reduce-scatter.2.cloned.1.call-start = ((), (), s32[]{:S(2)}) async-start(), calls=%async_computation.2 | async-start | bytes 9748480 | tf_op jit(solution)/shard_map/reduce_scatter | solution.py:612
  11.7 10.5 %collective-permute-start = (bf16[1,40,1664]{2,1,0:T(8,128)(2,1)S(1)}, bf16[1,40,1664]{2,1,0:T(8,128)(2,1)S(1)}, u32[]{:S(2)}, u32[]{:S(2)}) collective-permute-start(bf16[1,40,1664]{2,1,0:T(8,128)(2,1)S(1)} %fusion.7), channel_id=1, source_target_pairs={{0,16},{2,18},{4,20},{6,22},{8,24},{10,26},{12,28},{14,30},{16,0},... | collective-permute-start | bytes 399368 | tf_op jit(solution)/shard_map/ppermute | solution.py:25
  22.2 19.5 %collective-permute-start.1 = (bf16[2,40,1664]{2,1,0:T(8,128)(2,1)S(1)}, bf16[2,40,1664]{2,1,0:T(8,128)(2,1)S(1)}, u32[]{:S(2)}, u32[]{:S(2)}) collective-permute-start(bf16[2,40,1664]{2,1,0:T(8,128)(2,1)S(1)} %maximum_bitcast_fusion), channel_id=1, source_target_pairs={{0,8},{2,10},{4,12},{6,14},{8,0},{10,2},{12,4},{14,6},{16,24},{18,... | collective-permute-start | bytes 798728 | tf_op jit(solution)/shard_map/ppermute | solution.py:25
  41.9 9.3 %collective-permute-start.2 = (bf16[4,40,1664]{2,1,0:T(8,128)(2,1)S(1)}, bf16[4,40,1664]{2,1,0:T(8,128)(2,1)S(1)}, u32[]{:S(2)}, u32[]{:S(2)}) collective-permute-start(bf16[4,40,1664]{2,1,0:T(8,128)(2,1)S(1)} %bitcast.93), channel_id=1, source_target_pairs={{0,4},{2,6},{4,0},{6,2},{8,12},{10,14},{12,8},{14,10},{16,20},{18,... | collective-permute-start | bytes 1597448 | tf_op jit(solution)/shard_map/ppermute | solution.py:25
  51.6 2.7 collective-permute-start.3
  55.0 1.9 copy-start
  64.1 15.1 %collective-permute-start.4 = (bf16[1024,256]{1,0:T(8,128)(2,1)}, bf16[1024,256]{1,0:T(8,128)(2,1)S(1)}, u32[]{:S(2)}, u32[]{:S(2)}) collective-permute-start(bf16[1024,256]{1,0:T(8,128)(2,1)} %get-tuple-element.36.k_ref), channel_id=1, source_target_pairs={{0,1},{2,3},{4,5},{6,7},{8,9},{10,11},{12,13},{14,15},{16,17},{18,... | collective-permute-start | bytes 1572872 | tf_op jit(solution)/shard_map/ppermute | solution.py:79
  66.6 23.0 %collective-permute-start.5 = (bf16[1024,256]{1,0:T(8,128)(2,1)}, bf16[1024,256]{1,0:T(8,128)(2,1)S(1)}, u32[]{:S(2)}, u32[]{:S(2)}) collective-permute-start(bf16[1024,256]{1,0:T(8,128)(2,1)} %get-tuple-element.37.v_ref), channel_id=1, source_target_pairs={{0,1},{2,3},{4,5},{6,7},{8,9},{10,11},{12,13},{14,15},{16,17},{18,... | collective-permute-start | bytes 1572872 | tf_op jit(solution)/shard_map/ppermute | solution.py:79
  79.1 10.5 %copy-start.1 = (bf16[1024,256]{1,0:T(8,128)(2,1)}, bf16[1024,256]{1,0:T(8,128)(2,1)S(1)}, u32[]{:S(2)}) copy-start(bf16[1024,256]{1,0:T(8,128)(2,1)S(1)} %collective-permute-done.4.kb_ref) | copy-start | bytes 1572868
  89.6 0.8 copy-start.2
  110.0 1.3 slice-start
  200.4 2.7 copy-start.3
  200.4 4.1 %copy-start.9 = (f32[8,640]{1,0:T(8,128)S(1)}, f32[8,640]{1,0:T(8,128)}, u32[]{:S(2)}) copy-start(f32[8,640]{1,0:T(8,128)} %get-tuple-element.49) | copy-start | bytes 61444
  201.8 16.7 %collective-permute-start.6 = (bf16[1024,256]{1,0:T(8,128)(2,1)S(1)}, bf16[1024,256]{1,0:T(8,128)(2,1)S(1)}, u32[]{:S(2)}, u32[]{:S(2)}) collective-permute-start(bf16[1024,256]{1,0:T(8,128)(2,1)S(1)} %convert_element_type.93), channel_id=1, source_target_pairs={{1,0},{3,2},{5,4},{7,6},{9,8},{11,10},{13,12},{15,14},{17,16},{19,... | collective-permute-start | bytes 1572872 | tf_op jit(solution)/shard_map/ppermute | solution.py:79
  203.1 25.3 %collective-permute-start.7 = (bf16[1024,256]{1,0:T(8,128)(2,1)S(1)}, bf16[1024,256]{1,0:T(8,128)(2,1)S(1)}, u32[]{:S(2)}, u32[]{:S(2)}) collective-permute-start(bf16[1024,256]{1,0:T(8,128)(2,1)S(1)} %convert_element_type.94), channel_id=1, source_target_pairs={{1,0},{3,2},{5,4},{7,6},{9,8},{11,10},{13,12},{15,14},{17,16},{19,... | collective-permute-start | bytes 1572872 | tf_op jit(solution)/shard_map/ppermute | solution.py:79
  218.5 9.9 %copy-start.4 = (bf16[1024,256]{1,0:T(8,128)(2,1)}, bf16[1024,256]{1,0:T(8,128)(2,1)S(1)}, u32[]{:S(2)}) copy-start(bf16[1024,256]{1,0:T(8,128)(2,1)S(1)} %collective-permute-done.6.dkb_ref) | copy-start | bytes 1572868
  228.4 0.8 copy-start.5
  247.9 2.9 collective-permute-start.8
  252.3 38.2 %collective-permute-start.9 = (bf16[4,40,1664]{2,1,0:T(8,128)(2,1)S(1)}, bf16[4,40,1664]{2,1,0:T(8,128)(2,1)S(1)}, u32[]{:S(2)}, u32[]{:S(2)}) collective-permute-start(bf16[4,40,1664]{2,1,0:T(8,128)(2,1)S(1)} %dynamic-slice_bitcast_fusion.1), channel_id=1, source_target_pairs={{0,16},{2,18},{4,20},{6,22},{8,24},{10,26},{12,28},{14,30},{16,0},... | collective-permute-start | bytes 1597448 | tf_op jit(solution)/shard_map/ppermute | solution.py:25
  290.7 11.5 %collective-permute-start.10 = (bf16[2,40,1664]{2,1,0:T(8,128)(2,1)S(1)}, bf16[2,40,1664]{2,1,0:T(8,128)(2,1)S(1)}, u32[]{:S(2)}, u32[]{:S(2)}) collective-permute-start(bf16[2,40,1664]{2,1,0:T(8,128)(2,1)S(1)} %dynamic-slice_bitcast_fusion.2), channel_id=1, source_target_pairs={{0,8},{2,10},{4,12},{6,14},{8,0},{10,2},{12,4},{14,6},{16,24},{18,... | collective-permute-start | bytes 798728 | tf_op jit(solution)/shard_map/ppermute | solution.py:25
  302.3 5.1 %collective-permute-start.11 = (bf16[1,40,1664]{2,1,0:T(8,128)(2,1)S(1)}, bf16[1,40,1664]{2,1,0:T(8,128)(2,1)S(1)}, u32[]{:S(2)}, u32[]{:S(2)}) collective-permute-start(bf16[1,40,1664]{2,1,0:T(8,128)(2,1)S(1)} %constant_dynamic-slice_fusion), channel_id=1, source_target_pairs={{0,4},{2,6},{4,0},{6,2},{8,12},{10,14},{12,8},{14,10},{16,20},{18,... | collective-permute-start | bytes 399368 | tf_op jit(solution)/shard_map/ppermute | solution.py:25
  307.4 13.8 %collective-permute-start.12 = (bf16[40,1664]{1,0:T(8,128)(2,1)S(1)}, bf16[40,1664]{1,0:T(8,128)(2,1)S(1)}, u32[]{:S(2)}, u32[]{:S(2)}) collective-permute-start(bf16[40,1664]{1,0:T(8,128)(2,1)S(1)} %fusion.8), channel_id=1, source_target_pairs={{0,1},{1,0},{2,3},{3,2},{4,5},{5,4},{6,7},{7,6},{8,9},{9,8},{10,11... | collective-permute-start | bytes 399368 | tf_op jit(solution)/shard_map/ppermute | solution.py:25
  319.8 14.6 %collective-permute-start.13 = (bf16[40,7168]{1,0:T(8,128)(2,1)}, bf16[40,7168]{1,0:T(8,128)(2,1)S(1)}, u32[]{:S(2)}, u32[]{:S(2)}) collective-permute-start(bf16[40,7168]{1,0:T(8,128)(2,1)} %reduce-scatter.2.cloned.1.call-done), channel_id=1, source_target_pairs={{0,1},{1,0},{2,3},{3,2},{4,5},{5,4},{6,7},{7,6},{8,9},{9,8},{10,11... | collective-permute-start | bytes 1720328 | tf_op jit(solution)/shard_map/ppermute | solution.py:25
Sparse Core Ops, SparseCore 0:
  11.5 87.3 all-gather.1
  182.3 137.4 reduce-scatter.1
where the time goes:
time: 346 us; the launch traced here: 345 us
  waiting for transfers between devices  149 us (43%)
  Pallas kernels  103 us (30%)
  local copies, waits for them, and re-layouts  33.9 us (10%)
  starting transfers between devices  25.4 us (7%)
  other arithmetic  19.1 us (6%)
  between operations  14.6 us (4%)
    ppermute x10, waiting for transfers between devices, swap(): lax.ppermute(value, axis, [(source, source ^ mask) for source in range(co...  92.2 us
    pallas_call x1, Pallas kernels, per_device(): pl.pallas_call(functools.partial(middle_kernel, 512), grid=(steps,), in_s...  52.8 us
    ppermute x4, waiting for transfers between devices, shifted(): lax.ppermute(value, axis, [(source, source + steps) for source in range(l...  45.6 us
    ppermute x10, starting transfers between devices, swap(): lax.ppermute(value, axis, [(source, source ^ mask) for source in range(co...  18.9 us
    pallas_call x1, Pallas kernels, per_device(): pl.pallas_call(functools.partial(attention_back_kernel, score_scale), gri...  18.1 us
    pallas_call x1, Pallas kernels, per_device(): pl.pallas_call(functools.partial(head_back_kernel, head_dim), grid=(steps...  14.8 us
    reduce_scatter x1, waiting for transfers between devices, per_device(): lax.psum_scatter(rest_grads, 'fsdp', scatter_dimension=0, tiled=True)  10.9 us
    pallas_call x1, Pallas kernels, per_device(): pl.pallas_call(functools.partial(attention_kernel, score_scale), grid=(se...  10.3 us
  transfers between devices with their start and end apart: 16, of which 14 were waited for; matrix products, arithmetic and copies ran while one was open for 4% of the time, Pallas kernels for 15%

commit v1 on v0

v1 whole, which is shorter than its diff:
```python
import functools

import jax
import jax.numpy as jnp
from jax import lax
from jax.experimental import pallas as pl
from jax.experimental.pallas import tpu as pltpu
from jax.sharding import PartitionSpec as P

WINDOW = 512


EPSILON = 1e-06
MASKED = -1e30
ROOT = (2.0 / jnp.pi) ** 0.5
ROWS = 256
VMEM_BYTES = 60 * 1024 * 1024


LANES = 128


def swap(value, axis, mask):
    count = lax.axis_size(axis)
    return lax.ppermute(value, axis, [(source, source ^ mask) for source in range(count)])


def after(value, *others):
    return lax.optimization_barrier((value, others))[0]


def widen(held, axis, mask, *others):
    return jnp.concatenate([held, after(swap(held, axis, mask), *others)], axis=0)


def places(axis):
    count = lax.axis_size(axis)
    relative = jnp.arange(count, dtype=jnp.int32) ^ lax.axis_index(axis)
    place = jnp.zeros((count,), jnp.int32)
    low, high = 0, count // 2
    while high > 1:
        place = place + jnp.where((relative & high) != 0, 1 << low, 0)
        low, high = low + 1, high // 2
    return place


def cost(flops, spent):
    return pl.CostEstimate(flops=int(flops / spent / 16), bytes_accessed=0, transcendentals=0)


def add(left, right):
    return (left.astype(jnp.float32) + right.astype(jnp.float32)).astype(jnp.bfloat16)


def folded(value, axis, mask, dim):
    kept, sent = jnp.split(value, 2, axis=dim)
    return kept, swap(sent, axis, mask)


def other_spans(value, axis):
    mask = 2
    while mask < lax.axis_size(axis):
        value = add(value, swap(value, axis, mask))
        mask *= 2
    return value


def shifted(value, axis, steps):
    count = lax.axis_size(axis)
    leading, last = (max(0, -steps), min(count, count - steps))
    return lax.ppermute(value, axis, [(source, source + steps) for source in range(leading, last)])


def dot(left, right):
    return jnp.dot(left, right, preferred_element_type=jnp.float32)


def dot_nt(left, right):
    return lax.dot_general(left, right, (((1,), (1,)), ((), ())), preferred_element_type=jnp.float32)


def dot_tn(left, right):
    return lax.dot_general(left, right, (((0,), (0,)), ((), ())), preferred_element_type=jnp.float32)


def inverse_rms(rows):
    return lax.rsqrt(jnp.mean(rows * rows, axis=-1, keepdims=True) + EPSILON)


def rms_back(rows, scale, gain, grad):
    weighted = gain * grad
    inner = jnp.mean(rows * weighted, axis=-1, keepdims=True)
    return scale * weighted - rows * (scale * scale * scale * inner), grad * rows * scale


def turn(rows, cosine, sine):
    half = rows.shape[-1] // 2
    front, back = rows[:, :half], rows[:, half:]
    return jnp.concatenate([front * cosine - back * sine, back * cosine + front * sine], axis=-1)


def turn_back(rows, cosine, sine):
    return turn(rows, cosine, -sine)


def each_core(core, body):
    for value in (0, 1):
        pl.when(core == value)(functools.partial(body, value))


def whole_block(ref, place):
    return [ref[place]]


def join_pairs(out_ref, near_ref, far_ref, core, info_ref, rows, read=whole_block):
    pairs = 1
    while (2 * rows * pairs) % 16:
        pairs *= 2
    size = 2 * rows * pairs

    def body(value):
        first, second = (near_ref, far_ref) if value == 0 else (far_ref, near_ref)

        def group(index, carry):
            blocks = []
            for pair in range(pairs):
                place = info_ref[2 * (index * pairs + pair)]
                blocks += read(first, place) + read(second, place)
            if rows % 8:
                blocks = [block.astype(jnp.float32) for block in blocks]
            lines = pl.ds(pl.multiple_of(index * size, size), size)
            out_ref[lines, :] = jnp.concatenate(blocks, axis=0).astype(jnp.bfloat16)
            return carry

        lax.fori_loop(0, near_ref.shape[0] // pairs, group, 0)

    each_core(core, body)


def projection_kernel(
    head_dim,
    columns,
    x_ref,
    xb_ref,
    near_ref,
    far_ref,
    pick_ref,
    info_ref,
    cos_ref,
    sin_ref,
    cosb_ref,
    sinb_ref,
    q_ref,
    k_ref,
    v_ref,
    kb_ref,
    vb_ref,
    w_ref,
    gain_ref,
    head_gain_ref,
    all_ref,
):
    count = info_ref.shape[0] - 3

    @pl.when(pl.program_id(0) == 0)
    def _():
        join_pairs(all_ref, near_ref, far_ref, info_ref[count], info_ref, near_ref.shape[1])
        w_ref[...] = all_ref[:, :columns]
        gains = all_ref[:, columns : columns + LANES].astype(jnp.float32).T[:8]
        gain_ref[...] = gains
        head_gain_ref[...] = dot(gains.astype(jnp.bfloat16), pick_ref[...])

    gain = gain_ref[0:1, :]
    queries = q_ref.shape[1]
    x = x_ref[...].astype(jnp.float32)
    normed = (x * inverse_rms(x) * gain).astype(jnp.bfloat16)
    x = xb_ref[...].astype(jnp.float32)
    normed_before = (x * inverse_rms(x) * gain).astype(jnp.bfloat16)
    key_part = slice(queries, queries + head_dim)
    value_part = slice(queries + head_dim, queries + 2 * head_dim)

    def turned(rows, part, head_gain, cosine, sine):
        raw = dot(rows, w_ref[:, part])
        return turn(raw * inverse_rms(raw) * head_gain, cosine, sine).astype(jnp.bfloat16)

    for start in range(0, queries, head_dim):
        part = slice(start, start + head_dim)
        q_ref[:, part] = turned(normed, part, head_gain_ref[4:5, :], cos_ref[...], sin_ref[...])
    k_ref[...] = turned(normed, key_part, head_gain_ref[5:6, :], cos_ref[...], sin_ref[...])
    v_ref[...] = dot(normed, w_ref[:, value_part]).astype(jnp.bfloat16)
    kb_ref[...] = turned(normed_before, key_part, head_gain_ref[5:6, :], cosb_ref[...], sinb_ref[...])
    vb_ref[...] = dot(normed_before, w_ref[:, value_part]).astype(jnp.bfloat16)


def window_parts(rows, now, before, has_before, product):
    half = rows.shape[0] // 2
    low = lax.broadcasted_iota(jnp.int32, (half, half), 1) <= lax.broadcasted_iota(
        jnp.int32, (half, half), 0
    )
    top, bottom = rows[:half], rows[half:]
    before_left = product(top, before[:half])
    before_right = product(top, before[half:])
    before_low = product(bottom, before[half:])
    if has_before is not None:
        before_left = jnp.where(has_before, before_left, MASKED)
        before_right = jnp.where(has_before, before_right, MASKED)
        before_low = jnp.where(has_before, before_low, MASKED)
    upper = jnp.concatenate([jnp.where(low, product(top, now[:half]), before_left), before_right], axis=1)
    lower = jnp.concatenate(
        [product(bottom, now[:half]), jnp.where(low, product(bottom, now[half:]), before_low)], axis=1
    )
    return jnp.concatenate([upper, lower], axis=0)


def window_split(matrix):
    half = matrix.shape[0] // 2
    low = lax.broadcasted_iota(jnp.int32, (half, half), 1) <= lax.broadcasted_iota(
        jnp.int32, (half, half), 0
    )
    first, last = matrix[:half, :half], matrix[half:, half:]
    zero = jnp.zeros_like(first)
    return (
        jnp.where(low, first, zero),
        jnp.where(low, zero, first),
        jnp.where(low, last, zero),
        jnp.where(low, zero, last),
        matrix[:half, half:],
        matrix[half:, :half],
    )


def window_apply(matrix, now, before):
    half = matrix.shape[0] // 2
    first_now, first_before, last_now, last_before, right, left = window_split(matrix)
    top = dot(first_now, now[:half]) + dot(first_before, before[:half]) + dot(right, before[half:])
    bottom = dot(left, now[:half]) + dot(last_now, now[half:]) + dot(last_before, before[half:])
    return jnp.concatenate([top, bottom], axis=0)


def window_apply_back(matrix, rows):
    half = matrix.shape[0] // 2
    first_now, first_before, last_now, last_before, right, left = window_split(matrix)
    top, bottom = rows[:half], rows[half:]
    now = jnp.concatenate([dot_tn(first_now, top) + dot_tn(left, bottom), dot_tn(last_now, bottom)], axis=0)
    before = jnp.concatenate(
        [dot_tn(first_before, top), dot_tn(right, top) + dot_tn(last_before, bottom)], axis=0
    )
    return now, before


def window_probs(query, key, key_before, has_before, scale):
    scores = window_parts(query, key, key_before, has_before, dot_nt) * scale
    terms = jnp.exp(scores - jnp.max(scores, axis=-1, keepdims=True))
    return terms * (1.0 / jnp.sum(terms, axis=-1, keepdims=True))


def attention_kernel(scale, flag_ref, q_ref, k_ref, v_ref, kb_ref, vb_ref, o_ref):
    has_before = flag_ref[flag_ref.shape[0] - 1] > 0
    probs = window_probs(q_ref[...], k_ref[...], kb_ref[...], has_before, scale)
    o_ref[...] = window_apply(probs.astype(jnp.bfloat16), v_ref[...], vb_ref[...]).astype(jnp.bfloat16)


def attention_back_kernel(scale, flag_ref, q_ref, k_ref, v_ref, kb_ref, vb_ref, do_ref, *refs):
    dq_ref, dk_ref, dv_ref, dkb_ref, dvb_ref = refs[-5:]
    has_before = flag_ref[flag_ref.shape[0] - 1] > 0
    query, grad = q_ref[...], do_ref[...]
    probs = window_probs(query, k_ref[...], kb_ref[...], has_before, scale)
    grad_probs = window_parts(grad, v_ref[...], vb_ref[...], None, dot_nt)
    inner = jnp.sum(grad_probs * probs, axis=-1, keepdims=True)
    grad_scores = (probs * (grad_probs - inner)).astype(jnp.bfloat16)
    dq_ref[...] = window_apply(grad_scores, k_ref[...], kb_ref[...]) * scale
    key_now, key_before = window_apply_back(grad_scores, query)
    value_now, value_before = window_apply_back(probs.astype(jnp.bfloat16), grad)

    @pl.when(pl.program_id(0) == 0)
    def _():
        dk_ref[...] = key_now * scale
        dkb_ref[...] = key_before * scale
        dv_ref[...] = value_now
        dvb_ref[...] = value_before

    @pl.when(pl.program_id(0) > 0)
    def _():
        dk_ref[...] += key_now * scale
        dkb_ref[...] += key_before * scale
        dv_ref[...] += value_now
        dvb_ref[...] += value_before


def middle_kernel(
    chunk,
    down_rows,
    x_ref,
    dy_ref,
    att_ref,
    rows_near,
    rows_far,
    mine_near,
    mine_far,
    other_near,
    other_far,
    gain_ref,
    info_ref,
    out_ref,
    dmid_ref,
    datt_ref,
    gain_grad_ref,
    wide_near,
    wide_far,
    tall_near,
    tall_far,
    wo_ref,
    wg_ref,
    wu_ref,
    wd_ref,
    mlp_all,
    hidden_all,
    dmlp_all,
    dgate_all,
    dup_all,
    dattn_all,
    sems,
):
    count = info_ref.shape[0] - 3
    core, span = info_ref[count], info_ref[count + 1]
    half = rows_near.shape[2]
    out_rows = 2 * half - down_rows
    feature_rows = mine_near.shape[1]

    @pl.when(pl.program_id(0) == 0)
    def _():
        copies = [
            pltpu.make_async_copy(source, target, sems.at[index])
            for index, (source, target) in enumerate(
                (
                    (rows_near, tall_near),
                    (rows_far, tall_far),
                    (mine_near, wide_near.at[0]),
                    (other_near, wide_near.at[1]),
                    (mine_far, wide_far.at[0]),
                    (other_far, wide_far.at[1]),
                )
            )
        ]
        for copy in copies:
            copy.start()
        for copy in copies:
            copy.wait()

        def down_block(ref, place):
            return [ref[place, 0], ref[place, 1, : down_rows - half]]

        def out_block(ref, place):
            return [ref[place, 1, down_rows - half :]]

        join_pairs(wd_ref, tall_near, tall_far, core, info_ref, down_rows, down_block)
        join_pairs(wo_ref, tall_near, tall_far, core, info_ref, out_rows, out_block)
        for value in (0, 1):
            first, second = (wg_ref, wu_ref) if value == 0 else (wu_ref, wg_ref)

            @pl.when(span == value)
            def _():
                join_pairs(first, wide_near.at[0], wide_far.at[0], core, info_ref, feature_rows)
                join_pairs(second, wide_near.at[1], wide_far.at[1], core, info_ref, feature_rows)

    step = pl.program_id(0)
    block = x_ref.shape[0]
    rows = pl.ds(pl.multiple_of(step * block, block), block)
    ff = wg_ref.shape[1]
    gain_attn, gain_mlp, gain_final = gain_ref[1:2, :], gain_ref[2:3, :], gain_ref[3:4, :]
    x = x_ref[...].astype(jnp.float32)
    raw = dot(att_ref[rows, :], wo_ref[...])
    raw_scale = inverse_rms(raw)
    middle = x + raw * raw_scale * gain_attn
    middle_scale = inverse_rms(middle)
    mlp_low = (middle * middle_scale * gain_mlp).astype(jnp.bfloat16)
    mlp_all[rows, :] = mlp_low
    kept = []
    mlp_raw = None
    for start in range(0, ff, chunk):
        part = slice(start, start + chunk)
        gate = dot(mlp_low, wg_ref[:, part])
        up = dot(mlp_low, wu_ref[:, part])
        square = gate * gate
        bend = jnp.tanh(ROOT * (gate + 0.044715 * (gate * square)))
        lift = 0.5 * (1.0 + bend)
        gelu = gate * lift
        slope = lift + (0.5 * ROOT) * gate * (1.0 - bend * bend) * (1.0 + (3 * 0.044715) * square)
        hidden = (gelu * up).astype(jnp.bfloat16)
        hidden_all[rows, part] = hidden
        kept.append((up * slope, gelu))
        term = dot(hidden, wd_ref[part, :])
        mlp_raw = term if mlp_raw is None else mlp_raw + term
    mlp_scale = inverse_rms(mlp_raw)
    out_ref[...] = (middle + mlp_raw * mlp_scale * gain_final).astype(jnp.bfloat16)
    dy = dy_ref[...].astype(jnp.float32)
    grad_raw, final_rows = rms_back(mlp_raw, mlp_scale, gain_final, dy)
    dmlp_low = grad_raw.astype(jnp.bfloat16)
    dmlp_all[rows, :] = dmlp_low
    grad_in = None
    for index, start in enumerate(range(0, ff, chunk)):
        part = slice(start, start + chunk)
        grad_hidden = dot_nt(dmlp_low, wd_ref[part, :])
        up_slope, gelu = kept[index]
        dgate = (grad_hidden * up_slope).astype(jnp.bfloat16)
        dup = (grad_hidden * gelu).astype(jnp.bfloat16)
        dgate_all[rows, part] = dgate
        dup_all[rows, part] = dup
        term = dot_nt(dgate, wg_ref[:, part]) + dot_nt(dup, wu_ref[:, part])
        grad_in = term if grad_in is None else grad_in + term
    grad_middle, mlp_rows = rms_back(middle, middle_scale, gain_mlp, grad_in)
    grad_middle = dy + grad_middle
    dmid_ref[...] = grad_middle
    grad_attn, attn_rows = rms_back(raw, raw_scale, gain_attn, grad_middle)
    dattn_low = grad_attn.astype(jnp.bfloat16)
    dattn_all[rows, :] = dattn_low
    datt_ref[...] = dot_nt(dattn_low, wo_ref[...]).astype(jnp.bfloat16)
    sums = [jnp.sum(part, axis=0, keepdims=True) for part in (attn_rows, mlp_rows, final_rows)]
    gain_sums = jnp.concatenate(sums + [jnp.zeros((8 - len(sums), x.shape[1]), jnp.float32)], axis=0)

    @pl.when(step == 0)
    def _():
        gain_grad_ref[...] = gain_sums

    @pl.when(step > 0)
    def _():
        gain_grad_ref[...] += gain_sums

    @pl.when(step == pl.num_programs(0) - 1)
    def _():
        for start in range(0, ff, chunk):
            part = slice(start, start + chunk)
            gate_grad = dot_tn(mlp_all[...], dgate_all[:, part])
            up_grad = dot_tn(mlp_all[...], dup_all[:, part])
            down_grad = dot_tn(hidden_all[:, part], dmlp_all[...]).astype(jnp.bfloat16)

            def store(value):
                for index in range(0, count, 2):
                    place = info_ref[index]
                    for other in (0, 1):
                        to = wide_near if other == value else wide_far
                        lines = slice((index + other) * feature_rows, (index + other + 1) * feature_rows)
                        to[span, place, :, part] = gate_grad[lines].astype(jnp.bfloat16)
                        to[1 - span, place, :, part] = up_grad[lines].astype(jnp.bfloat16)
                for line in range(0, chunk, down_rows):
                    index = (start + line) // down_rows
                    to = tall_near if index % 2 == value else tall_far
                    place = info_ref[index]
                    to[place, span] = down_grad[line : line + half]
                    to[place, 1 - span, : down_rows - half] = down_grad[line + half : line + down_rows]

            each_core(core, store)
        for start in range(0, wo_ref.shape[0], chunk):
            part = slice(start, start + chunk)
            out_grad = dot_tn(att_ref[:, part], dattn_all[...]).astype(jnp.bfloat16)

            def store_out(value):
                for line in range(0, chunk, out_rows):
                    index = (start + line) // out_rows
                    to = tall_near if index % 2 == value else tall_far
                    to[info_ref[index], 1 - span, down_rows - half :] = out_grad[line : line + out_rows]

            each_core(core, store_out)


def head_back_kernel(
    head_dim,
    x_ref,
    xb_ref,
    w_ref,
    gain_ref,
    head_gain_ref,
    pick_ref,
    middle_gain_ref,
    info_ref,
    cos_ref,
    sin_ref,
    cosb_ref,
    sinb_ref,
    dq_ref,
    dk_ref,
    dv_ref,
    dkb_ref,
    dvb_ref,
    dmid_ref,
    token_ref,
    before_ref,
    near_ref,
    far_ref,
    normed_all,
    draw_all,
    normed_before_all,
    draw_before_all,
    gain_sum,
    head_sum,
    grad_all,
):
    step = pl.program_id(0)
    block = x_ref.shape[0]
    rows = pl.ds(pl.multiple_of(step * block, block), block)
    queries = dq_ref.shape[1]
    keys = slice(queries, queries + head_dim)
    pair = slice(queries, queries + 2 * head_dim)
    norm_gain = gain_ref[0:1, :]
    query_gain, key_gain = head_gain_ref[4:5, :], head_gain_ref[5:6, :]
    x = x_ref[...].astype(jnp.float32)
    x_scale = inverse_rms(x)
    normed = (x * x_scale * norm_gain).astype(jnp.bfloat16)
    normed_all[rows, :] = normed
    cosine, sine = cos_ref[...], sin_ref[...]
    query_rows = None
    for start in range(0, queries, head_dim):
        part = slice(start, start + head_dim)
        raw = dot(normed, w_ref[:, part])
        grad = turn_back(dq_ref[:, part], cosine, sine)
        grad_raw, head_rows = rms_back(raw, inverse_rms(raw), query_gain, grad)
        query_rows = head_rows if query_rows is None else query_rows + head_rows
        draw_all[rows, part] = grad_raw.astype(jnp.bfloat16)
    raw = dot(normed, w_ref[:, keys])
    grad_raw, key_rows = rms_back(raw, inverse_rms(raw), key_gain, turn_back(dk_ref[...], cosine, sine))
    draw_all[rows, keys] = grad_raw.astype(jnp.bfloat16)
    draw_all[rows, queries + head_dim : queries + 2 * head_dim] = dv_ref[...].astype(jnp.bfloat16)
    grad_normed = dot_nt(draw_all[rows, :], w_ref[...])
    grad_x, norm_rows = rms_back(x, x_scale, norm_gain, grad_normed)
    token_ref[...] = dmid_ref[...] + grad_x

    xb = xb_ref[...].astype(jnp.float32)
    xb_scale = inverse_rms(xb)
    normed_before = (xb * xb_scale * norm_gain).astype(jnp.bfloat16)
    normed_before_all[rows, :] = normed_before
    raw = dot(normed_before, w_ref[:, keys])
    grad = turn_back(dkb_ref[...], cosb_ref[...], sinb_ref[...])
    grad_raw, key_before_rows = rms_back(raw, inverse_rms(raw), key_gain, grad)
    draw_before = jnp.concatenate([grad_raw, dvb_ref[...]], axis=1).astype(jnp.bfloat16)
    draw_before_all[rows, :] = draw_before
    grad_xb, norm_before_rows = rms_back(xb, xb_scale, norm_gain, dot_nt(draw_before, w_ref[:, pair]))
    before_ref[...] = grad_xb.astype(jnp.bfloat16)

    norm_sums = jnp.sum(norm_rows + norm_before_rows, axis=0, keepdims=True)
    head_sums = jnp.concatenate(
        [
            jnp.zeros((4, head_dim), jnp.float32),
            jnp.sum(query_rows, axis=0, keepdims=True),
            jnp.sum(key_rows + key_before_rows, axis=0, keepdims=True),
            jnp.zeros((2, head_dim), jnp.float32),
        ],
        axis=0,
    )

    @pl.when(step == 0)
    def _():
        gain_sum[...] = jnp.zeros_like(gain_sum)
        gain_sum[0:1, :] = norm_sums
        gain_sum[1:4, :] = middle_gain_ref[0:3, :]
        head_sum[...] = head_sums

    @pl.when(step > 0)
    def _():
        gain_sum[0:1, :] += norm_sums
        head_sum[...] += head_sums

    @pl.when(step == pl.num_programs(0) - 1)
    def _():
        count = info_ref.shape[0] - 3
        core, span = info_ref[count], info_ref[count + 1]
        total = queries + 2 * head_dim
        feature_rows = near_ref.shape[2]
        half = near_ref.shape[3]
        for start in range(0, queries, 512):
            part = slice(start, start + 512)
            grad_all[:, part] = dot_tn(normed_all[...], draw_all[:, part])
        grad_all[:, pair] = dot_tn(normed_all[...], draw_all[:, pair]) + dot_tn(
            normed_before_all[...], draw_before_all[...]
        )
        heads = dot_nt(head_sum[...].astype(jnp.bfloat16), pick_ref[...])
        sums = jnp.concatenate(
            [gain_sum[...] + heads, jnp.zeros((LANES - gain_sum.shape[0], gain_sum.shape[1]), jnp.float32)],
            axis=0,
        )
        grad_all[:, total : total + LANES] = sums.T
        grad_all[:, total + LANES :] = jnp.zeros((grad_all.shape[0], grad_all.shape[1] - total - LANES), jnp.float32)

        def store(value):
            for index in range(count):
                to = near_ref if index % 2 == value else far_ref
                place = info_ref[index]
                lines = slice(index * feature_rows, (index + 1) * feature_rows)
                to[span, place] = grad_all[lines, :half].astype(jnp.bfloat16)
                to[1 - span, place] = grad_all[lines, half:].astype(jnp.bfloat16)

        each_core(core, store)


def angle_tables(offset, length_rows, head_dim):
    half_dim = head_dim // 2
    frequency = 10000.0 ** (-(jnp.arange(half_dim).astype(jnp.float32) * 2.0 / head_dim))
    positions = (offset + jnp.arange(length_rows)).astype(jnp.float32)
    angles = positions[:, None] * frequency[None, :]
    return (jnp.cos(angles), jnp.sin(angles))


def per_device(
    tokens,
    cotangent,
    norm_gain,
    query_weight,
    key_weight,
    value_weight,
    query_norm,
    key_norm,
    output_weight,
    attn_post_gain,
    mlp_pre_gain,
    gate_weight,
    up_weight,
    down_weight,
    mlp_post_gain,
):
    fsdp = lax.axis_size("fsdp")
    rows = norm_gain.shape[0]
    head_rows = query_norm.shape[0]
    gain_columns = jnp.stack(
        [
            norm_gain,
            attn_post_gain,
            mlp_pre_gain,
            mlp_post_gain,
            jnp.pad(query_norm, (0, rows - head_rows)),
            jnp.pad(key_norm, (0, rows - head_rows)),
        ],
        axis=1,
    )
    query_columns = query_weight.shape[1]
    head_dim = key_weight.shape[1]
    ff = gate_weight.shape[1]
    qkv_columns = query_columns + 2 * head_dim
    first_columns = -(-(qkv_columns + LANES) // (2 * LANES)) * 2 * LANES
    gain_columns = jnp.pad(
        gain_columns, ((0, 0), (0, first_columns - qkv_columns - gain_columns.shape[1]))
    )
    first_shard = jnp.concatenate([query_weight, key_weight, value_weight, gain_columns], axis=1)
    tall_shard = jnp.concatenate([down_weight, output_weight], axis=0)
    core = lax.axis_index("fsdp") & 1
    span = lax.axis_index("ctx") & 1
    low_span = span == 0
    info = jnp.concatenate(
        [
            places("fsdp"),
            jnp.stack([core, span, (lax.axis_index("ctx") > 0).astype(jnp.int32)]),
        ]
    )
    sequences, span_len, model_width = tokens.shape
    head_count = query_columns // head_dim
    assert span_len == WINDOW
    offset = lax.axis_index("ctx") * span_len
    score_scale = head_dim ** (-0.5)
    tables = angle_tables(offset, span_len, head_dim)
    tables_before = angle_tables(offset - span_len, span_len, head_dim)
    row = jnp.arange(fsdp * rows)
    pick = (
        (row[:, None] // rows == jnp.arange(head_dim)[None, :] // head_rows)
        & (row[:, None] % rows == jnp.arange(head_dim)[None, :] % head_rows)
    ).astype(jnp.bfloat16)
    chip_masks = [1 << bit for bit in range(fsdp.bit_length() - 2, 0, -1)]
    before = shifted(tokens, "ctx", 1)
    first_shard, info, pick, tables, tables_before = lax.optimization_barrier(
        (first_shard, info, pick, tables, tables_before)
    )
    mine_near = jnp.where(low_span, gate_weight, up_weight)[None]
    first_near, tall_near = first_shard[None], tall_shard[None]
    for mask in chip_masks:
        first_near = widen(first_near, "fsdp", mask)
        mine_near = widen(mine_near, "fsdp", mask, first_near)
        if mask != chip_masks[-1]:
            tall_near = widen(tall_near, "fsdp", mask, mine_near)
            mine_near = after(mine_near, tall_near)
    first_far = swap(first_near, "fsdp", 1)
    mine_far = swap(mine_near, "fsdp", 1)
    other_near = swap(mine_near, "ctx", 1)
    tall_late = swap(tall_near, "fsdp", chip_masks[-1])
    total = sequences * span_len
    steps = total // ROWS
    span_steps = span_len // ROWS
    x = tokens.reshape(total, model_width)
    x_before = before.reshape(total, model_width)
    upstream = cotangent.reshape(total, model_width)
    params = pltpu.CompilerParams(vmem_limit_bytes=VMEM_BYTES)
    whole = pl.BlockSpec(memory_space=pltpu.VMEM)
    scalars = pl.BlockSpec(memory_space=pltpu.SMEM)

    def by_rows(columns):
        return pl.BlockSpec((ROWS, columns), lambda i: (i, 0))

    table = pl.BlockSpec((ROWS, head_dim // 2), lambda i: (i % span_steps, 0))

    def bf16(*shape):
        return jax.ShapeDtypeStruct(shape, jnp.bfloat16)

    def f32(*shape):
        return jax.ShapeDtypeStruct(shape, jnp.float32)

    def scratch(*shape):
        return pltpu.VMEM(shape, jnp.bfloat16)

    one_head = by_rows(head_dim)
    model = by_rows(model_width)
    (
        query_low,
        key_low,
        value_low,
        key_prev,
        value_prev,
        first_full,
        gain_rows,
        head_gain_rows,
    ) = pl.pallas_call(
        functools.partial(projection_kernel, head_dim, qkv_columns),
        grid=(steps,),
        in_specs=[model, model, whole, whole, whole, scalars] + [table] * 4,
        out_specs=[by_rows(query_columns)] + [one_head] * 4 + [whole] * 3,
        out_shape=[bf16(total, query_columns)]
        + [bf16(total, head_dim)] * 4
        + [bf16(model_width, qkv_columns), f32(8, model_width), f32(8, head_dim)],
        scratch_shapes=[scratch(model_width, first_columns)],
        compiler_params=params,
        cost_estimate=cost(2 * total * model_width * (qkv_columns + 2 * head_dim), 0.25),
        name="projection",
    )(x, x_before, first_near, first_far, pick, info, *tables, *tables_before)
    other_near = after(other_near, query_low)
    other_far = swap(other_near, "fsdp", 1)
    tall_near = jnp.concatenate([tall_near, after(tall_late, query_low)], axis=0)
    tall_far = swap(tall_near, "fsdp", 1)
    head = pl.BlockSpec((span_len, head_dim), lambda s, h: (s, h))
    shared = pl.BlockSpec((span_len, head_dim), lambda s, h: (s, 0))
    attended_low = pl.pallas_call(
        functools.partial(attention_kernel, score_scale),
        grid=(sequences, head_count),
        in_specs=[scalars, head, shared, shared, shared, shared],
        out_specs=head,
        out_shape=bf16(total, query_columns),
        compiler_params=params,
        cost_estimate=cost(3 * total * span_len * query_columns, 0.14),
        name="attention",
    )(info, query_low, key_low, value_low, key_prev, value_prev)
    down_rows, out_rows = down_weight.shape[0], output_weight.shape[0]
    half_rows = (down_rows + out_rows) // 2
    chips = fsdp // 2
    (
        block_output,
        grad_middle,
        grad_attended,
        middle_gains,
        wide_grad_near,
        wide_grad_far,
        tall_grad_near,
        tall_grad_far,
    ) = pl.pallas_call(
        functools.partial(middle_kernel, 512, down_rows),
        grid=(steps,),
        in_specs=[model, model, whole] + [pl.BlockSpec(memory_space=pl.ANY)] * 6 + [whole, scalars],
        out_specs=[model, model, by_rows(query_columns)] + [whole] * 5,
        out_shape=[
            bf16(total, model_width),
            f32(total, model_width),
            bf16(total, query_columns),
            f32(8, model_width),
            bf16(2, chips, rows, ff),
            bf16(2, chips, rows, ff),
            bf16(chips, 2, half_rows, model_width),
            bf16(chips, 2, half_rows, model_width),
        ],
        scratch_shapes=[
            scratch(query_columns, model_width),
            scratch(model_width, ff),
            scratch(model_width, ff),
            scratch(ff, model_width),
            scratch(total, model_width),
            scratch(total, ff),
            scratch(total, model_width),
            scratch(total, ff),
            scratch(total, ff),
            scratch(total, model_width),
            pltpu.SemaphoreType.DMA((6,)),
        ],
        compiler_params=params,
        cost_estimate=cost(6 * total * model_width * (3 * ff + query_columns), 0.4),
        name="middle",
    )(
        x,
        upstream,
        attended_low,
        tall_near.reshape(chips, 2, half_rows, model_width),
        tall_far.reshape(chips, 2, half_rows, model_width),
        mine_near,
        mine_far,
        other_near,
        other_far,
        gain_rows,
        info,
    )
    far_mask, near_masks = chip_masks[0], chip_masks[:0:-1]
    wide_far_sum = swap(wide_grad_far, "fsdp", 1)
    tall_far_sum = swap(tall_grad_far, "fsdp", 1)

    def attention_back(sequence, grad, done):
        one = pl.BlockSpec((span_len, head_dim), lambda h: (sequence, h))
        for_all = pl.BlockSpec((span_len, head_dim), lambda h: (sequence, 0))
        return pl.pallas_call(
            functools.partial(attention_back_kernel, score_scale),
            grid=(head_count,),
            in_specs=[scalars, one] + [for_all] * 4 + [one] + [pl.BlockSpec(memory_space=pl.ANY)] * len(done),
            out_specs=[one] + [for_all] * 4,
            out_shape=[f32(total, query_columns)] + [f32(total, head_dim)] * 4,
            input_output_aliases={7 + index: index for index in range(len(done))},
            compiler_params=params,
            cost_estimate=cost(7.5 * span_len * span_len * query_columns, 0.2),
            name="attention_back",
        )(info, query_low, key_low, value_low, key_prev, value_prev, grad, *done)

    back = attention_back(0, grad_attended, ())
    wide_far_sum, tall_far_sum = after((wide_far_sum, tall_far_sum), back[0])
    wide = add(wide_grad_near, wide_far_sum)
    tall = add(tall_grad_near, tall_far_sum)
    bits = (2,) * len(chip_masks)
    wide = wide.reshape((2,) + bits + wide.shape[2:])
    tall = tall.reshape(bits + tall.shape[1:])
    wide_kept, wide_come = folded(wide, "fsdp", near_masks[0], 1)
    tall_kept, tall_come = folded(tall, "fsdp", near_masks[1], 1)
    wide, tall, grad_attended = lax.optimization_barrier((wide, tall, grad_attended))
    for sequence in range(1, sequences):
        back = attention_back(sequence, grad_attended, back)
    grad_query, grad_key, grad_value, key_send, value_send = back
    token_part, before_part, first_grad_near, first_grad_far = pl.pallas_call(
        functools.partial(head_back_kernel, head_dim),
        grid=(steps,),
        in_specs=[model, model]
        + [whole] * 5
        + [scalars]
        + [table] * 4
        + [by_rows(query_columns)]
        + [one_head] * 4
        + [model],
        out_specs=[model, model, whole, whole],
        out_shape=[
            f32(total, model_width),
            bf16(total, model_width),
            bf16(2, chips, rows, first_columns // 2),
            bf16(2, chips, rows, first_columns // 2),
        ],
        scratch_shapes=[
            scratch(total, model_width),
            scratch(total, qkv_columns),
            scratch(total, model_width),
            scratch(total, 2 * head_dim),
            pltpu.VMEM((8, model_width), jnp.float32),
            pltpu.VMEM((8, head_dim), jnp.float32),
            pltpu.VMEM((model_width, first_columns), jnp.float32),
        ],
        compiler_params=params,
        cost_estimate=cost(6 * total * model_width * (qkv_columns + 2 * head_dim), 0.38),
        name="head_back",
    )(
        x,
        x_before,
        first_full,
        gain_rows,
        head_gain_rows,
        pick,
        middle_gains,
        info,
        *tables,
        *tables_before,
        grad_query,
        grad_key,
        grad_value,
        key_send,
        value_send,
        grad_middle,
    )
    tall = add(tall_kept, after(tall_come, token_part))
    wide = add(wide_kept, after(wide_come, token_part))
    first_grad_far, before_part = after((first_grad_far, before_part), tall, wide)
    tall_kept, tall_come = folded(tall, "fsdp", near_masks[0], 0)
    wide_kept, wide_come = folded(wide, "fsdp", near_masks[1], 2)
    before_come = shifted(before_part, "ctx", -1)
    first = add(first_grad_near, swap(first_grad_far, "fsdp", 1))
    first = first.reshape((2,) + bits + first.shape[2:])
    first_kept, first_come = folded(first, "fsdp", near_masks[0], 1)
    first = add(first_kept, first_come)
    first_kept, first_come = folded(first, "fsdp", near_masks[1], 2)
    tall = add(tall_kept, after(tall_come, first))
    tall_kept, tall_come = folded(tall, "ctx", 1, len(bits))
    wide = add(wide_kept, after(wide_come, tall))
    wide_kept, wide_come = folded(wide, "ctx", 1, 0)
    first = add(first_kept, after(first_come, wide))
    first_kept, first_come = folded(first, "ctx", 1, 0)
    tall = add(tall_kept, after(tall_come, first))
    wide = add(wide_kept, after(wide_come, tall))
    first = add(first_kept, after(first_come, wide))
    for index in range(2, len(bits)):
        mask = (near_masks + [far_mask])[index]
        tall_kept, tall_come = folded(tall, "fsdp", mask, index)
        wide_kept, wide_come = folded(wide, "fsdp", mask, index + 1)
        first_kept, first_come = folded(first, "fsdp", mask, index + 1)
        tall = add(tall_kept, tall_come)
        wide = add(wide_kept, after(wide_come, tall))
        first = add(first_kept, after(first_come, wide))
    tall = other_spans(tall.reshape(tall.shape[-2:]), "ctx")
    wide = other_spans(wide.reshape(wide.shape[-2:]), "ctx")
    first = other_spans(first.reshape(first.shape[-2:]), "ctx")
    before_come = after(before_come, first)
    token_grad = (token_part + before_come.astype(jnp.float32)).astype(jnp.bfloat16)

    def both(mine):
        other = swap(mine, "ctx", 1)
        left = jnp.where(low_span, mine, other).astype(jnp.float32)
        right = jnp.where(low_span, other, mine).astype(jnp.float32)
        return left, right

    grad_gate, grad_up = both(wide)
    grad_tall = jnp.concatenate(both(tall), axis=0)
    grad_first = jnp.concatenate(both(first), axis=1)
    return (
        block_output.reshape(tokens.shape),
        token_grad.reshape(tokens.shape),
        grad_first[:, qkv_columns],
        grad_first[:, :query_columns],
        grad_first[:, query_columns : query_columns + head_dim],
        grad_first[:, query_columns + head_dim : qkv_columns],
        grad_first[:head_rows, qkv_columns + 4],
        grad_first[:head_rows, qkv_columns + 5],
        grad_tall[down_rows:],
        grad_first[:, qkv_columns + 1],
        grad_first[:, qkv_columns + 2],
        grad_gate,
        grad_up,
        grad_tall[:down_rows],
        grad_first[:, qkv_columns + 3],
    )


def solution(mesh):
    return jax.shard_map(
        per_device,
        mesh=mesh,
        in_specs=(
            P("fsdp", "ctx", None),
            P("fsdp", "ctx", None),
            P("fsdp"),
            P("fsdp", None),
            P("fsdp", None),
            P("fsdp", None),
            P("fsdp"),
            P("fsdp"),
            P("fsdp", None),
            P("fsdp"),
            P("fsdp"),
            P("fsdp", None),
            P("fsdp", None),
            P("fsdp", None),
            P("fsdp"),
        ),
        out_specs=(
            P("fsdp", "ctx", None),
            P("fsdp", "ctx", None),
            P("fsdp"),
            P("fsdp", None),
            P("fsdp", None),
            P("fsdp", None),
            P("fsdp"),
            P("fsdp"),
            P("fsdp", None),
            P("fsdp"),
            P("fsdp"),
            P("fsdp", None),
            P("fsdp", None),
            P("fsdp", None),
            P("fsdp"),
        ),
        check_vma=False,
    )
```

time: 346 us -> 320 us (0.925)
  waiting for transfers between devices: 149 us -> 114 us
  Pallas kernels: 103 us -> 129 us
  local copies, waits for them, and re-layouts: 33.9 us -> 13.1 us
  between operations: 14.6 us -> 1.68 us
  starting transfers between devices: 25.4 us -> 33 us
  other arithmetic: 19.1 us -> 26.4 us
    ppermute x4 -> x2, waiting for transfers between devices: 45.6 us -> 0.01 us  [shifted(): lax.ppermute(value, axis, [(source, source + steps) for source in range(l...]
    pallas_call x3 -> x4, Pallas kernels: 78.1 us -> 100 us  [the longest x1 70.4 us: per_device(): pl.pallas_call(functools.partial(middle_kernel, 512, down_rows), grid=(st...]
    ppermute x10 -> x32, waiting for transfers between devices: 92.2 us -> 114 us  [swap(): lax.ppermute(value, axis, [(source, source ^ mask) for source in range(co...]
    reduce_scatter x1 -> x0, waiting for transfers between devices: 10.9 us -> none  [per_device(): lax.psum_scatter(rest_grads, 'fsdp', scatter_dimension=0, tiled=True)]
    reshape x6 -> x0, local copies, waits for them, and re-layouts: 9.96 us -> none  [the longest x1 3.96 us: per_device(): down_full = rest_full[:, 2 * ff:3 * ff].reshape(ff, -1)]
    ppermute x10 -> x32, starting transfers between devices: 18.9 us -> 28.3 us  [swap(): lax.ppermute(value, axis, [(source, source ^ mask) for source in range(co...]
    convert_element_type x5 -> x19, other arithmetic: 3.13 us -> 12.5 us  [the longest x14 9.2 us: add(): (left.astype(jnp.float32) + right.astype(jnp.float32)).astype(jnp.bfloat16)]
    slice x13 -> x4, local copies, waits for them, and re-layouts: 10.4 us -> 2.75 us  [the longest x1 0.74 us: per_device(): grad_first[:, qkv_columns + 3]]
  transfers between devices with their start and end apart: 16 -> 34, of which waited for: 14 -> 17; matrix products, arithmetic and copies ran while one was open for 4% -> 8% of each run, Pallas kernels for 15% -> 18%
where the time goes in v1:
time: 320 us; the launch traced here: 317 us
  Pallas kernels  129 us (40%)
  waiting for transfers between devices  114 us (36%)
  starting transfers between devices  33 us (10%)
  other arithmetic  26.4 us (8%)
  local copies, waits for them, and re-layouts  13.1 us (4%)
    ppermute x32, waiting for transfers between devices, swap(): lax.ppermute(value, axis, [(source, source ^ mask) for source in range(co...  114 us
    pallas_call x1, Pallas kernels, per_device(): pl.pallas_call(functools.partial(middle_kernel, 512, down_rows), grid=(st...  70.4 us
    ppermute x32, starting transfers between devices, swap(): lax.ppermute(value, axis, [(source, source ^ mask) for source in range(co...  28.3 us
    pallas_call x2, Pallas kernels, attention_back(): pl.pallas_call(functools.partial(attention_back_kernel, score_scale), gri...  20.8 us
    pallas_call x1, Pallas kernels, per_device(): pl.pallas_call(functools.partial(head_back_kernel, head_dim), grid=(steps...  17.9 us
    pallas_call x1, Pallas kernels, per_device(): pl.pallas_call(functools.partial(attention_kernel, score_scale), grid=(se...  10.3 us
    pallas_call x1, Pallas kernels, per_device(): pl.pallas_call(functools.partial(projection_kernel, head_dim, qkv_columns...  9.27 us
    convert_element_type x14, other arithmetic, add(): (left.astype(jnp.float32) + right.astype(jnp.float32)).astype(jnp.bfloat16)  9.2 us
  transfers between devices with their start and end apart: 34, of which 17 were waited for; matrix products, arithmetic and copies ran while one was open for 8% of the time, Pallas kernels for 18%

profile of v1, /device:TPU:0, one launch (start us, length us, event | category | flops | bytes accessed | tf_op | source)
XLA Modules:
  0.0 316.5 jit_solution(7662117785658505127)
XLA Ops:
  0.7 1.1 select_bitcast_fusion
  1.7 4.1 %collective-permute-start.6 = (bf16[1,40,2048]{2,1,0:T(8,128)(2,1)S(1)}, bf16[1,40,2048]{2,1,0:T(8,128)(2,1)S(1)}, u32[]{:S(2)}, u32[]{:S(2)}) collective-permute-start(bf16[1,40,2048]{2,1,0:T(8,128)(2,1)S(1)} %select_bitcast_fusion), channel_id=1, source_target_pairs={{0,16},{2,18},{4,20},{6,22},{8,24},{10,26},{12,28},{14,30},{16,0},... | collective-permute-start | bytes 491528 | tf_op jit(solution)/shard_map/ppermute | solution.py:25
  7.4 3.0 multiply_sine_fusion
  13.0 3.0 collective-permute-start.5
  16.0 3.5 %collective-permute-start = (bf16[2,512,640]{2,1,0:T(8,128)(2,1)S(1)}, bf16[2,512,640]{2,1,0:T(8,128)(2,1)S(1)}, u32[]{:S(2)}, u32[]{:S(2)}) collective-permute-start(bf16[2,512,640]{2,1,0:T(8,128)(2,1)S(1)} %copy-done.1), channel_id=1, source_target_pairs={{0,1},{2,3},{4,5},{6,7},{8,9},{10,11},{12,13},{14,15},{16,17},{18,... | collective-permute-start | bytes 3932168 | tf_op jit(solution)/shard_map/ppermute | solution.py:71
  19.4 9.1 %collective-permute-done.1 = bf16[1,40,1792]{2,1,0:T(8,128)(2,1)S(1)} collective-permute-done((bf16[1,40,1792]{2,1,0:T(8,128)(2,1)S(1)}, bf16[1,40,1792]{2,1,0:T(8,128)(2,1)S(1)}, u32[]{:S(2)}, u32[]{:S(2)}) %collective-permute-start.1) | collective-permute-done | bytes 143392 | tf_op jit(solution)/shard_map/ppermute | solution.py:25
  28.7 4.0 %collective-permute-done.5 = bf16[1,192,640]{2,1,0:T(8,128)(2,1)S(1)} collective-permute-done((bf16[1,192,640]{2,1,0:T(8,128)(2,1)S(1)}, bf16[1,192,640]{2,1,0:T(8,128)(2,1)S(1)}, u32[]{:S(2)}, u32[]{:S(2)}) %collective-permute-start.5) | collective-permute-done | bytes 245792 | tf_op jit(solution)/shard_map/ppermute | solution.py:25
  32.9 2.0 collective-permute-start.8
  34.9 4.0 %collective-permute-done.2 = bf16[2,40,1792]{2,1,0:T(8,128)(2,1)S(1)} collective-permute-done((bf16[2,40,1792]{2,1,0:T(8,128)(2,1)S(1)}, bf16[2,40,1792]{2,1,0:T(8,128)(2,1)S(1)}, u32[]{:S(2)}, u32[]{:S(2)}) %collective-permute-start.2) | collective-permute-done | bytes 286752 | tf_op jit(solution)/shard_map/ppermute | solution.py:25
  38.9 1.6 collective-permute-start.3
  40.5 15.8 %collective-permute-done.8 = bf16[2,40,2048]{2,1,0:T(8,128)(2,1)S(1)} collective-permute-done((bf16[2,40,2048]{2,1,0:T(8,128)(2,1)S(1)}, bf16[2,40,2048]{2,1,0:T(8,128)(2,1)S(1)}, u32[]{:S(2)}, u32[]{:S(2)}) %collective-permute-start.8) | collective-permute-done | bytes 327712 | tf_op jit(solution)/shard_map/ppermute | solution.py:25
  56.4 1.1 pad_maximum_fusion.3
  57.4 1.5 collective-permute-start.11
  60.7 14.4 %collective-permute-done.11 = bf16[4,40,2048]{2,1,0:T(8,128)(2,1)S(1)} collective-permute-done((bf16[4,40,2048]{2,1,0:T(8,128)(2,1)S(1)}, bf16[4,40,2048]{2,1,0:T(8,128)(2,1)S(1)}, u32[]{:S(2)}, u32[]{:S(2)}) %collective-permute-start.11) | collective-permute-done | bytes 655392 | tf_op jit(solution)/shard_map/ppermute | solution.py:25
  75.9 1.5 collective-permute-start.13
  78.9 9.3 %projection.1 = (bf16[1024,1024]{1,0:T(8,128)(2,1)}, bf16[1024,256]{1,0:T(8,128)(2,1)}, bf16[1024,256]{1,0:T(8,128)(2,1)}, bf16[1024,256]{1,0:T(8,128)(2,1)}, bf...) custom-call(bf16[1024,640]{1,0:T(8,128)(2,1)} %bitcast.45, ...), custom_call_target="tpu_custom_call" | custom-call | flops 671088640 | tf_op jit(solution)/shard_map/projection/pallas_call | solution.py:716
  88.1 7.1 %collective-permute-done.9 = bf16[4,192,640]{2,1,0:T(8,128)(2,1)} collective-permute-done((bf16[4,192,640]{2,1,0:T(8,128)(2,1)}, bf16[4,192,640]{2,1,0:T(8,128)(2,1)}, u32[]{:S(2)}, u32[]{:S(2)}) %collective-permute-start.9) | collective-permute-done | bytes 983072 | tf_op jit(solution)/shard_map/ppermute | solution.py:25
  95.3 2.8 pad_maximum_fusion.1
  98.5 6.6 %collective-permute-done.13.other_near = bf16[8,40,2048]{2,1,0:T(8,128)(2,1)} collective-permute-done((bf16[8,40,2048]{2,1,0:T(8,128)(2,1)}, bf16[8,40,2048]{2,1,0:T(8,128)(2,1)}, u32[]{:S(2)}, u32[]{:S(2)}) %collective-permute-start.13) | collective-permute-done | bytes 1310752 | tf_op jit(solution)/shard_map/ppermute | solution.py:25
  105.2 10.3 %attention.1.att_ref = bf16[1024,1024]{1,0:T(8,128)(2,1)} custom-call(s32[19]{0:T(128)} %pad_add_fusion.info_ref.flag_ref, bf16[1024,1024]{1,0:T(8,128)(2,1)} %get-tuple-element.84.q_ref, bf16[1024,256]{1,0:T(8,128)(2,1)} %get-tuple-element.85.k_ref, bf16[1024,256]{1,0:T(8,128)(2,1)} %get-tuple-element.86.v_ref, bf16[1024,256]{1,0:T(8,128)(2,1)} %get-tuple-element.87.kb_ref, ...), custom_call_target="tpu_custom_call" | custom-call | flops 719023552 | tf_op jit(solution)/shard_map/attention/pallas_call | solution.py:735
  115.5 2.8 pad_maximum_fusion.rows_near
  119.7 70.4 %middle.1 = (bf16[1024,640]{1,0:T(8,128)(2,1)}, f32[1024,640]{1,0:T(8,128)}, bf16[1024,1024]{1,0:T(8,128)(2,1)}, f32[8,640]{1,0:T(8,128)}, bf16[2,8,40,2048]{3,2...) custom-call(bf16[1024,640]{1,0:T(8,128)(2,1)} %bitcast.46, ...), custom_call_target="tpu_custom_call" | custom-call | flops 4404019200 | tf_op jit(solution)/shard_map/middle/pallas_call | solution.py:757
  190.8 10.4 %attention_back.2 = (f32[1024,1024]{1,0:T(8,128)}, f32[1024,256]{1,0:T(8,128)}, f32[1024,256]{1,0:T(8,128)}, f32[1024,256]{1,0:T(8,128)}, f32[1024,256]{1,0:T(8,128)}) custom-call(s32[19]{0:T(128)} %pad_add_fusion.info_ref.flag_ref, bf16[1024,1024]{1,0:T(8,128)(2,1)} %get-tuple-element.84.q_ref, bf16[1024,256]{1,0:T(8,128)(2,1)} %get-tuple-element.85.k_ref, ...), custom_call_target="tpu_custom_call" | custom-call | flops 629145600 | tf_op jit(solution)/shard_map/attention_back/pallas_call | solution.py:808
  201.2 1.3 copy-done.6
  202.6 3.9 %add_convert_fusion = bf16[2,8,40,2048]{3,2,1,0:T(8,128)(2,1)S(1)} fusion(bf16[2,8,40,2048]{3,2,1,0:T(8,128)(2,1)} %collective-permute-done.15, bf16[2,8,40,2048]{3,2,1,0:T(8,128)(2,1)} %get-tuple-element.103), kind=kLoop, calls=%fused_computation | loop fusion | flops 5242880 | bytes 7864320 | tf_op jit(solution)/shard_map/convert_element_type | solution.py:52
  206.6 1.6 collective-permute-start.18
  208.8 1.3 copy-done
  210.0 1.1 split.97
  211.1 10.4 %attention_back.3 = (f32[1024,1024]{1,0:T(8,128)}, f32[1024,256]{1,0:T(8,128)}, f32[1024,256]{1,0:T(8,128)}, f32[1024,256]{1,0:T(8,128)}, f32[1024,256]{1,0:T(8,128)}) custom-call(s32[19]{0:T(128)} %pad_add_fusion.info_ref.flag_ref, ...), custom_call_target="tpu_custom_call", output_to_operand_aliasing={{0}: (7, {}), {1}: (8, {}), {2}: (9, {}), {3}: (10, {}), {4... | custom-call | flops 629145600 | tf_op jit(solution)/shard_map/attention_back/pallas_call | solution.py:808
  221.5 17.9 %head_back.1 = (f32[1024,640]{1,0:T(8,128)}, bf16[1024,640]{1,0:T(8,128)(2,1)}, bf16[2,8,40,896]{3,2,1,0:T(8,128)(2,1)}, bf16[2,8,40,896]{3,2,1,0:T(8,128)(2,1)}) custom-call(bf16[1024,640]{1,0:T(8,128)(2,1)} %bitcast.47, bf16[1024,640]{1,0:T(8,128)(2,1)} %bitcast.49, bf16[640,1536]{1,0:T(8,128)(2,1)} %get-tuple-element.100.w_ref, ...), custom_call_target="tpu_custom_call" | custom-call | flops 1324516992 | tf_op jit(solution)/shard_map/head_back/pallas_call | solution.py:833
  239.4 1.7 add_convert_fusion.5
  241.2 1.9 add_convert_fusion.3
  243.4 2.6 collective-permute-done.20
  246.4 1.5 collective-permute-start.21
  248.6 2.1 collective-permute-start.23
  250.7 1.3 collective-permute-start.19
  252.0 10.3 %collective-permute-done.21 = bf16[2,1,2,2,40,896]{5,4,3,2,1,0:T(8,128)(2,1)S(1)} collective-permute-done((bf16[2,1,2,2,40,896]{5,4,3,2,1,0:T(8,128)(2,1)S(1)}, bf16[2,1,2,2,40,896]{5,4,3,2,1,0:T(8,128)(2,1)S(1)}, u32[]{:S(2)}, u32[]{:S(2)}) %collective-permute-start.21) | collective-permute-done | bytes 573472 | tf_op jit(solution)/shard_map/ppermute | solution.py:25
  262.4 9.6 %collective-permute-done.24 = bf16[1,1,2,2,96,640]{5,4,3,2,1,0:T(8,128)(2,1)S(1)} collective-permute-done((bf16[1,1,2,2,96,640]{5,4,3,2,1,0:T(8,128)(2,1)S(1)}, bf16[1,1,2,2,96,640]{5,4,3,2,1,0:T(8,128)(2,1)S(1)}, u32[]{:S(2)}, u32[]{:S(2)}) %collective-permute-start.24) | collective-permute-done | bytes 491552 | tf_op jit(solution)/shard_map/ppermute | solution.py:25
  272.2 1.6 collective-permute-start.27
  273.8 1.9 collective-permute-start.22
  276.6 5.2 %collective-permute-done.22 = bf16[2,1,1,2,40,896]{5,4,3,2,1,0:T(8,128)(2,1)S(1)} collective-permute-done((bf16[2,1,1,2,40,896]{5,4,3,2,1,0:T(8,128)(2,1)S(1)}, bf16[2,1,1,2,40,896]{5,4,3,2,1,0:T(8,128)(2,1)S(1)}, u32[]{:S(2)}, u32[]{:S(2)}) %collective-permute-start.22) | collective-permute-done | bytes 286752 | tf_op jit(solution)/shard_map/ppermute | solution.py:25
  281.9 7.7 %collective-permute-done.27 = bf16[1,1,2,1,96,640]{5,4,3,2,1,0:T(8,128)(2,1)S(1)} collective-permute-done((bf16[1,1,2,1,96,640]{5,4,3,2,1,0:T(8,128)(2,1)S(1)}, bf16[1,1,2,1,96,640]{5,4,3,2,1,0:T(8,128)(2,1)S(1)}, u32[]{:S(2)}, u32[]{:S(2)}) %collective-permute-start.27) | collective-permute-done | bytes 245792 | tf_op jit(solution)/shard_map/ppermute | solution.py:25
  289.8 6.7 %collective-permute-done.26 = bf16[1,1,1,2,40,2048]{5,4,3,2,1,0:T(8,128)(2,1)S(1)} collective-permute-done((bf16[1,1,1,2,40,2048]{5,4,3,2,1,0:T(8,128)(2,1)S(1)}, bf16[1,1,1,2,40,2048]{5,4,3,2,1,0:T(8,128)(2,1)S(1)}, u32[]{:S(2)}, u32[]{:S(2)}) %collective-permute-start.26) | collective-permute-done | bytes 327712 | tf_op jit(solution)/shard_map/ppermute | solution.py:25
  296.8 2.4 collective-permute-done.25
  299.9 6.3 %collective-permute-done.29 = bf16[1,1,1,1,40,2048]{5,4,3,2,1,0:T(8,128)(2,1)S(1)} collective-permute-done((bf16[1,1,1,1,40,2048]{5,4,3,2,1,0:T(8,128)(2,1)S(1)}, bf16[1,1,1,1,40,2048]{5,4,3,2,1,0:T(8,128)(2,1)S(1)}, u32[]{:S(2)}, u32[]{:S(2)}) %collective-permute-start.29) | collective-permute-done | bytes 163872 | tf_op jit(solution)/shard_map/ppermute | solution.py:25
  307.0 1.4 collective-permute-start.31
  308.5 1.4 add_convert_fusion.2
  311.3 1.1 collective-permute-done.31
  (123 shorter events, 21.5 us)
Async XLA Ops:
  0.6 12.3 %copy-start.10 = (bf16[128,640]{1,0:T(8,128)(2,1)S(1)}, bf16[128,640]{1,0:T(8,128)(2,1)}, u32[]{:S(2)}) copy-start(bf16[128,640]{1,0:T(8,128)(2,1)} %param.28) | copy-start | bytes 491524
  0.7 12.3 %copy-start.11 = (bf16[64,640]{1,0:T(8,128)(2,1)S(1)}, bf16[64,640]{1,0:T(8,128)(2,1)}, u32[]{:S(2)}) copy-start(bf16[64,640]{1,0:T(8,128)(2,1)} %param.23) | copy-start | bytes 245764
  0.7 15.3 %copy-start.1 = (bf16[2,512,640]{2,1,0:T(8,128)(2,1)S(1)}, bf16[2,512,640]{2,1,0:T(8,128)(2,1)}, u32[]{:S(2)}) copy-start(bf16[2,512,640]{2,1,0:T(8,128)(2,1)} %param.15) | copy-start | bytes 3932164
  1.7 26.9 %collective-permute-start.6 = (bf16[1,40,2048]{2,1,0:T(8,128)(2,1)S(1)}, bf16[1,40,2048]{2,1,0:T(8,128)(2,1)S(1)}, u32[]{:S(2)}, u32[]{:S(2)}) collective-permute-start(bf16[1,40,2048]{2,1,0:T(8,128)(2,1)S(1)} %select_bitcast_fusion), channel_id=1, source_target_pairs={{0,16},{2,18},{4,20},{6,22},{8,24},{10,26},{12,28},{14,30},{16,0},... | collective-permute-start | bytes 491528 | tf_op jit(solution)/shard_map/ppermute | solution.py:25
  12.9 15.6 %collective-permute-start.1 = (bf16[1,40,1792]{2,1,0:T(8,128)(2,1)S(1)}, bf16[1,40,1792]{2,1,0:T(8,128)(2,1)S(1)}, u32[]{:S(2)}, u32[]{:S(2)}) collective-permute-start(bf16[1,40,1792]{2,1,0:T(8,128)(2,1)S(1)} %bitcast.54), channel_id=1, source_target_pairs={{0,16},{2,18},{4,20},{6,22},{8,24},{10,26},{12,28},{14,30},{16,0},... | collective-permute-start | bytes 430088 | tf_op jit(solution)/shard_map/ppermute | solution.py:25
  13.0 19.7 %collective-permute-start.5 = (bf16[1,192,640]{2,1,0:T(8,128)(2,1)S(1)}, bf16[1,192,640]{2,1,0:T(8,128)(2,1)S(1)}, u32[]{:S(2)}, u32[]{:S(2)}) collective-permute-start(bf16[1,192,640]{2,1,0:T(8,128)(2,1)S(1)} %bitcast.40), channel_id=1, source_target_pairs={{0,16},{2,18},{4,20},{6,22},{8,24},{10,26},{12,28},{14,30},{16,0},... | collective-permute-start | bytes 737288 | tf_op jit(solution)/shard_map/ppermute | solution.py:25
  16.0 61.5 %collective-permute-start = (bf16[2,512,640]{2,1,0:T(8,128)(2,1)S(1)}, bf16[2,512,640]{2,1,0:T(8,128)(2,1)S(1)}, u32[]{:S(2)}, u32[]{:S(2)}) collective-permute-start(bf16[2,512,640]{2,1,0:T(8,128)(2,1)S(1)} %copy-done.1), channel_id=1, source_target_pairs={{0,1},{2,3},{4,5},{6,7},{8,9},{10,11},{12,13},{14,15},{16,17},{18,... | collective-permute-start | bytes 3932168 | tf_op jit(solution)/shard_map/ppermute | solution.py:71
  28.6 10.3 %collective-permute-start.2 = (bf16[2,40,1792]{2,1,0:T(8,128)(2,1)S(1)}, bf16[2,40,1792]{2,1,0:T(8,128)(2,1)S(1)}, u32[]{:S(2)}, u32[]{:S(2)}) collective-permute-start(bf16[2,40,1792]{2,1,0:T(8,128)(2,1)S(1)} %pad_maximum_fusion.8), channel_id=1, source_target_pairs={{0,8},{2,10},{4,12},{6,14},{8,0},{10,2},{12,4},{14,6},{16,24},{18,... | collective-permute-start | bytes 860168 | tf_op jit(solution)/shard_map/ppermute | solution.py:25
  32.8 23.6 %collective-permute-start.7 = (bf16[2,192,640]{2,1,0:T(8,128)(2,1)S(1)}, bf16[2,192,640]{2,1,0:T(8,128)(2,1)S(1)}, u32[]{:S(2)}, u32[]{:S(2)}) collective-permute-start(bf16[2,192,640]{2,1,0:T(8,128)(2,1)S(1)} %pad_maximum_fusion.5), channel_id=1, source_target_pairs={{0,8},{2,10},{4,12},{6,14},{8,0},{10,2},{12,4},{14,6},{16,24},{18,... | collective-permute-start | bytes 1474568 | tf_op jit(solution)/shard_map/ppermute | solution.py:25
  32.9 23.5 %collective-permute-start.8 = (bf16[2,40,2048]{2,1,0:T(8,128)(2,1)S(1)}, bf16[2,40,2048]{2,1,0:T(8,128)(2,1)S(1)}, u32[]{:S(2)}, u32[]{:S(2)}) collective-permute-start(bf16[2,40,2048]{2,1,0:T(8,128)(2,1)S(1)} %pad_maximum_fusion.7), channel_id=1, source_target_pairs={{0,8},{2,10},{4,12},{6,14},{8,0},{10,2},{12,4},{14,6},{16,24},{18,... | collective-permute-start | bytes 983048 | tf_op jit(solution)/shard_map/ppermute | solution.py:25
  38.9 20.0 %collective-permute-start.3 = (bf16[4,40,1792]{2,1,0:T(8,128)(2,1)S(1)}, bf16[4,40,1792]{2,1,0:T(8,128)(2,1)S(1)}, u32[]{:S(2)}, u32[]{:S(2)}) collective-permute-start(bf16[4,40,1792]{2,1,0:T(8,128)(2,1)S(1)} %pad_maximum_fusion.4), channel_id=1, source_target_pairs={{0,4},{2,6},{4,0},{6,2},{8,12},{10,14},{12,8},{14,10},{16,20},{18,... | collective-permute-start | bytes 1720328 | tf_op jit(solution)/shard_map/ppermute | solution.py:25
  57.4 17.6 %collective-permute-start.11 = (bf16[4,40,2048]{2,1,0:T(8,128)(2,1)S(1)}, bf16[4,40,2048]{2,1,0:T(8,128)(2,1)S(1)}, u32[]{:S(2)}, u32[]{:S(2)}) collective-permute-start(bf16[4,40,2048]{2,1,0:T(8,128)(2,1)S(1)} %constant_dynamic-update-slice_fusion.2), channel_id=1, source_target_pairs={{0,4},{2,6},{4,0},{6,2},{8,12},{10,14},{12,8},{14,10},{16,20},{18,... | collective-permute-start | bytes 1966088 | tf_op jit(solution)/shard_map/ppermute | solution.py:25
  59.1 18.4 %copy-start.3 = (bf16[8,40,1792]{2,1,0:T(8,128)(2,1)}, bf16[8,40,1792]{2,1,0:T(8,128)(2,1)S(1)}, u32[]{:S(2)}) copy-start(bf16[8,40,1792]{2,1,0:T(8,128)(2,1)S(1)} %pad_maximum_fusion.2.near_ref) | copy-start | bytes 3440644
  59.1 18.3 %collective-permute-start.4 = (bf16[8,40,1792]{2,1,0:T(8,128)(2,1)S(1)}, bf16[8,40,1792]{2,1,0:T(8,128)(2,1)S(1)}, u32[]{:S(2)}, u32[]{:S(2)}) collective-permute-start(bf16[8,40,1792]{2,1,0:T(8,128)(2,1)S(1)} %pad_maximum_fusion.2.near_ref), channel_id=1, source_target_pairs={{0,2},{2,0},{4,6},{6,4},{8,10},{10,8},{12,14},{14,12},{16,18},{18,... | collective-permute-start | bytes 3440648 | tf_op jit(solution)/shard_map/ppermute | solution.py:25
  59.2 36.1 %collective-permute-start.9 = (bf16[4,192,640]{2,1,0:T(8,128)(2,1)}, bf16[4,192,640]{2,1,0:T(8,128)(2,1)}, u32[]{:S(2)}, u32[]{:S(2)}) collective-permute-start(bf16[4,192,640]{2,1,0:T(8,128)(2,1)} %pad_maximum_fusion.3), channel_id=1, source_target_pairs={{0,4},{2,6},{4,0},{6,2},{8,12},{10,14},{12,8},{14,10},{16,20},{18,... | collective-permute-start | bytes 2949128 | tf_op jit(solution)/shard_map/ppermute | solution.py:25
  75.9 29.2 %collective-permute-start.13 = (bf16[8,40,2048]{2,1,0:T(8,128)(2,1)}, bf16[8,40,2048]{2,1,0:T(8,128)(2,1)}, u32[]{:S(2)}, u32[]{:S(2)}) collective-permute-start(bf16[8,40,2048]{2,1,0:T(8,128)(2,1)} %constant_dynamic-update-slice_fusion.4.mine_near), channel_id=1, source_target_pairs={{0,1},{1,0},{2,3},{3,2},{4,5},{5,4},{6,7},{7,6},{8,9},{9,8},{10,11... | collective-permute-start | bytes 3932168 | tf_op jit(solution)/shard_map/ppermute | solution.py:25
  77.4 1.4 copy-start.2
  98.0 20.2 %collective-permute-start.10 = (bf16[8,192,640]{2,1,0:T(8,128)(2,1)}, bf16[8,192,640]{2,1,0:T(8,128)(2,1)}, u32[]{:S(2)}, u32[]{:S(2)}) collective-permute-start(bf16[8,192,640]{2,1,0:T(8,128)(2,1)} %pad_maximum_fusion.1), channel_id=1, source_target_pairs={{0,2},{2,0},{4,6},{6,4},{8,10},{10,8},{12,14},{14,12},{16,18},{18,... | collective-permute-start | bytes 5898248 | tf_op jit(solution)/shard_map/ppermute | solution.py:25
  98.0 20.2 %collective-permute-start.12 = (bf16[8,40,2048]{2,1,0:T(8,128)(2,1)}, bf16[8,40,2048]{2,1,0:T(8,128)(2,1)S(1)}, u32[]{:S(2)}, u32[]{:S(2)}) collective-permute-start(bf16[8,40,2048]{2,1,0:T(8,128)(2,1)} %constant_dynamic-update-slice_fusion.4.mine_near), channel_id=1, source_target_pairs={{0,2},{2,0},{4,6},{6,4},{8,10},{10,8},{12,14},{14,12},{16,18},{18,... | collective-permute-start | bytes 3932168 | tf_op jit(solution)/shard_map/ppermute | solution.py:25
  105.2 13.1 %collective-permute-start.14 = (bf16[8,40,2048]{2,1,0:T(8,128)(2,1)}, bf16[8,40,2048]{2,1,0:T(8,128)(2,1)S(1)}, u32[]{:S(2)}, u32[]{:S(2)}) collective-permute-start(bf16[8,40,2048]{2,1,0:T(8,128)(2,1)} %collective-permute-done.13.other_near), channel_id=1, source_target_pairs={{0,2},{2,0},{4,6},{6,4},{8,10},{10,8},{12,14},{14,12},{16,18},{18,... | collective-permute-start | bytes 3932168 | tf_op jit(solution)/shard_map/ppermute | solution.py:25
  118.2 1.5 copy-start.14
  190.2 11.1 %collective-permute-start.15 = (bf16[2,8,40,2048]{3,2,1,0:T(8,128)(2,1)}, bf16[2,8,40,2048]{3,2,1,0:T(8,128)(2,1)}, u32[]{:S(2)}, u32[]{:S(2)}) collective-permute-start(bf16[2,8,40,2048]{3,2,1,0:T(8,128)(2,1)} %get-tuple-element.104), channel_id=1, source_target_pairs={{0,2},{2,0},{4,6},{6,4},{8,10},{10,8},{12,14},{14,12},{16,18},{18,... | collective-permute-start | bytes 7864328 | tf_op jit(solution)/shard_map/ppermute | solution.py:25
  190.8 10.4 %collective-permute-start.16 = (bf16[8,2,96,640]{3,2,1,0:T(8,128)(2,1)}, bf16[8,2,96,640]{3,2,1,0:T(8,128)(2,1)S(1)}, u32[]{:S(2)}, u32[]{:S(2)}) collective-permute-start(bf16[8,2,96,640]{3,2,1,0:T(8,128)(2,1)} %get-tuple-element.105), channel_id=1, source_target_pairs={{0,2},{2,0},{4,6},{6,4},{8,10},{10,8},{12,14},{14,12},{16,18},{18,... | collective-permute-start | bytes 5898248 | tf_op jit(solution)/shard_map/ppermute | solution.py:25
  201.2 1.3 copy-start.6
  202.6 5.6 %copy-start.7 = (bf16[8,2,96,640]{3,2,1,0:T(8,128)(2,1)S(1)}, bf16[8,2,96,640]{3,2,1,0:T(8,128)(2,1)}, u32[]{:S(2)}) copy-start(bf16[8,2,96,640]{3,2,1,0:T(8,128)(2,1)} %copy-done.6) | copy-start | bytes 5898244
  206.5 1.7 copy-start.5
  206.6 34.6 %collective-permute-start.18 = (bf16[2,1,2,2,40,2048]{5,4,3,2,1,0:T(8,128)(2,1)S(1)}, bf16[2,1,2,2,40,2048]{5,4,3,2,1,0:T(8,128)(2,1)}, u32[]{:S(2)}, u32[]{:S(2)}) collective-permute-start(bf16[2,1,2,2,40,2048]{5,4,3,2,1,0:T(8,128)(2,1)S(1)} %split.99), channel_id=1, source_target_pairs={{0,4},{2,6},{4,0},{6,2},{8,12},{10,14},{12,8},{14,10},{16,20},{18,... | collective-permute-start | bytes 3932168 | tf_op jit(solution)/shard_map/ppermute | solution.py:25
  208.8 1.3 copy-start
  211.1 28.3 %collective-permute-start.17 = (bf16[2,1,2,2,96,640]{5,4,3,2,1,0:T(8,128)(2,1)}, bf16[2,1,2,2,96,640]{5,4,3,2,1,0:T(8,128)(2,1)}, u32[]{:S(2)}, u32[]{:S(2)}) collective-permute-start(bf16[2,1,2,2,96,640]{5,4,3,2,1,0:T(8,128)(2,1)} %split.97), channel_id=1, source_target_pairs={{0,8},{2,10},{4,12},{6,14},{8,0},{10,2},{12,4},{14,6},{16,24},{18,... | collective-permute-start | bytes 2949128 | tf_op jit(solution)/shard_map/ppermute | solution.py:25
  241.2 2.0 copy-start.15
  241.2 4.8 %copy-start.9 = (bf16[2,8,40,896]{3,2,1,0:T(8,128)(2,1)S(1)}, bf16[2,8,40,896]{3,2,1,0:T(8,128)(2,1)}, u32[]{:S(2)}) copy-start(bf16[2,8,40,896]{3,2,1,0:T(8,128)(2,1)} %get-tuple-element.128) | copy-start | bytes 3440644
  243.2 2.9 collective-permute-start.20
  246.3 4.4 %copy-start.12 = (bf16[1024,640]{1,0:T(8,128)(2,1)S(1)}, bf16[1024,640]{1,0:T(8,128)(2,1)}, u32[]{:S(2)}) copy-start(bf16[1024,640]{1,0:T(8,128)(2,1)} %get-tuple-element.127) | copy-start | bytes 3932164
  246.4 15.9 %collective-permute-start.21 = (bf16[2,1,2,2,40,896]{5,4,3,2,1,0:T(8,128)(2,1)S(1)}, bf16[2,1,2,2,40,896]{5,4,3,2,1,0:T(8,128)(2,1)S(1)}, u32[]{:S(2)}, u32[]{:S(2)}) collective-permute-start(bf16[2,1,2,2,40,896]{5,4,3,2,1,0:T(8,128)(2,1)S(1)} %split.101), channel_id=1, source_target_pairs={{0,4},{2,6},{4,0},{6,2},{8,12},{10,14},{12,8},{14,10},{16,20},{18,... | collective-permute-start | bytes 1720328 | tf_op jit(solution)/shard_map/ppermute | solution.py:25
  247.9 24.2 %collective-permute-start.24 = (bf16[1,1,2,2,96,640]{5,4,3,2,1,0:T(8,128)(2,1)S(1)}, bf16[1,1,2,2,96,640]{5,4,3,2,1,0:T(8,128)(2,1)S(1)}, u32[]{:S(2)}, u32[]{:S(2)}) collective-permute-start(bf16[1,1,2,2,96,640]{5,4,3,2,1,0:T(8,128)(2,1)S(1)} %split.107), channel_id=1, source_target_pairs={{0,4},{2,6},{4,0},{6,2},{8,12},{10,14},{12,8},{14,10},{16,20},{18,... | collective-permute-start | bytes 1474568 | tf_op jit(solution)/shard_map/ppermute | solution.py:25
  248.6 23.6 %collective-permute-start.23 = (bf16[2,1,1,2,40,2048]{5,4,3,2,1,0:T(8,128)(2,1)S(1)}, bf16[2,1,1,2,40,2048]{5,4,3,2,1,0:T(8,128)(2,1)S(1)}, u32[]{:S(2)}, u32[]{:S(2)}) collective-permute-start(bf16[2,1,1,2,40,2048]{5,4,3,2,1,0:T(8,128)(2,1)S(1)} %split.105), channel_id=1, source_target_pairs={{0,8},{2,10},{4,12},{6,14},{8,0},{10,2},{12,4},{14,6},{16,24},{18,... | collective-permute-start | bytes 1966088 | tf_op jit(solution)/shard_map/ppermute | solution.py:25
  250.7 57.7 %collective-permute-start.19 = (bf16[1024,640]{1,0:T(8,128)(2,1)S(1)}, bf16[1024,640]{1,0:T(8,128)(2,1)S(1)}, u32[]{:S(2)}, u32[]{:S(2)}) collective-permute-start(bf16[1024,640]{1,0:T(8,128)(2,1)S(1)} %copy-done.12), channel_id=1, source_target_pairs={{1,0},{3,2},{5,4},{7,6},{9,8},{11,10},{13,12},{15,14},{17,16},{19,... | collective-permute-start | bytes 3932168 | tf_op jit(solution)/shard_map/ppermute | solution.py:71
  272.2 17.3 %collective-permute-start.27 = (bf16[1,1,2,1,96,640]{5,4,3,2,1,0:T(8,128)(2,1)S(1)}, bf16[1,1,2,1,96,640]{5,4,3,2,1,0:T(8,128)(2,1)S(1)}, u32[]{:S(2)}, u32[]{:S(2)}) collective-permute-start(bf16[1,1,2,1,96,640]{5,4,3,2,1,0:T(8,128)(2,1)S(1)} %split.113), channel_id=1, source_target_pairs={{0,1},{1,0},{2,3},{3,2},{4,5},{5,4},{6,7},{7,6},{8,9},{9,8},{10,11... | collective-permute-start | bytes 737288 | tf_op jit(solution)/shard_map/ppermute | solution.py:25
  273.8 7.9 %collective-permute-start.22 = (bf16[2,1,1,2,40,896]{5,4,3,2,1,0:T(8,128)(2,1)S(1)}, bf16[2,1,1,2,40,896]{5,4,3,2,1,0:T(8,128)(2,1)S(1)}, u32[]{:S(2)}, u32[]{:S(2)}) collective-permute-start(bf16[2,1,1,2,40,896]{5,4,3,2,1,0:T(8,128)(2,1)S(1)} %split.103), channel_id=1, source_target_pairs={{0,8},{2,10},{4,12},{6,14},{8,0},{10,2},{12,4},{14,6},{16,24},{18,... | collective-permute-start | bytes 860168 | tf_op jit(solution)/shard_map/ppermute | solution.py:25
  276.0 20.5 %collective-permute-start.26 = (bf16[1,1,1,2,40,2048]{5,4,3,2,1,0:T(8,128)(2,1)S(1)}, bf16[1,1,1,2,40,2048]{5,4,3,2,1,0:T(8,128)(2,1)S(1)}, u32[]{:S(2)}, u32[]{:S(2)}) collective-permute-start(bf16[1,1,1,2,40,2048]{5,4,3,2,1,0:T(8,128)(2,1)S(1)} %split.111), channel_id=1, source_target_pairs={{0,1},{1,0},{2,3},{3,2},{4,5},{5,4},{6,7},{7,6},{8,9},{9,8},{10,11... | collective-permute-start | bytes 983048 | tf_op jit(solution)/shard_map/ppermute | solution.py:25
  281.9 26.6 %copy-start.4 = (f32[1024,640]{1,0:T(8,128)S(1)}, f32[1024,640]{1,0:T(8,128)}, u32[]{:S(2)}) copy-start(f32[1024,640]{1,0:T(8,128)} %get-tuple-element.122) | copy-start | bytes 7864324
  289.7 7.1 %collective-permute-start.30 = (bf16[1,1,1,1,96,640]{5,4,3,2,1,0:T(8,128)(2,1)S(1)}, bf16[1,1,1,1,96,640]{5,4,3,2,1,0:T(8,128)(2,1)S(1)}, u32[]{:S(2)}, u32[]{:S(2)}) collective-permute-start(bf16[1,1,1,1,96,640]{5,4,3,2,1,0:T(8,128)(2,1)S(1)} %split.119), channel_id=1, source_target_pairs={{0,16},{2,18},{4,20},{6,22},{8,24},{10,26},{12,28},{14,30},{16,0},... | collective-permute-start | bytes 368648 | tf_op jit(solution)/shard_map/ppermute | solution.py:25
  289.7 9.5 %collective-permute-start.25 = (bf16[1,1,1,2,40,896]{5,4,3,2,1,0:T(8,128)(2,1)S(1)}, bf16[1,1,1,2,40,896]{5,4,3,2,1,0:T(8,128)(2,1)S(1)}, u32[]{:S(2)}, u32[]{:S(2)}) collective-permute-start(bf16[1,1,1,2,40,896]{5,4,3,2,1,0:T(8,128)(2,1)S(1)} %split.109), channel_id=1, source_target_pairs={{0,1},{1,0},{2,3},{3,2},{4,5},{5,4},{6,7},{7,6},{8,9},{9,8},{10,11... | collective-permute-start | bytes 430088 | tf_op jit(solution)/shard_map/ppermute | solution.py:25
  296.6 9.6 %collective-permute-start.29 = (bf16[1,1,1,1,40,2048]{5,4,3,2,1,0:T(8,128)(2,1)S(1)}, bf16[1,1,1,1,40,2048]{5,4,3,2,1,0:T(8,128)(2,1)S(1)}, u32[]{:S(2)}, u32[]{:S(2)}) collective-permute-start(bf16[1,1,1,1,40,2048]{5,4,3,2,1,0:T(8,128)(2,1)S(1)} %split.117), channel_id=1, source_target_pairs={{0,16},{2,18},{4,20},{6,22},{8,24},{10,26},{12,28},{14,30},{16,0},... | collective-permute-start | bytes 491528 | tf_op jit(solution)/shard_map/ppermute | solution.py:25
  296.8 13.1 %collective-permute-start.32 = (bf16[96,640]{1,0:T(8,128)(2,1)S(1)}, bf16[96,640]{1,0:T(8,128)(2,1)S(1)}, u32[]{:S(2)}, u32[]{:S(2)}) collective-permute-start(bf16[96,640]{1,0:T(8,128)(2,1)S(1)} %bitcast.60), channel_id=1, source_target_pairs={{0,1},{1,0},{2,3},{3,2},{4,5},{5,4},{6,7},{7,6},{8,9},{9,8},{10,11... | collective-permute-start | bytes 368648 | tf_op jit(solution)/shard_map/ppermute | solution.py:25
  299.3 7.7 %collective-permute-start.28 = (bf16[1,1,1,1,40,896]{5,4,3,2,1,0:T(8,128)(2,1)S(1)}, bf16[1,1,1,1,40,896]{5,4,3,2,1,0:T(8,128)(2,1)S(1)}, u32[]{:S(2)}, u32[]{:S(2)}) collective-permute-start(bf16[1,1,1,1,40,896]{5,4,3,2,1,0:T(8,128)(2,1)S(1)} %split.115), channel_id=1, source_target_pairs={{0,16},{2,18},{4,20},{6,22},{8,24},{10,26},{12,28},{14,30},{16,0},... | collective-permute-start | bytes 215048 | tf_op jit(solution)/shard_map/ppermute | solution.py:25
  306.3 8.9 %collective-permute-start.33 = (bf16[40,2048]{1,0:T(8,128)(2,1)S(1)}, bf16[40,2048]{1,0:T(8,128)(2,1)S(1)}, u32[]{:S(2)}, u32[]{:S(2)}) collective-permute-start(bf16[40,2048]{1,0:T(8,128)(2,1)S(1)} %bitcast.59), channel_id=1, source_target_pairs={{0,1},{1,0},{2,3},{3,2},{4,5},{5,4},{6,7},{7,6},{8,9},{9,8},{10,11... | collective-permute-start | bytes 491528 | tf_op jit(solution)/shard_map/ppermute | solution.py:25
  307.0 5.4 %collective-permute-start.31 = (bf16[40,896]{1,0:T(8,128)(2,1)S(1)}, bf16[40,896]{1,0:T(8,128)(2,1)S(1)}, u32[]{:S(2)}, u32[]{:S(2)}) collective-permute-start(bf16[40,896]{1,0:T(8,128)(2,1)S(1)} %fusion.2), channel_id=1, source_target_pairs={{0,1},{1,0},{2,3},{3,2},{4,5},{5,4},{6,7},{7,6},{8,9},{9,8},{10,11... | collective-permute-start | bytes 215048 | tf_op jit(solution)/shard_map/ppermute | solution.py:25
  (2 other events, 2.1 us)

commit v2 on v1

--- a/solution.py
+++ b/solution.py
@@ -562,10 +562,9 @@
     @pl.when(step == pl.num_programs(0) - 1)
     def _():
         count = info_ref.shape[0] - 3
-        core, span = info_ref[count], info_ref[count + 1]
+        core = info_ref[count]
         total = queries + 2 * head_dim
-        feature_rows = near_ref.shape[2]
-        half = near_ref.shape[3]
+        feature_rows = near_ref.shape[1]
         for start in range(0, queries, 512):
             part = slice(start, start + 512)
             grad_all[:, part] = dot_tn(normed_all[...], draw_all[:, part])
@@ -585,8 +584,7 @@
                 to = near_ref if index % 2 == value else far_ref
                 place = info_ref[index]
                 lines = slice(index * feature_rows, (index + 1) * feature_rows)
-                to[span, place] = grad_all[lines, :half].astype(jnp.bfloat16)
-                to[1 - span, place] = grad_all[lines, half:].astype(jnp.bfloat16)
+                to[place] = grad_all[lines, :].astype(jnp.bfloat16)
 
         each_core(core, store)
 
@@ -668,12 +666,18 @@
     )
     mine_near = jnp.where(low_span, gate_weight, up_weight)[None]
     first_near, tall_near = first_shard[None], tall_shard[None]
-    for mask in chip_masks:
-        first_near = widen(first_near, "fsdp", mask)
-        mine_near = widen(mine_near, "fsdp", mask, first_near)
-        if mask != chip_masks[-1]:
-            tall_near = widen(tall_near, "fsdp", mask, mine_near)
-            mine_near = after(mine_near, tall_near)
+    for step, mask in enumerate(chip_masks):
+        if step == len(chip_masks) - 1:
+            mine_near = after(mine_near, tall_first, before)
+        mine_near = widen(mine_near, "fsdp", mask)
+        first_near = widen(first_near, "fsdp", mask, mine_near)
+        if step == 0:
+            tall_near = after(tall_near, mine_near)
+        if step < len(chip_masks) - 1:
+            tall_near = widen(tall_near, "fsdp", mask)
+        if step == 0:
+            tall_first = tall_near
+    first_near = after(first_near, tall_near)
     first_far = swap(first_near, "fsdp", 1)
     mine_far = swap(mine_near, "fsdp", 1)
     other_near = swap(mine_near, "ctx", 1)
@@ -844,8 +848,8 @@
         out_shape=[
             f32(total, model_width),
             bf16(total, model_width),
-            bf16(2, chips, rows, first_columns // 2),
-            bf16(2, chips, rows, first_columns // 2),
+            bf16(chips, rows, first_columns),
+            bf16(chips, rows, first_columns),
         ],
         scratch_shapes=[
             scratch(total, model_width),
@@ -884,30 +888,31 @@
     wide_kept, wide_come = folded(wide, "fsdp", near_masks[1], 2)
     before_come = shifted(before_part, "ctx", -1)
     first = add(first_grad_near, swap(first_grad_far, "fsdp", 1))
-    first = first.reshape((2,) + bits + first.shape[2:])
-    first_kept, first_come = folded(first, "fsdp", near_masks[0], 1)
+    first = first.reshape(bits + first.shape[1:])
+    first_kept, first_come = folded(first, "fsdp", near_masks[0], 0)
     first = add(first_kept, first_come)
-    first_kept, first_come = folded(first, "fsdp", near_masks[1], 2)
+    first_kept, first_come = folded(first, "fsdp", near_masks[1], 1)
     tall = add(tall_kept, after(tall_come, first))
     tall_kept, tall_come = folded(tall, "ctx", 1, len(bits))
     wide = add(wide_kept, after(wide_come, tall))
     wide_kept, wide_come = folded(wide, "ctx", 1, 0)
-    first = add(first_kept, after(first_come, wide))
-    first_kept, first_come = folded(first, "ctx", 1, 0)
-    tall = add(tall_kept, after(tall_come, first))
-    wide = add(wide_kept, after(wide_come, tall))
-    first = add(first_kept, after(first_come, wide))
     for index in range(2, len(bits)):
         mask = (near_masks + [far_mask])[index]
+        first = add(first_kept, after(first_come, wide))
+        first_kept, first_come = folded(first, "fsdp", mask, index)
+        if index == 2:
+            tall = add(tall_kept, after(tall_come, first))
         tall_kept, tall_come = folded(tall, "fsdp", mask, index)
+        if index == 2:
+            wide = add(wide_kept, after(wide_come, tall))
         wide_kept, wide_come = folded(wide, "fsdp", mask, index + 1)
-        first_kept, first_come = folded(first, "fsdp", mask, index + 1)
-        tall = add(tall_kept, tall_come)
+        tall = add(tall_kept, after(tall_come, first))
         wide = add(wide_kept, after(wide_come, tall))
-        first = add(first_kept, after(first_come, wide))
+    first = add(first_kept, after(first_come, tall))
     tall = other_spans(tall.reshape(tall.shape[-2:]), "ctx")
     wide = other_spans(wide.reshape(wide.shape[-2:]), "ctx")
     first = other_spans(first.reshape(first.shape[-2:]), "ctx")
+    first_come = swap(first, "ctx", 1)
     before_come = after(before_come, first)
     token_grad = (token_part + before_come.astype(jnp.float32)).astype(jnp.bfloat16)
 
@@ -919,7 +924,7 @@
 
     grad_gate, grad_up = both(wide)
     grad_tall = jnp.concatenate(both(tall), axis=0)
-    grad_first = jnp.concatenate(both(first), axis=1)
+    grad_first = first.astype(jnp.float32) + first_come.astype(jnp.float32)
     return (
         block_output.reshape(tokens.shape),
         token_grad.reshape(tokens.shape),

time: 320 us -> 312 us (0.975)
  waiting for transfers between devices: 114 us -> 106 us
  starting transfers between devices: 33 us -> 36.2 us
    ppermute x32 -> x31, waiting for transfers between devices: 114 us -> 105 us  [swap(): lax.ppermute(value, axis, [(source, source ^ mask) for source in range(co...]
    concatenate x2 -> x1, other arithmetic: 5.53 us -> 1.57 us  [per_device(): jnp.concatenate([tall_near, after(tall_late, query_low)], axis=0)]
    ppermute x32 -> x31, starting transfers between devices: 28.3 us -> 31.4 us  [swap(): lax.ppermute(value, axis, [(source, source ^ mask) for source in range(co...]
    convert_element_type x14 -> x12, other arithmetic: 9.2 us -> 10.5 us  [add(): (left.astype(jnp.float32) + right.astype(jnp.float32)).astype(jnp.bfloat16)]
    unnamed x35 -> x30, local copies, waits for them, and re-layouts: 6.45 us -> 6.47 us
  transfers between devices with their start and end apart: 34 -> 33, of which waited for: 17 -> 19; matrix products, arithmetic and copies ran while one was open for 8% -> 7% of each run, Pallas kernels for 18% -> 19%
where the time goes in v2:
time: 312 us; the launch traced here: 309 us
  Pallas kernels  129 us (41%)
  waiting for transfers between devices  106 us (34%)
  starting transfers between devices  36.2 us (12%)
  other arithmetic  23.5 us (8%)
  local copies, waits for them, and re-layouts  12.9 us (4%)
    ppermute x31, waiting for transfers between devices, swap(): lax.ppermute(value, axis, [(source, source ^ mask) for source in range(co...  105 us
    pallas_call x1, Pallas kernels, per_device(): pl.pallas_call(functools.partial(middle_kernel, 512, down_rows), grid=(st...  70.3 us
    ppermute x31, starting transfers between devices, swap(): lax.ppermute(value, axis, [(source, source ^ mask) for source in range(co...  31.4 us
    pallas_call x2, Pallas kernels, attention_back(): pl.pallas_call(functools.partial(attention_back_kernel, score_scale), gri...  20.8 us
    pallas_call x1, Pallas kernels, per_device(): pl.pallas_call(functools.partial(head_back_kernel, head_dim), grid=(steps...  18 us
    convert_element_type x12, other arithmetic, add(): (left.astype(jnp.float32) + right.astype(jnp.float32)).astype(jnp.bfloat16)  10.5 us
    pallas_call x1, Pallas kernels, per_device(): pl.pallas_call(functools.partial(attention_kernel, score_scale), grid=(se...  10.3 us
    pallas_call x1, Pallas kernels, per_device(): pl.pallas_call(functools.partial(projection_kernel, head_dim, qkv_columns...  9.26 us
  transfers between devices with their start and end apart: 33, of which 19 were waited for; matrix products, arithmetic and copies ran while one was open for 7% of the time, Pallas kernels for 19%

profile of v2, /device:TPU:0, one launch (start us, length us, event | category | flops | bytes accessed | tf_op | source)
XLA Modules:
  0.0 308.6 jit_solution(1613615678612957338)
XLA Ops:
  1.7 4.1 %collective-permute-start.2 = (bf16[1,40,2048]{2,1,0:T(8,128)(2,1)S(1)}, bf16[1,40,2048]{2,1,0:T(8,128)(2,1)S(1)}, u32[]{:S(2)}, u32[]{:S(2)}) collective-permute-start(bf16[1,40,2048]{2,1,0:T(8,128)(2,1)S(1)} %select_bitcast_fusion), channel_id=1, source_target_pairs={{0,16},{2,18},{4,20},{6,22},{8,24},{10,26},{12,28},{14,30},{16,0},... | collective-permute-start | bytes 491528 | tf_op jit(solution)/shard_map/ppermute | solution.py:25
  5.8 3.5 %collective-permute-start = (bf16[2,512,640]{2,1,0:T(8,128)(2,1)}, bf16[2,512,640]{2,1,0:T(8,128)(2,1)S(1)}, u32[]{:S(2)}, u32[]{:S(2)}) collective-permute-start(bf16[2,512,640]{2,1,0:T(8,128)(2,1)} %param.15), channel_id=1, source_target_pairs={{0,1},{2,3},{4,5},{6,7},{8,9},{10,11},{12,13},{14,15},{16,17},{18,... | collective-permute-start | bytes 3932168 | tf_op jit(solution)/shard_map/ppermute | solution.py:71
  10.8 3.0 multiply_sine_fusion
  16.8 2.7 collective-permute-start.6
  19.4 1.6 collective-permute-start.4
  21.0 10.7 %collective-permute-done.1 = bf16[1,40,1792]{2,1,0:T(8,128)(2,1)S(1)} collective-permute-done((bf16[1,40,1792]{2,1,0:T(8,128)(2,1)S(1)}, bf16[1,40,1792]{2,1,0:T(8,128)(2,1)S(1)}, u32[]{:S(2)}, u32[]{:S(2)}) %collective-permute-start.1) | collective-permute-done | bytes 143392 | tf_op jit(solution)/shard_map/ppermute | solution.py:25
  31.8 4.0 %collective-permute-done.6 = bf16[1,192,640]{2,1,0:T(8,128)(2,1)S(1)} collective-permute-done((bf16[1,192,640]{2,1,0:T(8,128)(2,1)S(1)}, bf16[1,192,640]{2,1,0:T(8,128)(2,1)S(1)}, u32[]{:S(2)}, u32[]{:S(2)}) %collective-permute-start.6) | collective-permute-done | bytes 245792 | tf_op jit(solution)/shard_map/ppermute | solution.py:25
  37.2 1.5 collective-permute-start.7
  38.7 1.6 collective-permute-start.8
  40.3 1.7 collective-permute-done.3
  42.1 1.6 collective-permute-start.5
  43.7 8.8 %collective-permute-done.8 = bf16[2,192,640]{2,1,0:T(8,128)(2,1)S(1)} collective-permute-done((bf16[2,192,640]{2,1,0:T(8,128)(2,1)S(1)}, bf16[2,192,640]{2,1,0:T(8,128)(2,1)S(1)}, u32[]{:S(2)}, u32[]{:S(2)}) %collective-permute-start.8) | collective-permute-done | bytes 491552 | tf_op jit(solution)/shard_map/ppermute | solution.py:25
  53.4 1.5 collective-permute-done.7
  54.9 1.3 pad_maximum_fusion.1.mine_near
  56.2 8.6 %collective-permute-done.5 = bf16[4,40,1792]{2,1,0:T(8,128)(2,1)S(1)} collective-permute-done((bf16[4,40,1792]{2,1,0:T(8,128)(2,1)S(1)}, bf16[4,40,1792]{2,1,0:T(8,128)(2,1)S(1)}, u32[]{:S(2)}, u32[]{:S(2)}) %collective-permute-start.5) | collective-permute-done | bytes 573472 | tf_op jit(solution)/shard_map/ppermute | solution.py:25
  65.0 1.6 collective-permute-start.10
  66.6 2.4 collective-permute-start.13
  70.0 9.3 %projection.1 = (bf16[1024,1024]{1,0:T(8,128)(2,1)}, bf16[1024,256]{1,0:T(8,128)(2,1)}, bf16[1024,256]{1,0:T(8,128)(2,1)}, bf16[1024,256]{1,0:T(8,128)(2,1)}, bf...) custom-call(bf16[1024,640]{1,0:T(8,128)(2,1)} %bitcast.39, ...), custom_call_target="tpu_custom_call" | custom-call | flops 671088640 | tf_op jit(solution)/shard_map/projection/pallas_call | solution.py:720
  79.3 10.0 %collective-permute-done.10 = bf16[4,192,640]{2,1,0:T(8,128)(2,1)} collective-permute-done((bf16[4,192,640]{2,1,0:T(8,128)(2,1)S(1)}, bf16[4,192,640]{2,1,0:T(8,128)(2,1)}, u32[]{:S(2)}, u32[]{:S(2)}) %collective-permute-start.10) | collective-permute-done | bytes 983072 | tf_op jit(solution)/shard_map/ppermute | solution.py:25
  89.3 1.6 pad_maximum_fusion
  91.4 6.9 %collective-permute-done.13.other_near = bf16[8,40,2048]{2,1,0:T(8,128)(2,1)} collective-permute-done((bf16[8,40,2048]{2,1,0:T(8,128)(2,1)}, bf16[8,40,2048]{2,1,0:T(8,128)(2,1)}, u32[]{:S(2)}, u32[]{:S(2)}) %collective-permute-start.13) | collective-permute-done | bytes 1310752 | tf_op jit(solution)/shard_map/ppermute | solution.py:25
  98.4 10.3 %attention.1.att_ref = bf16[1024,1024]{1,0:T(8,128)(2,1)} custom-call(s32[19]{0:T(128)} %pad_add_fusion.info_ref.flag_ref, bf16[1024,1024]{1,0:T(8,128)(2,1)} %get-tuple-element.89.q_ref, bf16[1024,256]{1,0:T(8,128)(2,1)} %get-tuple-element.90.k_ref, bf16[1024,256]{1,0:T(8,128)(2,1)} %get-tuple-element.91.v_ref, bf16[1024,256]{1,0:T(8,128)(2,1)} %get-tuple-element.92.kb_ref, ...), custom_call_target="tpu_custom_call" | custom-call | flops 719023552 | tf_op jit(solution)/shard_map/attention/pallas_call | solution.py:739
  109.7 70.3 %middle.1 = (bf16[1024,640]{1,0:T(8,128)(2,1)}, f32[1024,640]{1,0:T(8,128)}, bf16[1024,1024]{1,0:T(8,128)(2,1)}, f32[8,640]{1,0:T(8,128)}, bf16[2,8,40,2048]{3,2...) custom-call(bf16[1024,640]{1,0:T(8,128)(2,1)} %bitcast.40, ...), custom_call_target="tpu_custom_call" | custom-call | flops 4404019200 | tf_op jit(solution)/shard_map/middle/pallas_call | solution.py:761
  180.7 10.4 %attention_back.2 = (f32[1024,1024]{1,0:T(8,128)}, f32[1024,256]{1,0:T(8,128)}, f32[1024,256]{1,0:T(8,128)}, f32[1024,256]{1,0:T(8,128)}, f32[1024,256]{1,0:T(8,128)}) custom-call(s32[19]{0:T(128)} %pad_add_fusion.info_ref.flag_ref, bf16[1024,1024]{1,0:T(8,128)(2,1)} %get-tuple-element.89.q_ref, bf16[1024,256]{1,0:T(8,128)(2,1)} %get-tuple-element.90.k_ref, ...), custom_call_target="tpu_custom_call" | custom-call | flops 629145600 | tf_op jit(solution)/shard_map/attention_back/pallas_call | solution.py:812
  191.1 1.5 copy-done.4
  192.6 3.8 %add_convert_fusion = bf16[2,8,40,2048]{3,2,1,0:T(8,128)(2,1)S(1)} fusion(bf16[2,8,40,2048]{3,2,1,0:T(8,128)(2,1)} %copy-done.4, bf16[2,8,40,2048]{3,2,1,0:T(8,128)(2,1)} %get-tuple-element.101), kind=kLoop, calls=%fused_computation | loop fusion | flops 5242880 | bytes 7864320 | tf_op jit(solution)/shard_map/convert_element_type | solution.py:52
  197.9 2.1 add_convert_fusion.1
  200.0 1.3 copy-done
  202.3 1.6 collective-permute-start.17
  203.9 10.4 %attention_back.3 = (f32[1024,1024]{1,0:T(8,128)}, f32[1024,256]{1,0:T(8,128)}, f32[1024,256]{1,0:T(8,128)}, f32[1024,256]{1,0:T(8,128)}, f32[1024,256]{1,0:T(8,128)}) custom-call(s32[19]{0:T(128)} %pad_add_fusion.info_ref.flag_ref, ...), custom_call_target="tpu_custom_call", output_to_operand_aliasing={{0}: (7, {}), {1}: (8, {}), {2}: (9, {}), {3}: (10, {}), {4... | custom-call | flops 629145600 | tf_op jit(solution)/shard_map/attention_back/pallas_call | solution.py:812
  214.3 18.0 %head_back.1 = (f32[1024,640]{1,0:T(8,128)}, bf16[1024,640]{1,0:T(8,128)(2,1)}, bf16[8,40,1792]{2,1,0:T(8,128)(2,1)}, bf16[8,40,1792]{2,1,0:T(8,128)(2,1)}) custom-call(bf16[1024,640]{1,0:T(8,128)(2,1)} %bitcast.41, bf16[1024,640]{1,0:T(8,128)(2,1)} %bitcast.43, bf16[640,1536]{1,0:T(8,128)(2,1)} %get-tuple-element.98.w_ref, ...), custom_call_target="tpu_custom_call" | custom-call | flops 1324516992 | tf_op jit(solution)/shard_map/head_back/pallas_call | solution.py:837
  232.3 1.7 add_convert_fusion.5
  234.1 2.0 add_convert_fusion.3
  236.4 2.6 collective-permute-done.20
  240.2 1.4 collective-permute-start.24
  242.1 1.3 collective-permute-start.19
  243.4 11.8 %collective-permute-done.21 = bf16[1,2,2,40,1792]{4,3,2,1,0:T(8,128)(2,1)S(1)} collective-permute-done((bf16[1,2,2,40,1792]{4,3,2,1,0:T(8,128)(2,1)S(1)}, bf16[1,2,2,40,1792]{4,3,2,1,0:T(8,128)(2,1)S(1)}, u32[]{:S(2)}, u32[]{:S(2)}) %collective-permute-start.21) | collective-permute-done | bytes 573472 | tf_op jit(solution)/shard_map/ppermute | solution.py:25
  255.4 9.6 %collective-permute-done.24 = bf16[1,1,2,2,96,640]{5,4,3,2,1,0:T(8,128)(2,1)S(1)} collective-permute-done((bf16[1,1,2,2,96,640]{5,4,3,2,1,0:T(8,128)(2,1)S(1)}, bf16[1,1,2,2,96,640]{5,4,3,2,1,0:T(8,128)(2,1)S(1)}, u32[]{:S(2)}, u32[]{:S(2)}) %collective-permute-start.24) | collective-permute-done | bytes 491552 | tf_op jit(solution)/shard_map/ppermute | solution.py:25
  265.2 1.8 collective-permute-start.26
  268.1 6.8 %collective-permute-done.22 = bf16[1,1,2,40,1792]{4,3,2,1,0:T(8,128)(2,1)S(1)} collective-permute-done((bf16[1,1,2,40,1792]{4,3,2,1,0:T(8,128)(2,1)S(1)}, bf16[1,1,2,40,1792]{4,3,2,1,0:T(8,128)(2,1)S(1)}, u32[]{:S(2)}, u32[]{:S(2)}) %collective-permute-start.22) | collective-permute-done | bytes 286752 | tf_op jit(solution)/shard_map/ppermute | solution.py:25
  274.9 6.1 %collective-permute-done.26 = bf16[1,1,2,1,96,640]{5,4,3,2,1,0:T(8,128)(2,1)S(1)} collective-permute-done((bf16[1,1,2,1,96,640]{5,4,3,2,1,0:T(8,128)(2,1)S(1)}, bf16[1,1,2,1,96,640]{5,4,3,2,1,0:T(8,128)(2,1)S(1)}, u32[]{:S(2)}, u32[]{:S(2)}) %collective-permute-start.26) | collective-permute-done | bytes 245792 | tf_op jit(solution)/shard_map/ppermute | solution.py:25
  281.5 2.6 collective-permute-start.25
  284.1 2.3 collective-permute-done.30
  286.9 7.8 %collective-permute-done.27 = bf16[1,1,1,1,96,640]{5,4,3,2,1,0:T(8,128)(2,1)S(1)} collective-permute-done((bf16[1,1,1,1,96,640]{5,4,3,2,1,0:T(8,128)(2,1)S(1)}, bf16[1,1,1,1,96,640]{5,4,3,2,1,0:T(8,128)(2,1)S(1)}, u32[]{:S(2)}, u32[]{:S(2)}) %collective-permute-start.27) | collective-permute-done | bytes 122912 | tf_op jit(solution)/shard_map/ppermute | solution.py:25
  294.8 3.0 collective-permute-done.25
  297.9 1.4 add_convert_fusion.2
  299.9 1.5 collective-permute-start.32
  302.8 1.7 collective-permute-done.28
  (113 shorter events, 24.3 us)
Async XLA Ops:
  0.6 16.0 %copy-start.10 = (bf16[128,640]{1,0:T(8,128)(2,1)S(1)}, bf16[128,640]{1,0:T(8,128)(2,1)}, u32[]{:S(2)}) copy-start(bf16[128,640]{1,0:T(8,128)(2,1)} %param.28) | copy-start | bytes 491524
  0.7 16.0 %copy-start.11 = (bf16[64,640]{1,0:T(8,128)(2,1)S(1)}, bf16[64,640]{1,0:T(8,128)(2,1)}, u32[]{:S(2)}) copy-start(bf16[64,640]{1,0:T(8,128)(2,1)} %param.23) | copy-start | bytes 245764
  1.7 15.0 %collective-permute-start.2 = (bf16[1,40,2048]{2,1,0:T(8,128)(2,1)S(1)}, bf16[1,40,2048]{2,1,0:T(8,128)(2,1)S(1)}, u32[]{:S(2)}, u32[]{:S(2)}) collective-permute-start(bf16[1,40,2048]{2,1,0:T(8,128)(2,1)S(1)} %select_bitcast_fusion), channel_id=1, source_target_pairs={{0,16},{2,18},{4,20},{6,22},{8,24},{10,26},{12,28},{14,30},{16,0},... | collective-permute-start | bytes 491528 | tf_op jit(solution)/shard_map/ppermute | solution.py:25
  5.8 31.5 %collective-permute-start = (bf16[2,512,640]{2,1,0:T(8,128)(2,1)}, bf16[2,512,640]{2,1,0:T(8,128)(2,1)S(1)}, u32[]{:S(2)}, u32[]{:S(2)}) collective-permute-start(bf16[2,512,640]{2,1,0:T(8,128)(2,1)} %param.15), channel_id=1, source_target_pairs={{0,1},{2,3},{4,5},{6,7},{8,9},{10,11},{12,13},{14,15},{16,17},{18,... | collective-permute-start | bytes 3932168 | tf_op jit(solution)/shard_map/ppermute | solution.py:71
  16.3 15.4 %collective-permute-start.1 = (bf16[1,40,1792]{2,1,0:T(8,128)(2,1)S(1)}, bf16[1,40,1792]{2,1,0:T(8,128)(2,1)S(1)}, u32[]{:S(2)}, u32[]{:S(2)}) collective-permute-start(bf16[1,40,1792]{2,1,0:T(8,128)(2,1)S(1)} %bitcast.44), channel_id=1, source_target_pairs={{0,16},{2,18},{4,20},{6,22},{8,24},{10,26},{12,28},{14,30},{16,0},... | collective-permute-start | bytes 430088 | tf_op jit(solution)/shard_map/ppermute | solution.py:25
  16.8 19.1 %collective-permute-start.6 = (bf16[1,192,640]{2,1,0:T(8,128)(2,1)S(1)}, bf16[1,192,640]{2,1,0:T(8,128)(2,1)S(1)}, u32[]{:S(2)}, u32[]{:S(2)}) collective-permute-start(bf16[1,192,640]{2,1,0:T(8,128)(2,1)S(1)} %maximum_bitcast_fusion), channel_id=1, source_target_pairs={{0,16},{2,18},{4,20},{6,22},{8,24},{10,26},{12,28},{14,30},{16,0},... | collective-permute-start | bytes 737288 | tf_op jit(solution)/shard_map/ppermute | solution.py:25
  19.4 16.5 %collective-permute-start.4 = (bf16[2,40,2048]{2,1,0:T(8,128)(2,1)S(1)}, bf16[2,40,2048]{2,1,0:T(8,128)(2,1)S(1)}, u32[]{:S(2)}, u32[]{:S(2)}) collective-permute-start(bf16[2,40,2048]{2,1,0:T(8,128)(2,1)S(1)} %pad_maximum_fusion.8), channel_id=1, source_target_pairs={{0,8},{2,10},{4,12},{6,14},{8,0},{10,2},{12,4},{14,6},{16,24},{18,... | collective-permute-start | bytes 983048 | tf_op jit(solution)/shard_map/ppermute | solution.py:25
  31.8 10.3 %collective-permute-start.3 = (bf16[2,40,1792]{2,1,0:T(8,128)(2,1)S(1)}, bf16[2,40,1792]{2,1,0:T(8,128)(2,1)S(1)}, u32[]{:S(2)}, u32[]{:S(2)}) collective-permute-start(bf16[2,40,1792]{2,1,0:T(8,128)(2,1)S(1)} %pad_maximum_fusion.9), channel_id=1, source_target_pairs={{0,8},{2,10},{4,12},{6,14},{8,0},{10,2},{12,4},{14,6},{16,24},{18,... | collective-permute-start | bytes 860168 | tf_op jit(solution)/shard_map/ppermute | solution.py:25
  37.2 18.9 %copy-start.1 = (bf16[2,512,640]{2,1,0:T(8,128)(2,1)}, bf16[2,512,640]{2,1,0:T(8,128)(2,1)S(1)}, u32[]{:S(2)}) copy-start(bf16[2,512,640]{2,1,0:T(8,128)(2,1)S(1)} %collective-permute-done) | copy-start | bytes 3932164
  37.2 17.7 %collective-permute-start.7 = (bf16[4,40,2048]{2,1,0:T(8,128)(2,1)S(1)}, bf16[4,40,2048]{2,1,0:T(8,128)(2,1)S(1)}, u32[]{:S(2)}, u32[]{:S(2)}) collective-permute-start(bf16[4,40,2048]{2,1,0:T(8,128)(2,1)S(1)} %pad_maximum_fusion.4), channel_id=1, source_target_pairs={{0,4},{2,6},{4,0},{6,2},{8,12},{10,14},{12,8},{14,10},{16,20},{18,... | collective-permute-start | bytes 1966088 | tf_op jit(solution)/shard_map/ppermute | solution.py:25
  38.7 13.7 %collective-permute-start.8 = (bf16[2,192,640]{2,1,0:T(8,128)(2,1)S(1)}, bf16[2,192,640]{2,1,0:T(8,128)(2,1)S(1)}, u32[]{:S(2)}, u32[]{:S(2)}) collective-permute-start(bf16[2,192,640]{2,1,0:T(8,128)(2,1)S(1)} %pad_maximum_fusion.6), channel_id=1, source_target_pairs={{0,8},{2,10},{4,12},{6,14},{8,0},{10,2},{12,4},{14,6},{16,24},{18,... | collective-permute-start | bytes 1474568 | tf_op jit(solution)/shard_map/ppermute | solution.py:25
  42.1 22.7 %collective-permute-start.5 = (bf16[4,40,1792]{2,1,0:T(8,128)(2,1)S(1)}, bf16[4,40,1792]{2,1,0:T(8,128)(2,1)S(1)}, u32[]{:S(2)}, u32[]{:S(2)}) collective-permute-start(bf16[4,40,1792]{2,1,0:T(8,128)(2,1)S(1)} %pad_maximum_fusion.5), channel_id=1, source_target_pairs={{0,4},{2,6},{4,0},{6,2},{8,12},{10,14},{12,8},{14,10},{16,20},{18,... | collective-permute-start | bytes 1720328 | tf_op jit(solution)/shard_map/ppermute | solution.py:25
  52.5 0.8 copy-start.7
  64.9 4.1 %copy-start.2 = (bf16[8,40,1792]{2,1,0:T(8,128)(2,1)}, bf16[8,40,1792]{2,1,0:T(8,128)(2,1)S(1)}, u32[]{:S(2)}) copy-start(bf16[8,40,1792]{2,1,0:T(8,128)(2,1)S(1)} %pad_maximum_fusion.2.near_ref) | copy-start | bytes 3440644
  64.9 4.0 %collective-permute-start.9 = (bf16[8,40,1792]{2,1,0:T(8,128)(2,1)S(1)}, bf16[8,40,1792]{2,1,0:T(8,128)(2,1)S(1)}, u32[]{:S(2)}, u32[]{:S(2)}) collective-permute-start(bf16[8,40,1792]{2,1,0:T(8,128)(2,1)S(1)} %pad_maximum_fusion.2.near_ref), channel_id=1, source_target_pairs={{0,2},{2,0},{4,6},{6,4},{8,10},{10,8},{12,14},{14,12},{16,18},{18,... | collective-permute-start | bytes 3440648 | tf_op jit(solution)/shard_map/ppermute | solution.py:25
  65.0 24.3 %collective-permute-start.10 = (bf16[4,192,640]{2,1,0:T(8,128)(2,1)S(1)}, bf16[4,192,640]{2,1,0:T(8,128)(2,1)}, u32[]{:S(2)}, u32[]{:S(2)}) collective-permute-start(bf16[4,192,640]{2,1,0:T(8,128)(2,1)S(1)} %pad_maximum_fusion.3), channel_id=1, source_target_pairs={{0,4},{2,6},{4,0},{6,2},{8,12},{10,14},{12,8},{14,10},{16,20},{18,... | collective-permute-start | bytes 2949128 | tf_op jit(solution)/shard_map/ppermute | solution.py:25
  66.6 31.8 %collective-permute-start.13 = (bf16[8,40,2048]{2,1,0:T(8,128)(2,1)}, bf16[8,40,2048]{2,1,0:T(8,128)(2,1)}, u32[]{:S(2)}, u32[]{:S(2)}) collective-permute-start(bf16[8,40,2048]{2,1,0:T(8,128)(2,1)} %pad_maximum_fusion.1.mine_near), channel_id=1, source_target_pairs={{0,1},{1,0},{2,3},{3,2},{4,5},{5,4},{6,7},{7,6},{8,9},{9,8},{10,11... | collective-permute-start | bytes 3932168 | tf_op jit(solution)/shard_map/ppermute | solution.py:25
  69.0 1.0 copy-start.8
  90.9 17.8 %copy-start.6 = (bf16[8,192,640]{2,1,0:T(8,128)(2,1)}, bf16[8,192,640]{2,1,0:T(8,128)(2,1)S(1)}, u32[]{:S(2)}) copy-start(bf16[8,192,640]{2,1,0:T(8,128)(2,1)S(1)} %pad_maximum_fusion) | copy-start | bytes 5898244
  90.9 17.8 %collective-permute-start.11 = (bf16[8,192,640]{2,1,0:T(8,128)(2,1)S(1)}, bf16[8,192,640]{2,1,0:T(8,128)(2,1)}, u32[]{:S(2)}, u32[]{:S(2)}) collective-permute-start(bf16[8,192,640]{2,1,0:T(8,128)(2,1)S(1)} %pad_maximum_fusion), channel_id=1, source_target_pairs={{0,2},{2,0},{4,6},{6,4},{8,10},{10,8},{12,14},{14,12},{16,18},{18,... | collective-permute-start | bytes 5898248 | tf_op jit(solution)/shard_map/ppermute | solution.py:25
  90.9 17.7 %collective-permute-start.12 = (bf16[8,40,2048]{2,1,0:T(8,128)(2,1)}, bf16[8,40,2048]{2,1,0:T(8,128)(2,1)S(1)}, u32[]{:S(2)}, u32[]{:S(2)}) collective-permute-start(bf16[8,40,2048]{2,1,0:T(8,128)(2,1)} %pad_maximum_fusion.1.mine_near), channel_id=1, source_target_pairs={{0,2},{2,0},{4,6},{6,4},{8,10},{10,8},{12,14},{14,12},{16,18},{18,... | collective-permute-start | bytes 3932168 | tf_op jit(solution)/shard_map/ppermute | solution.py:25
  98.4 10.3 %collective-permute-start.14 = (bf16[8,40,2048]{2,1,0:T(8,128)(2,1)}, bf16[8,40,2048]{2,1,0:T(8,128)(2,1)}, u32[]{:S(2)}, u32[]{:S(2)}) collective-permute-start(bf16[8,40,2048]{2,1,0:T(8,128)(2,1)} %collective-permute-done.13.other_near), channel_id=1, source_target_pairs={{0,2},{2,0},{4,6},{6,4},{8,10},{10,8},{12,14},{14,12},{16,18},{18,... | collective-permute-start | bytes 3932168 | tf_op jit(solution)/shard_map/ppermute | solution.py:25
  108.7 1.1 copy-start.13
  180.0 11.1 %collective-permute-start.15 = (bf16[2,8,40,2048]{3,2,1,0:T(8,128)(2,1)}, bf16[2,8,40,2048]{3,2,1,0:T(8,128)(2,1)S(1)}, u32[]{:S(2)}, u32[]{:S(2)}) collective-permute-start(bf16[2,8,40,2048]{3,2,1,0:T(8,128)(2,1)} %get-tuple-element.102), channel_id=1, source_target_pairs={{0,2},{2,0},{4,6},{6,4},{8,10},{10,8},{12,14},{14,12},{16,18},{18,... | collective-permute-start | bytes 7864328 | tf_op jit(solution)/shard_map/ppermute | solution.py:25
  180.7 10.5 %collective-permute-start.16 = (bf16[8,2,96,640]{3,2,1,0:T(8,128)(2,1)}, bf16[8,2,96,640]{3,2,1,0:T(8,128)(2,1)}, u32[]{:S(2)}, u32[]{:S(2)}) collective-permute-start(bf16[8,2,96,640]{3,2,1,0:T(8,128)(2,1)} %get-tuple-element.103), channel_id=1, source_target_pairs={{0,2},{2,0},{4,6},{6,4},{8,10},{10,8},{12,14},{14,12},{16,18},{18,... | collective-permute-start | bytes 5898248 | tf_op jit(solution)/shard_map/ppermute | solution.py:25
  191.1 1.5 copy-start.4
  196.4 1.5 copy-start.5
  196.5 37.6 %collective-permute-start.18 = (bf16[2,1,2,2,40,2048]{5,4,3,2,1,0:T(8,128)(2,1)S(1)}, bf16[2,1,2,2,40,2048]{5,4,3,2,1,0:T(8,128)(2,1)}, u32[]{:S(2)}, u32[]{:S(2)}) collective-permute-start(bf16[2,1,2,2,40,2048]{5,4,3,2,1,0:T(8,128)(2,1)S(1)} %split.94), channel_id=1, source_target_pairs={{0,4},{2,6},{4,0},{6,2},{8,12},{10,14},{12,8},{14,10},{16,20},{18,... | collective-permute-start | bytes 3932168 | tf_op jit(solution)/shard_map/ppermute | solution.py:25
  200.0 1.3 copy-start
  202.3 30.0 %collective-permute-start.17 = (bf16[2,1,2,2,96,640]{5,4,3,2,1,0:T(8,128)(2,1)}, bf16[2,1,2,2,96,640]{5,4,3,2,1,0:T(8,128)(2,1)}, u32[]{:S(2)}, u32[]{:S(2)}) collective-permute-start(bf16[2,1,2,2,96,640]{5,4,3,2,1,0:T(8,128)(2,1)} %split.92), channel_id=1, source_target_pairs={{0,8},{2,10},{4,12},{6,14},{8,0},{10,2},{12,4},{14,6},{16,24},{18,... | collective-permute-start | bytes 2949128 | tf_op jit(solution)/shard_map/ppermute | solution.py:25
  234.1 2.0 copy-start.14
  234.1 4.9 %copy-start.9 = (bf16[8,40,1792]{2,1,0:T(8,128)(2,1)S(1)}, bf16[8,40,1792]{2,1,0:T(8,128)(2,1)}, u32[]{:S(2)}) copy-start(bf16[8,40,1792]{2,1,0:T(8,128)(2,1)} %get-tuple-element.126) | copy-start | bytes 3440644
  236.1 2.9 collective-permute-start.20
  239.3 2.9 copy-start.12
  239.4 15.9 %collective-permute-start.21 = (bf16[1,2,2,40,1792]{4,3,2,1,0:T(8,128)(2,1)S(1)}, bf16[1,2,2,40,1792]{4,3,2,1,0:T(8,128)(2,1)S(1)}, u32[]{:S(2)}, u32[]{:S(2)}) collective-permute-start(bf16[1,2,2,40,1792]{4,3,2,1,0:T(8,128)(2,1)S(1)} %bitcast.51), channel_id=1, source_target_pairs={{0,4},{2,6},{4,0},{6,2},{8,12},{10,14},{12,8},{14,10},{16,20},{18,... | collective-permute-start | bytes 1720328 | tf_op jit(solution)/shard_map/ppermute | solution.py:25
  240.2 24.9 %collective-permute-start.24 = (bf16[1,1,2,2,96,640]{5,4,3,2,1,0:T(8,128)(2,1)S(1)}, bf16[1,1,2,2,96,640]{5,4,3,2,1,0:T(8,128)(2,1)S(1)}, u32[]{:S(2)}, u32[]{:S(2)}) collective-permute-start(bf16[1,1,2,2,96,640]{5,4,3,2,1,0:T(8,128)(2,1)S(1)} %split.102), channel_id=1, source_target_pairs={{0,4},{2,6},{4,0},{6,2},{8,12},{10,14},{12,8},{14,10},{16,20},{18,... | collective-permute-start | bytes 1474568 | tf_op jit(solution)/shard_map/ppermute | solution.py:25
  241.6 23.6 %collective-permute-start.23 = (bf16[2,1,1,2,40,2048]{5,4,3,2,1,0:T(8,128)(2,1)S(1)}, bf16[2,1,1,2,40,2048]{5,4,3,2,1,0:T(8,128)(2,1)S(1)}, u32[]{:S(2)}, u32[]{:S(2)}) collective-permute-start(bf16[2,1,1,2,40,2048]{5,4,3,2,1,0:T(8,128)(2,1)S(1)} %split.100), channel_id=1, source_target_pairs={{0,8},{2,10},{4,12},{6,14},{8,0},{10,2},{12,4},{14,6},{16,24},{18,... | collective-permute-start | bytes 1966088 | tf_op jit(solution)/shard_map/ppermute | solution.py:25
  242.1 55.7 %collective-permute-start.19 = (bf16[1024,640]{1,0:T(8,128)(2,1)S(1)}, bf16[1024,640]{1,0:T(8,128)(2,1)S(1)}, u32[]{:S(2)}, u32[]{:S(2)}) collective-permute-start(bf16[1024,640]{1,0:T(8,128)(2,1)S(1)} %copy-done.12), channel_id=1, source_target_pairs={{1,0},{3,2},{5,4},{7,6},{9,8},{11,10},{13,12},{15,14},{17,16},{19,... | collective-permute-start | bytes 3932168 | tf_op jit(solution)/shard_map/ppermute | solution.py:71
  265.2 15.8 %collective-permute-start.26 = (bf16[1,1,2,1,96,640]{5,4,3,2,1,0:T(8,128)(2,1)S(1)}, bf16[1,1,2,1,96,640]{5,4,3,2,1,0:T(8,128)(2,1)S(1)}, u32[]{:S(2)}, u32[]{:S(2)}) collective-permute-start(bf16[1,1,2,1,96,640]{5,4,3,2,1,0:T(8,128)(2,1)S(1)} %split.106), channel_id=1, source_target_pairs={{0,1},{1,0},{2,3},{3,2},{4,5},{5,4},{6,7},{7,6},{8,9},{9,8},{10,11... | collective-permute-start | bytes 737288 | tf_op jit(solution)/shard_map/ppermute | solution.py:25
  267.0 7.8 %collective-permute-start.22 = (bf16[1,1,2,40,1792]{4,3,2,1,0:T(8,128)(2,1)S(1)}, bf16[1,1,2,40,1792]{4,3,2,1,0:T(8,128)(2,1)S(1)}, u32[]{:S(2)}, u32[]{:S(2)}) collective-permute-start(bf16[1,1,2,40,1792]{4,3,2,1,0:T(8,128)(2,1)S(1)} %split.98), channel_id=1, source_target_pairs={{0,8},{2,10},{4,12},{6,14},{8,0},{10,2},{12,4},{14,6},{16,24},{18,... | collective-permute-start | bytes 860168 | tf_op jit(solution)/shard_map/ppermute | solution.py:25
  267.7 30.2 %copy-start.3 = (f32[1024,640]{1,0:T(8,128)S(1)}, f32[1024,640]{1,0:T(8,128)}, u32[]{:S(2)}) copy-start(f32[1024,640]{1,0:T(8,128)} %get-tuple-element.120) | copy-start | bytes 7864324
  267.7 18.6 %collective-permute-start.30 = (bf16[1,1,1,2,40,2048]{5,4,3,2,1,0:T(8,128)(2,1)S(1)}, bf16[1,1,1,2,40,2048]{5,4,3,2,1,0:T(8,128)(2,1)S(1)}, u32[]{:S(2)}, u32[]{:S(2)}) collective-permute-start(bf16[1,1,1,2,40,2048]{5,4,3,2,1,0:T(8,128)(2,1)S(1)} %split.110), channel_id=1, source_target_pairs={{0,1},{1,0},{2,3},{3,2},{4,5},{5,4},{6,7},{7,6},{8,9},{9,8},{10,11... | collective-permute-start | bytes 983048 | tf_op jit(solution)/shard_map/ppermute | solution.py:25
  281.1 13.6 %collective-permute-start.27 = (bf16[1,1,1,1,96,640]{5,4,3,2,1,0:T(8,128)(2,1)S(1)}, bf16[1,1,1,1,96,640]{5,4,3,2,1,0:T(8,128)(2,1)S(1)}, u32[]{:S(2)}, u32[]{:S(2)}) collective-permute-start(bf16[1,1,1,1,96,640]{5,4,3,2,1,0:T(8,128)(2,1)S(1)} %split.108), channel_id=1, source_target_pairs={{0,16},{2,18},{4,20},{6,22},{8,24},{10,26},{12,28},{14,30},{16,0},... | collective-permute-start | bytes 368648 | tf_op jit(solution)/shard_map/ppermute | solution.py:25
  281.5 16.3 %collective-permute-start.25 = (bf16[1,1,1,40,1792]{4,3,2,1,0:T(8,128)(2,1)S(1)}, bf16[1,1,1,40,1792]{4,3,2,1,0:T(8,128)(2,1)S(1)}, u32[]{:S(2)}, u32[]{:S(2)}) collective-permute-start(bf16[1,1,1,40,1792]{4,3,2,1,0:T(8,128)(2,1)S(1)} %split.104), channel_id=1, source_target_pairs={{0,16},{2,18},{4,20},{6,22},{8,24},{10,26},{12,28},{14,30},{16,0},... | collective-permute-start | bytes 430088 | tf_op jit(solution)/shard_map/ppermute | solution.py:25
  286.5 13.4 %collective-permute-start.31 = (bf16[1,1,1,1,40,2048]{5,4,3,2,1,0:T(8,128)(2,1)S(1)}, bf16[1,1,1,1,40,2048]{5,4,3,2,1,0:T(8,128)(2,1)S(1)}, u32[]{:S(2)}, u32[]{:S(2)}) collective-permute-start(bf16[1,1,1,1,40,2048]{5,4,3,2,1,0:T(8,128)(2,1)S(1)} %split.112), channel_id=1, source_target_pairs={{0,16},{2,18},{4,20},{6,22},{8,24},{10,26},{12,28},{14,30},{16,0},... | collective-permute-start | bytes 491528 | tf_op jit(solution)/shard_map/ppermute | solution.py:25
  294.7 6.6 %collective-permute-start.29 = (bf16[96,640]{1,0:T(8,128)(2,1)S(1)}, bf16[96,640]{1,0:T(8,128)(2,1)S(1)}, u32[]{:S(2)}, u32[]{:S(2)}) collective-permute-start(bf16[96,640]{1,0:T(8,128)(2,1)S(1)} %bitcast.52), channel_id=1, source_target_pairs={{0,1},{1,0},{2,3},{3,2},{4,5},{5,4},{6,7},{7,6},{8,9},{9,8},{10,11... | collective-permute-start | bytes 368648 | tf_op jit(solution)/shard_map/ppermute | solution.py:25
  297.8 6.7 %collective-permute-start.28 = (bf16[40,1792]{1,0:T(8,128)(2,1)S(1)}, bf16[40,1792]{1,0:T(8,128)(2,1)S(1)}, u32[]{:S(2)}, u32[]{:S(2)}) collective-permute-start(bf16[40,1792]{1,0:T(8,128)(2,1)S(1)} %fusion.4), channel_id=1, source_target_pairs={{0,1},{1,0},{2,3},{3,2},{4,5},{5,4},{6,7},{7,6},{8,9},{9,8},{10,11... | collective-permute-start | bytes 430088 | tf_op jit(solution)/shard_map/ppermute | solution.py:25
  299.9 7.4 %collective-permute-start.32 = (bf16[40,2048]{1,0:T(8,128)(2,1)S(1)}, bf16[40,2048]{1,0:T(8,128)(2,1)S(1)}, u32[]{:S(2)}, u32[]{:S(2)}) collective-permute-start(bf16[40,2048]{1,0:T(8,128)(2,1)S(1)} %fusion.2), channel_id=1, source_target_pairs={{0,1},{1,0},{2,3},{3,2},{4,5},{5,4},{6,7},{7,6},{8,9},{9,8},{10,11... | collective-permute-start | bytes 491528 | tf_op jit(solution)/shard_map/ppermute | solution.py:25

commit v3 on v2

--- a/solution.py
+++ b/solution.py
@@ -45,7 +45,7 @@
 
 
 def cost(flops, spent):
-    return pl.CostEstimate(flops=int(flops / spent / 16), bytes_accessed=0, transcendentals=0)
+    return pl.CostEstimate(flops=int(flops / spent / 4096), bytes_accessed=0, transcendentals=0)
 
 
 def add(left, right):
@@ -730,10 +730,6 @@
         cost_estimate=cost(2 * total * model_width * (qkv_columns + 2 * head_dim), 0.25),
         name="projection",
     )(x, x_before, first_near, first_far, pick, info, *tables, *tables_before)
-    other_near = after(other_near, query_low)
-    other_far = swap(other_near, "fsdp", 1)
-    tall_near = jnp.concatenate([tall_near, after(tall_late, query_low)], axis=0)
-    tall_far = swap(tall_near, "fsdp", 1)
     head = pl.BlockSpec((span_len, head_dim), lambda s, h: (s, h))
     shared = pl.BlockSpec((span_len, head_dim), lambda s, h: (s, 0))
     attended_low = pl.pallas_call(
@@ -746,6 +742,10 @@
         cost_estimate=cost(3 * total * span_len * query_columns, 0.14),
         name="attention",
     )(info, query_low, key_low, value_low, key_prev, value_prev)
+    tall_near = jnp.concatenate([tall_near, after(tall_late, attended_low)], axis=0)
+    tall_far = swap(tall_near, "fsdp", 1)
+    other_near = after(other_near, tall_near)
+    other_far = swap(other_near, "fsdp", 1)
     down_rows, out_rows = down_weight.shape[0], output_weight.shape[0]
     half_rows = (down_rows + out_rows) // 2
     chips = fsdp // 2
@@ -892,28 +892,29 @@
     first_kept, first_come = folded(first, "fsdp", near_masks[0], 0)
     first = add(first_kept, first_come)
     first_kept, first_come = folded(first, "fsdp", near_masks[1], 1)
+    wide = add(wide_kept, after(wide_come, first))
+    wide_kept, wide_come = folded(wide, "ctx", 1, 0)
+    first = add(first_kept, after(first_come, wide))
+    first_kept, first_come = folded(first, "fsdp", (near_masks + [far_mask])[2], 2)
     tall = add(tall_kept, after(tall_come, first))
     tall_kept, tall_come = folded(tall, "ctx", 1, len(bits))
-    wide = add(wide_kept, after(wide_come, tall))
-    wide_kept, wide_come = folded(wide, "ctx", 1, 0)
+    first = add(first_kept, after(first_come, tall))
+    wide = add(wide_kept, after(wide_come, first))
+    tall = add(tall_kept, after(tall_come, wide))
     for index in range(2, len(bits)):
         mask = (near_masks + [far_mask])[index]
-        first = add(first_kept, after(first_come, wide))
-        first_kept, first_come = folded(first, "fsdp", mask, index)
-        if index == 2:
-            tall = add(tall_kept, after(tall_come, first))
+        if index > 2:
+            first_kept, first_come = folded(first, "fsdp", mask, index)
+            first = add(first_kept, first_come)
+        wide_kept, wide_come = folded(wide, "fsdp", mask, index + 1)
         tall_kept, tall_come = folded(tall, "fsdp", mask, index)
-        if index == 2:
-            wide = add(wide_kept, after(wide_come, tall))
-        wide_kept, wide_come = folded(wide, "fsdp", mask, index + 1)
-        tall = add(tall_kept, after(tall_come, first))
-        wide = add(wide_kept, after(wide_come, tall))
-    first = add(first_kept, after(first_come, tall))
+        wide = add(wide_kept, wide_come)
+        tall = add(tall_kept, after(tall_come, wide))
     tall = other_spans(tall.reshape(tall.shape[-2:]), "ctx")
     wide = other_spans(wide.reshape(wide.shape[-2:]), "ctx")
     first = other_spans(first.reshape(first.shape[-2:]), "ctx")
     first_come = swap(first, "ctx", 1)
-    before_come = after(before_come, first)
+    before_come = after(before_come, tall)
     token_grad = (token_part + before_come.astype(jnp.float32)).astype(jnp.bfloat16)
 
     def both(mine):

time: 312 us -> 300 us (0.962)
  waiting for transfers between devices: 106 us -> 94.7 us
    ppermute x31, waiting for transfers between devices: 105 us -> 93.5 us  [swap(): lax.ppermute(value, axis, [(source, source ^ mask) for source in range(co...]
    unnamed x30 -> x36, local copies, waits for them, and re-layouts: 6.47 us -> 5.9 us
    convert_element_type x12 -> x13, other arithmetic: 10.5 us -> 10.3 us  [add(): (left.astype(jnp.float32) + right.astype(jnp.float32)).astype(jnp.bfloat16)]
  transfers between devices with their start and end apart: 33 -> 33, of which waited for: 19 -> 21; matrix products, arithmetic and copies ran while one was open for 7% -> 7% of each run, Pallas kernels for 19% -> 20%
where the time goes in v3:
time: 300 us; the launch traced here: 297 us
  Pallas kernels  129 us (43%)
  waiting for transfers between devices  94.7 us (32%)
  starting transfers between devices  35.4 us (12%)
  other arithmetic  23 us (8%)
  local copies, waits for them, and re-layouts  13.4 us (4%)
    ppermute x31, waiting for transfers between devices, swap(): lax.ppermute(value, axis, [(source, source ^ mask) for source in range(co...  93.5 us
    pallas_call x1, Pallas kernels, per_device(): pl.pallas_call(functools.partial(middle_kernel, 512, down_rows), grid=(st...  70.5 us
    ppermute x31, starting transfers between devices, swap(): lax.ppermute(value, axis, [(source, source ^ mask) for source in range(co...  30.6 us
    pallas_call x2, Pallas kernels, attention_back(): pl.pallas_call(functools.partial(attention_back_kernel, score_scale), gri...  20.7 us
    pallas_call x1, Pallas kernels, per_device(): pl.pallas_call(functools.partial(head_back_kernel, head_dim), grid=(steps...  17.9 us
    pallas_call x1, Pallas kernels, per_device(): pl.pallas_call(functools.partial(attention_kernel, score_scale), grid=(se...  10.3 us
    convert_element_type x13, other arithmetic, add(): (left.astype(jnp.float32) + right.astype(jnp.float32)).astype(jnp.bfloat16)  10.3 us
    pallas_call x1, Pallas kernels, per_device(): pl.pallas_call(functools.partial(projection_kernel, head_dim, qkv_columns...  9.27 us
  transfers between devices with their start and end apart: 33, of which 21 were waited for; matrix products, arithmetic and copies ran while one was open for 7% of the time, Pallas kernels for 20%

profile of v3, /device:TPU:0, one launch (start us, length us, event | category | flops | bytes accessed | tf_op | source)
XLA Modules:
  0.0 297.0 jit_solution(13298798880560153036)
XLA Ops:
  1.7 4.1 %collective-permute-start.2 = (bf16[1,40,2048]{2,1,0:T(8,128)(2,1)S(1)}, bf16[1,40,2048]{2,1,0:T(8,128)(2,1)S(1)}, u32[]{:S(2)}, u32[]{:S(2)}) collective-permute-start(bf16[1,40,2048]{2,1,0:T(8,128)(2,1)S(1)} %select_bitcast_fusion), channel_id=1, source_target_pairs={{0,16},{2,18},{4,20},{6,22},{8,24},{10,26},{12,28},{14,30},{16,0},... | collective-permute-start | bytes 491528 | tf_op jit(solution)/shard_map/ppermute | solution.py:25
  5.8 3.5 %collective-permute-start = (bf16[2,512,640]{2,1,0:T(8,128)(2,1)}, bf16[2,512,640]{2,1,0:T(8,128)(2,1)S(1)}, u32[]{:S(2)}, u32[]{:S(2)}) collective-permute-start(bf16[2,512,640]{2,1,0:T(8,128)(2,1)} %param.15), channel_id=1, source_target_pairs={{0,1},{2,3},{4,5},{6,7},{8,9},{10,11},{12,13},{14,15},{16,17},{18,... | collective-permute-start | bytes 3932168 | tf_op jit(solution)/shard_map/ppermute | solution.py:71
  10.8 3.0 %multiply_sine_fusion = (f32[512,128]{1,0:T(8,128)}, f32[512,128]{1,0:T(8,128)}, f32[512,128]{1,0:T(8,128)}, f32[512,128]{1,0:T(8,128)}) fusion(f32[512]{0:T(512)S(1)} %add_convert_fusion.14, f32[128]{0:T(128)S(1)} %negate_power_fusion, f32[512]{0:T(512)S(1)} %add_convert_fusion.15), kind=kLoop, calls=%fused_computation.21 | loop fusion | flops 131072 | bytes 1053184 | tf_op jit(solution)/shard_map/sin | solution.py:597
  16.8 2.7 collective-permute-start.6
  19.4 1.6 collective-permute-start.4
  21.0 10.7 %collective-permute-done.1 = bf16[1,40,1792]{2,1,0:T(8,128)(2,1)S(1)} collective-permute-done((bf16[1,40,1792]{2,1,0:T(8,128)(2,1)S(1)}, bf16[1,40,1792]{2,1,0:T(8,128)(2,1)S(1)}, u32[]{:S(2)}, u32[]{:S(2)}) %collective-permute-start.1) | collective-permute-done | bytes 143392 | tf_op jit(solution)/shard_map/ppermute | solution.py:25
  31.9 4.0 %collective-permute-done.6 = bf16[1,192,640]{2,1,0:T(8,128)(2,1)S(1)} collective-permute-done((bf16[1,192,640]{2,1,0:T(8,128)(2,1)S(1)}, bf16[1,192,640]{2,1,0:T(8,128)(2,1)S(1)}, u32[]{:S(2)}, u32[]{:S(2)}) %collective-permute-start.6) | collective-permute-done | bytes 245792 | tf_op jit(solution)/shard_map/ppermute | solution.py:25
  37.2 1.5 collective-permute-start.7
  38.7 1.6 collective-permute-start.8
  40.3 1.7 collective-permute-done.3
  42.1 1.6 collective-permute-start.5
  43.7 8.8 %collective-permute-done.8 = bf16[2,192,640]{2,1,0:T(8,128)(2,1)S(1)} collective-permute-done((bf16[2,192,640]{2,1,0:T(8,128)(2,1)S(1)}, bf16[2,192,640]{2,1,0:T(8,128)(2,1)S(1)}, u32[]{:S(2)}, u32[]{:S(2)}) %collective-permute-start.8) | collective-permute-done | bytes 491552 | tf_op jit(solution)/shard_map/ppermute | solution.py:25
  52.6 2.3 collective-permute-done.7
  56.1 8.7 %collective-permute-done.5 = bf16[4,40,1792]{2,1,0:T(8,128)(2,1)S(1)} collective-permute-done((bf16[4,40,1792]{2,1,0:T(8,128)(2,1)S(1)}, bf16[4,40,1792]{2,1,0:T(8,128)(2,1)S(1)}, u32[]{:S(2)}, u32[]{:S(2)}) %collective-permute-start.5) | collective-permute-done | bytes 573472 | tf_op jit(solution)/shard_map/ppermute | solution.py:25
  65.0 1.6 collective-permute-start.10
  66.6 2.4 collective-permute-start.13
  70.0 9.3 %projection.1 = (bf16[1024,1024]{1,0:T(8,128)(2,1)}, bf16[1024,256]{1,0:T(8,128)(2,1)}, bf16[1024,256]{1,0:T(8,128)(2,1)}, bf16[1024,256]{1,0:T(8,128)(2,1)}, bf...) custom-call(bf16[1024,640]{1,0:T(8,128)(2,1)} %bitcast.35, ...), custom_call_target="tpu_custom_call" | custom-call | flops 2621440 | tf_op jit(solution)/shard_map/projection/pallas_call | solution.py:720
  79.3 10.3 %attention.1.att_ref = bf16[1024,1024]{1,0:T(8,128)(2,1)} custom-call(s32[19]{0:T(128)} %pad_add_fusion.info_ref.flag_ref, bf16[1024,1024]{1,0:T(8,128)(2,1)} %get-tuple-element.88.q_ref, bf16[1024,256]{1,0:T(8,128)(2,1)} %get-tuple-element.89.k_ref, bf16[1024,256]{1,0:T(8,128)(2,1)} %get-tuple-element.90.v_ref, bf16[1024,256]{1,0:T(8,128)(2,1)} %get-tuple-element.91.kb_ref, ...), custom_call_target="tpu_custom_call" | custom-call | flops 2808685 | tf_op jit(solution)/shard_map/attention/pallas_call | solution.py:735
  89.6 1.4 pad_maximum_fusion
  91.7 6.7 %collective-permute-done.13.other_near = bf16[8,40,2048]{2,1,0:T(8,128)(2,1)} collective-permute-done((bf16[8,40,2048]{2,1,0:T(8,128)(2,1)}, bf16[8,40,2048]{2,1,0:T(8,128)(2,1)}, u32[]{:S(2)}, u32[]{:S(2)}) %collective-permute-start.13) | collective-permute-done | bytes 1310752 | tf_op jit(solution)/shard_map/ppermute | solution.py:25
  98.4 3.2 %collective-permute-done.14.other_far = bf16[8,40,2048]{2,1,0:T(8,128)(2,1)S(1)} collective-permute-done((bf16[8,40,2048]{2,1,0:T(8,128)(2,1)}, bf16[8,40,2048]{2,1,0:T(8,128)(2,1)S(1)}, u32[]{:S(2)}, u32[]{:S(2)}) %collective-permute-start.14) | collective-permute-done | bytes 1310752 | tf_op jit(solution)/shard_map/ppermute | solution.py:25
  101.6 1.3 copy-done.6
  103.3 70.5 %middle.1 = (bf16[1024,640]{1,0:T(8,128)(2,1)}, f32[1024,640]{1,0:T(8,128)}, bf16[1024,1024]{1,0:T(8,128)(2,1)}, f32[8,640]{1,0:T(8,128)}, bf16[2,8,40,2048]{3,2...) custom-call(bf16[1024,640]{1,0:T(8,128)(2,1)} %bitcast.36, ...), custom_call_target="tpu_custom_call" | custom-call | flops 17203200 | tf_op jit(solution)/shard_map/middle/pallas_call | solution.py:761
  174.5 10.4 %attention_back.2 = (f32[1024,1024]{1,0:T(8,128)}, f32[1024,256]{1,0:T(8,128)}, f32[1024,256]{1,0:T(8,128)}, f32[1024,256]{1,0:T(8,128)}, f32[1024,256]{1,0:T(8,128)}) custom-call(s32[19]{0:T(128)} %pad_add_fusion.info_ref.flag_ref, bf16[1024,1024]{1,0:T(8,128)(2,1)} %get-tuple-element.88.q_ref, bf16[1024,256]{1,0:T(8,128)(2,1)} %get-tuple-element.89.k_ref, ...), custom_call_target="tpu_custom_call" | custom-call | flops 2457600 | tf_op jit(solution)/shard_map/attention_back/pallas_call | solution.py:812
  184.8 1.6 copy-done.5
  186.4 3.8 %add_convert_fusion = bf16[2,8,40,2048]{3,2,1,0:T(8,128)(2,1)S(1)} fusion(bf16[2,8,40,2048]{3,2,1,0:T(8,128)(2,1)} %copy-done.5, bf16[2,8,40,2048]{3,2,1,0:T(8,128)(2,1)} %get-tuple-element.100), kind=kLoop, calls=%fused_computation | loop fusion | flops 5242880 | bytes 7864320 | tf_op jit(solution)/shard_map/convert_element_type | solution.py:52
  192.2 2.1 add_convert_fusion.1
  194.3 1.3 copy-done.1
  196.7 1.6 collective-permute-start.17
  198.3 10.4 %attention_back.3 = (f32[1024,1024]{1,0:T(8,128)}, f32[1024,256]{1,0:T(8,128)}, f32[1024,256]{1,0:T(8,128)}, f32[1024,256]{1,0:T(8,128)}, f32[1024,256]{1,0:T(8,128)}) custom-call(s32[19]{0:T(128)} %pad_add_fusion.info_ref.flag_ref, ...), custom_call_target="tpu_custom_call", output_to_operand_aliasing={{0}: (7, {}), {1}: (8, {}), {2}: (9, {}), {3}: (10, {}), {4... | custom-call | flops 2457600 | tf_op jit(solution)/shard_map/attention_back/pallas_call | solution.py:812
  208.7 17.9 %head_back.1 = (f32[1024,640]{1,0:T(8,128)}, bf16[1024,640]{1,0:T(8,128)(2,1)}, bf16[8,40,1792]{2,1,0:T(8,128)(2,1)}, bf16[8,40,1792]{2,1,0:T(8,128)(2,1)}) custom-call(bf16[1024,640]{1,0:T(8,128)(2,1)} %bitcast.37, bf16[1024,640]{1,0:T(8,128)(2,1)} %bitcast.44, bf16[640,1536]{1,0:T(8,128)(2,1)} %get-tuple-element.97.w_ref, ...), custom_call_target="tpu_custom_call" | custom-call | flops 5173894 | tf_op jit(solution)/shard_map/head_back/pallas_call | solution.py:837
  226.6 1.4 add_convert_fusion.5
  228.1 1.9 add_convert_fusion.3
  230.1 2.8 collective-permute-done.21
  233.3 1.3 collective-permute-start.22
  236.1 1.3 collective-permute-start.19
  237.3 11.8 %collective-permute-done.22 = bf16[1,2,2,40,1792]{4,3,2,1,0:T(8,128)(2,1)S(1)} collective-permute-done((bf16[1,2,2,40,1792]{4,3,2,1,0:T(8,128)(2,1)S(1)}, bf16[1,2,2,40,1792]{4,3,2,1,0:T(8,128)(2,1)S(1)}, u32[]{:S(2)}, u32[]{:S(2)}) %collective-permute-start.22) | collective-permute-done | bytes 573472 | tf_op jit(solution)/shard_map/ppermute | solution.py:25
  249.3 1.8 collective-permute-done.24
  251.9 1.8 collective-permute-start.26
  253.7 5.2 %collective-permute-done.23 = bf16[1,1,2,40,1792]{4,3,2,1,0:T(8,128)(2,1)S(1)} collective-permute-done((bf16[1,1,2,40,1792]{4,3,2,1,0:T(8,128)(2,1)S(1)}, bf16[1,1,2,40,1792]{4,3,2,1,0:T(8,128)(2,1)S(1)}, u32[]{:S(2)}, u32[]{:S(2)}) %collective-permute-start.23) | collective-permute-done | bytes 286752 | tf_op jit(solution)/shard_map/ppermute | solution.py:25
  259.6 1.8 collective-permute-start.25
  261.4 6.4 %collective-permute-done.27 = bf16[1,1,1,40,1792]{4,3,2,1,0:T(8,128)(2,1)S(1)} collective-permute-done((bf16[1,1,1,40,1792]{4,3,2,1,0:T(8,128)(2,1)S(1)}, bf16[1,1,1,40,1792]{4,3,2,1,0:T(8,128)(2,1)S(1)}, u32[]{:S(2)}, u32[]{:S(2)}) %collective-permute-start.27) | collective-permute-done | bytes 143392 | tf_op jit(solution)/shard_map/ppermute | solution.py:25
  267.8 1.8 collective-permute-start.30
  269.6 7.1 %collective-permute-done.26 = bf16[1,1,1,2,40,2048]{5,4,3,2,1,0:T(8,128)(2,1)S(1)} collective-permute-done((bf16[1,1,1,2,40,2048]{5,4,3,2,1,0:T(8,128)(2,1)S(1)}, bf16[1,1,1,2,40,2048]{5,4,3,2,1,0:T(8,128)(2,1)S(1)}, u32[]{:S(2)}, u32[]{:S(2)}) %collective-permute-start.26) | collective-permute-done | bytes 327712 | tf_op jit(solution)/shard_map/ppermute | solution.py:25
  277.2 4.6 %collective-permute-done.25 = bf16[1,1,2,1,96,640]{5,4,3,2,1,0:T(8,128)(2,1)S(1)} collective-permute-done((bf16[1,1,2,1,96,640]{5,4,3,2,1,0:T(8,128)(2,1)S(1)}, bf16[1,1,2,1,96,640]{5,4,3,2,1,0:T(8,128)(2,1)S(1)}, u32[]{:S(2)}, u32[]{:S(2)}) %collective-permute-start.25) | collective-permute-done | bytes 245792 | tf_op jit(solution)/shard_map/ppermute | solution.py:25
  287.1 3.0 %collective-permute-done.28 = bf16[1,1,1,1,96,640]{5,4,3,2,1,0:T(8,128)(2,1)S(1)} collective-permute-done((bf16[1,1,1,1,96,640]{5,4,3,2,1,0:T(8,128)(2,1)S(1)}, bf16[1,1,1,1,96,640]{5,4,3,2,1,0:T(8,128)(2,1)S(1)}, u32[]{:S(2)}, u32[]{:S(2)}) %collective-permute-start.28) | collective-permute-done | bytes 122912 | tf_op jit(solution)/shard_map/ppermute | solution.py:25
  290.2 1.4 add_convert_fusion.2
  293.6 1.4 collective-permute-done.31
  (119 shorter events, 26.9 us)
Async XLA Ops:
  0.6 16.0 %copy-start.14 = (bf16[128,640]{1,0:T(8,128)(2,1)S(1)}, bf16[128,640]{1,0:T(8,128)(2,1)}, u32[]{:S(2)}) copy-start(bf16[128,640]{1,0:T(8,128)(2,1)} %param.28) | copy-start | bytes 491524
  0.7 16.0 %copy-start.15 = (bf16[64,640]{1,0:T(8,128)(2,1)S(1)}, bf16[64,640]{1,0:T(8,128)(2,1)}, u32[]{:S(2)}) copy-start(bf16[64,640]{1,0:T(8,128)(2,1)} %param.23) | copy-start | bytes 245764
  1.7 15.0 %collective-permute-start.2 = (bf16[1,40,2048]{2,1,0:T(8,128)(2,1)S(1)}, bf16[1,40,2048]{2,1,0:T(8,128)(2,1)S(1)}, u32[]{:S(2)}, u32[]{:S(2)}) collective-permute-start(bf16[1,40,2048]{2,1,0:T(8,128)(2,1)S(1)} %select_bitcast_fusion), channel_id=1, source_target_pairs={{0,16},{2,18},{4,20},{6,22},{8,24},{10,26},{12,28},{14,30},{16,0},... | collective-permute-start | bytes 491528 | tf_op jit(solution)/shard_map/ppermute | solution.py:25
  5.8 31.5 %collective-permute-start = (bf16[2,512,640]{2,1,0:T(8,128)(2,1)}, bf16[2,512,640]{2,1,0:T(8,128)(2,1)S(1)}, u32[]{:S(2)}, u32[]{:S(2)}) collective-permute-start(bf16[2,512,640]{2,1,0:T(8,128)(2,1)} %param.15), channel_id=1, source_target_pairs={{0,1},{2,3},{4,5},{6,7},{8,9},{10,11},{12,13},{14,15},{16,17},{18,... | collective-permute-start | bytes 3932168 | tf_op jit(solution)/shard_map/ppermute | solution.py:71
  16.3 15.4 %collective-permute-start.1 = (bf16[1,40,1792]{2,1,0:T(8,128)(2,1)S(1)}, bf16[1,40,1792]{2,1,0:T(8,128)(2,1)S(1)}, u32[]{:S(2)}, u32[]{:S(2)}) collective-permute-start(bf16[1,40,1792]{2,1,0:T(8,128)(2,1)S(1)} %bitcast.45), channel_id=1, source_target_pairs={{0,16},{2,18},{4,20},{6,22},{8,24},{10,26},{12,28},{14,30},{16,0},... | collective-permute-start | bytes 430088 | tf_op jit(solution)/shard_map/ppermute | solution.py:25
  16.8 19.1 %collective-permute-start.6 = (bf16[1,192,640]{2,1,0:T(8,128)(2,1)S(1)}, bf16[1,192,640]{2,1,0:T(8,128)(2,1)S(1)}, u32[]{:S(2)}, u32[]{:S(2)}) collective-permute-start(bf16[1,192,640]{2,1,0:T(8,128)(2,1)S(1)} %maximum_bitcast_fusion), channel_id=1, source_target_pairs={{0,16},{2,18},{4,20},{6,22},{8,24},{10,26},{12,28},{14,30},{16,0},... | collective-permute-start | bytes 737288 | tf_op jit(solution)/shard_map/ppermute | solution.py:25
  19.4 16.5 %collective-permute-start.4 = (bf16[2,40,2048]{2,1,0:T(8,128)(2,1)S(1)}, bf16[2,40,2048]{2,1,0:T(8,128)(2,1)S(1)}, u32[]{:S(2)}, u32[]{:S(2)}) collective-permute-start(bf16[2,40,2048]{2,1,0:T(8,128)(2,1)S(1)} %pad_maximum_fusion.8), channel_id=1, source_target_pairs={{0,8},{2,10},{4,12},{6,14},{8,0},{10,2},{12,4},{14,6},{16,24},{18,... | collective-permute-start | bytes 983048 | tf_op jit(solution)/shard_map/ppermute | solution.py:25
  31.8 10.3 %collective-permute-start.3 = (bf16[2,40,1792]{2,1,0:T(8,128)(2,1)S(1)}, bf16[2,40,1792]{2,1,0:T(8,128)(2,1)S(1)}, u32[]{:S(2)}, u32[]{:S(2)}) collective-permute-start(bf16[2,40,1792]{2,1,0:T(8,128)(2,1)S(1)} %pad_maximum_fusion.9), channel_id=1, source_target_pairs={{0,8},{2,10},{4,12},{6,14},{8,0},{10,2},{12,4},{14,6},{16,24},{18,... | collective-permute-start | bytes 860168 | tf_op jit(solution)/shard_map/ppermute | solution.py:25
  37.2 18.9 %copy-start.2 = (bf16[2,512,640]{2,1,0:T(8,128)(2,1)}, bf16[2,512,640]{2,1,0:T(8,128)(2,1)S(1)}, u32[]{:S(2)}) copy-start(bf16[2,512,640]{2,1,0:T(8,128)(2,1)S(1)} %collective-permute-done) | copy-start | bytes 3932164
  37.2 17.7 %collective-permute-start.7 = (bf16[4,40,2048]{2,1,0:T(8,128)(2,1)S(1)}, bf16[4,40,2048]{2,1,0:T(8,128)(2,1)S(1)}, u32[]{:S(2)}, u32[]{:S(2)}) collective-permute-start(bf16[4,40,2048]{2,1,0:T(8,128)(2,1)S(1)} %pad_maximum_fusion.4), channel_id=1, source_target_pairs={{0,4},{2,6},{4,0},{6,2},{8,12},{10,14},{12,8},{14,10},{16,20},{18,... | collective-permute-start | bytes 1966088 | tf_op jit(solution)/shard_map/ppermute | solution.py:25
  38.7 13.7 %collective-permute-start.8 = (bf16[2,192,640]{2,1,0:T(8,128)(2,1)S(1)}, bf16[2,192,640]{2,1,0:T(8,128)(2,1)S(1)}, u32[]{:S(2)}, u32[]{:S(2)}) collective-permute-start(bf16[2,192,640]{2,1,0:T(8,128)(2,1)S(1)} %pad_maximum_fusion.6), channel_id=1, source_target_pairs={{0,8},{2,10},{4,12},{6,14},{8,0},{10,2},{12,4},{14,6},{16,24},{18,... | collective-permute-start | bytes 1474568 | tf_op jit(solution)/shard_map/ppermute | solution.py:25
  42.1 22.7 %collective-permute-start.5 = (bf16[4,40,1792]{2,1,0:T(8,128)(2,1)S(1)}, bf16[4,40,1792]{2,1,0:T(8,128)(2,1)S(1)}, u32[]{:S(2)}, u32[]{:S(2)}) collective-permute-start(bf16[4,40,1792]{2,1,0:T(8,128)(2,1)S(1)} %pad_maximum_fusion.5), channel_id=1, source_target_pairs={{0,4},{2,6},{4,0},{6,2},{8,12},{10,14},{12,8},{14,10},{16,20},{18,... | collective-permute-start | bytes 1720328 | tf_op jit(solution)/shard_map/ppermute | solution.py:25
  52.5 3.6 %copy-start.8 = (bf16[2,192,640]{2,1,0:T(8,128)(2,1)}, bf16[2,192,640]{2,1,0:T(8,128)(2,1)S(1)}, u32[]{:S(2)}) copy-start(bf16[2,192,640]{2,1,0:T(8,128)(2,1)S(1)} %collective-permute-done.8) | copy-start | bytes 1474564
  64.9 4.1 %copy-start.3 = (bf16[8,40,1792]{2,1,0:T(8,128)(2,1)}, bf16[8,40,1792]{2,1,0:T(8,128)(2,1)S(1)}, u32[]{:S(2)}) copy-start(bf16[8,40,1792]{2,1,0:T(8,128)(2,1)S(1)} %pad_maximum_fusion.2.near_ref) | copy-start | bytes 3440644
  64.9 4.0 %collective-permute-start.9 = (bf16[8,40,1792]{2,1,0:T(8,128)(2,1)S(1)}, bf16[8,40,1792]{2,1,0:T(8,128)(2,1)S(1)}, u32[]{:S(2)}, u32[]{:S(2)}) collective-permute-start(bf16[8,40,1792]{2,1,0:T(8,128)(2,1)S(1)} %pad_maximum_fusion.2.near_ref), channel_id=1, source_target_pairs={{0,2},{2,0},{4,6},{6,4},{8,10},{10,8},{12,14},{14,12},{16,18},{18,... | collective-permute-start | bytes 3440648 | tf_op jit(solution)/shard_map/ppermute | solution.py:25
  65.0 24.6 %collective-permute-start.10 = (bf16[4,192,640]{2,1,0:T(8,128)(2,1)S(1)}, bf16[4,192,640]{2,1,0:T(8,128)(2,1)}, u32[]{:S(2)}, u32[]{:S(2)}) collective-permute-start(bf16[4,192,640]{2,1,0:T(8,128)(2,1)S(1)} %pad_maximum_fusion.3), channel_id=1, source_target_pairs={{0,4},{2,6},{4,0},{6,2},{8,12},{10,14},{12,8},{14,10},{16,20},{18,... | collective-permute-start | bytes 2949128 | tf_op jit(solution)/shard_map/ppermute | solution.py:25
  66.6 31.8 %collective-permute-start.13 = (bf16[8,40,2048]{2,1,0:T(8,128)(2,1)}, bf16[8,40,2048]{2,1,0:T(8,128)(2,1)}, u32[]{:S(2)}, u32[]{:S(2)}) collective-permute-start(bf16[8,40,2048]{2,1,0:T(8,128)(2,1)} %pad_maximum_fusion.1.mine_near), channel_id=1, source_target_pairs={{0,1},{1,0},{2,3},{3,2},{4,5},{5,4},{6,7},{7,6},{8,9},{9,8},{10,11... | collective-permute-start | bytes 3932168 | tf_op jit(solution)/shard_map/ppermute | solution.py:25
  79.3 10.4 %copy-start.9 = (bf16[2,192,640]{2,1,0:T(8,128)(2,1)S(1)}, bf16[2,192,640]{2,1,0:T(8,128)(2,1)}, u32[]{:S(2)}) copy-start(bf16[2,192,640]{2,1,0:T(8,128)(2,1)} %copy-done.8) | copy-start | bytes 1474564
  91.1 12.2 %copy-start = (bf16[8,192,640]{2,1,0:T(8,128)(2,1)}, bf16[8,192,640]{2,1,0:T(8,128)(2,1)S(1)}, u32[]{:S(2)}) copy-start(bf16[8,192,640]{2,1,0:T(8,128)(2,1)S(1)} %pad_maximum_fusion) | copy-start | bytes 5898244
  91.1 10.5 %collective-permute-start.11 = (bf16[8,192,640]{2,1,0:T(8,128)(2,1)S(1)}, bf16[8,192,640]{2,1,0:T(8,128)(2,1)S(1)}, u32[]{:S(2)}, u32[]{:S(2)}) collective-permute-start(bf16[8,192,640]{2,1,0:T(8,128)(2,1)S(1)} %pad_maximum_fusion), channel_id=1, source_target_pairs={{0,2},{2,0},{4,6},{6,4},{8,10},{10,8},{12,14},{14,12},{16,18},{18,... | collective-permute-start | bytes 5898248 | tf_op jit(solution)/shard_map/ppermute | solution.py:25
  91.2 7.2 %collective-permute-start.12 = (bf16[8,40,2048]{2,1,0:T(8,128)(2,1)}, bf16[8,40,2048]{2,1,0:T(8,128)(2,1)S(1)}, u32[]{:S(2)}, u32[]{:S(2)}) collective-permute-start(bf16[8,40,2048]{2,1,0:T(8,128)(2,1)} %pad_maximum_fusion.1.mine_near), channel_id=1, source_target_pairs={{0,2},{2,0},{4,6},{6,4},{8,10},{10,8},{12,14},{14,12},{16,18},{18,... | collective-permute-start | bytes 3932168 | tf_op jit(solution)/shard_map/ppermute | solution.py:25
  98.4 3.2 %collective-permute-start.14 = (bf16[8,40,2048]{2,1,0:T(8,128)(2,1)}, bf16[8,40,2048]{2,1,0:T(8,128)(2,1)S(1)}, u32[]{:S(2)}, u32[]{:S(2)}) collective-permute-start(bf16[8,40,2048]{2,1,0:T(8,128)(2,1)} %collective-permute-done.13.other_near), channel_id=1, source_target_pairs={{0,2},{2,0},{4,6},{6,4},{8,10},{10,8},{12,14},{14,12},{16,18},{18,... | collective-permute-start | bytes 3932168 | tf_op jit(solution)/shard_map/ppermute | solution.py:25
  98.4 4.9 %copy-start.10 = (bf16[8,40,2048]{2,1,0:T(8,128)(2,1)}, bf16[8,40,2048]{2,1,0:T(8,128)(2,1)S(1)}, u32[]{:S(2)}) copy-start(bf16[8,40,2048]{2,1,0:T(8,128)(2,1)S(1)} %collective-permute-done.12.mine_far) | copy-start | bytes 3932164
  101.6 1.7 copy-start.11
  173.9 11.0 %collective-permute-start.15 = (bf16[2,8,40,2048]{3,2,1,0:T(8,128)(2,1)}, bf16[2,8,40,2048]{3,2,1,0:T(8,128)(2,1)S(1)}, u32[]{:S(2)}, u32[]{:S(2)}) collective-permute-start(bf16[2,8,40,2048]{3,2,1,0:T(8,128)(2,1)} %get-tuple-element.101), channel_id=1, source_target_pairs={{0,2},{2,0},{4,6},{6,4},{8,10},{10,8},{12,14},{14,12},{16,18},{18,... | collective-permute-start | bytes 7864328 | tf_op jit(solution)/shard_map/ppermute | solution.py:25
  174.1 10.7 %collective-permute-start.16 = (bf16[8,2,96,640]{3,2,1,0:T(8,128)(2,1)}, bf16[8,2,96,640]{3,2,1,0:T(8,128)(2,1)}, u32[]{:S(2)}, u32[]{:S(2)}) collective-permute-start(bf16[8,2,96,640]{3,2,1,0:T(8,128)(2,1)} %get-tuple-element.102), channel_id=1, source_target_pairs={{0,2},{2,0},{4,6},{6,4},{8,10},{10,8},{12,14},{14,12},{16,18},{18,... | collective-permute-start | bytes 5898248 | tf_op jit(solution)/shard_map/ppermute | solution.py:25
  184.8 1.6 copy-start.5
  190.2 2.0 copy-start.7
  191.4 36.7 %collective-permute-start.18 = (bf16[2,1,2,2,40,2048]{5,4,3,2,1,0:T(8,128)(2,1)}, bf16[2,1,2,2,40,2048]{5,4,3,2,1,0:T(8,128)(2,1)}, u32[]{:S(2)}, u32[]{:S(2)}) collective-permute-start(bf16[2,1,2,2,40,2048]{5,4,3,2,1,0:T(8,128)(2,1)} %split.94), channel_id=1, source_target_pairs={{0,4},{2,6},{4,0},{6,2},{8,12},{10,14},{12,8},{14,10},{16,20},{18,... | collective-permute-start | bytes 3932168 | tf_op jit(solution)/shard_map/ppermute | solution.py:25
  196.7 29.9 %collective-permute-start.17 = (bf16[2,1,2,2,96,640]{5,4,3,2,1,0:T(8,128)(2,1)}, bf16[2,1,2,2,96,640]{5,4,3,2,1,0:T(8,128)(2,1)S(1)}, u32[]{:S(2)}, u32[]{:S(2)}) collective-permute-start(bf16[2,1,2,2,96,640]{5,4,3,2,1,0:T(8,128)(2,1)} %split.92), channel_id=1, source_target_pairs={{0,8},{2,10},{4,12},{6,14},{8,0},{10,2},{12,4},{14,6},{16,24},{18,... | collective-permute-start | bytes 2949128 | tf_op jit(solution)/shard_map/ppermute | solution.py:25
  228.0 2.0 copy-start.17
  228.0 4.8 %copy-start.13 = (bf16[8,40,1792]{2,1,0:T(8,128)(2,1)S(1)}, bf16[8,40,1792]{2,1,0:T(8,128)(2,1)}, u32[]{:S(2)}) copy-start(bf16[8,40,1792]{2,1,0:T(8,128)(2,1)} %get-tuple-element.125) | copy-start | bytes 3440644
  230.0 2.9 collective-permute-start.21
  233.2 2.9 copy-start.16
  233.3 15.9 %collective-permute-start.22 = (bf16[1,2,2,40,1792]{4,3,2,1,0:T(8,128)(2,1)S(1)}, bf16[1,2,2,40,1792]{4,3,2,1,0:T(8,128)(2,1)S(1)}, u32[]{:S(2)}, u32[]{:S(2)}) collective-permute-start(bf16[1,2,2,40,1792]{4,3,2,1,0:T(8,128)(2,1)S(1)} %bitcast.54), channel_id=1, source_target_pairs={{0,4},{2,6},{4,0},{6,2},{8,12},{10,14},{12,8},{14,10},{16,20},{18,... | collective-permute-start | bytes 1720328 | tf_op jit(solution)/shard_map/ppermute | solution.py:25
  234.6 16.6 %collective-permute-start.24 = (bf16[2,1,1,2,40,2048]{5,4,3,2,1,0:T(8,128)(2,1)S(1)}, bf16[2,1,1,2,40,2048]{5,4,3,2,1,0:T(8,128)(2,1)S(1)}, u32[]{:S(2)}, u32[]{:S(2)}) collective-permute-start(bf16[2,1,1,2,40,2048]{5,4,3,2,1,0:T(8,128)(2,1)S(1)} %split.102), channel_id=1, source_target_pairs={{0,8},{2,10},{4,12},{6,14},{8,0},{10,2},{12,4},{14,6},{16,24},{18,... | collective-permute-start | bytes 1966088 | tf_op jit(solution)/shard_map/ppermute | solution.py:25
  235.2 23.8 %collective-permute-start.20 = (bf16[1,1,2,2,96,640]{5,4,3,2,1,0:T(8,128)(2,1)S(1)}, bf16[1,1,2,2,96,640]{5,4,3,2,1,0:T(8,128)(2,1)S(1)}, u32[]{:S(2)}, u32[]{:S(2)}) collective-permute-start(bf16[1,1,2,2,96,640]{5,4,3,2,1,0:T(8,128)(2,1)S(1)} %split.96), channel_id=1, source_target_pairs={{0,4},{2,6},{4,0},{6,2},{8,12},{10,14},{12,8},{14,10},{16,20},{18,... | collective-permute-start | bytes 1474568 | tf_op jit(solution)/shard_map/ppermute | solution.py:25
  236.1 54.2 %collective-permute-start.19 = (bf16[1024,640]{1,0:T(8,128)(2,1)S(1)}, bf16[1024,640]{1,0:T(8,128)(2,1)S(1)}, u32[]{:S(2)}, u32[]{:S(2)}) collective-permute-start(bf16[1024,640]{1,0:T(8,128)(2,1)S(1)} %copy-done.16), channel_id=1, source_target_pairs={{1,0},{3,2},{5,4},{7,6},{9,8},{11,10},{13,12},{15,14},{17,16},{19,... | collective-permute-start | bytes 3932168 | tf_op jit(solution)/shard_map/ppermute | solution.py:71
  251.2 7.7 %collective-permute-start.23 = (bf16[1,1,2,40,1792]{4,3,2,1,0:T(8,128)(2,1)S(1)}, bf16[1,1,2,40,1792]{4,3,2,1,0:T(8,128)(2,1)S(1)}, u32[]{:S(2)}, u32[]{:S(2)}) collective-permute-start(bf16[1,1,2,40,1792]{4,3,2,1,0:T(8,128)(2,1)S(1)} %split.100), channel_id=1, source_target_pairs={{0,8},{2,10},{4,12},{6,14},{8,0},{10,2},{12,4},{14,6},{16,24},{18,... | collective-permute-start | bytes 860168 | tf_op jit(solution)/shard_map/ppermute | solution.py:25
  251.9 24.8 %collective-permute-start.26 = (bf16[1,1,1,2,40,2048]{5,4,3,2,1,0:T(8,128)(2,1)S(1)}, bf16[1,1,1,2,40,2048]{5,4,3,2,1,0:T(8,128)(2,1)S(1)}, u32[]{:S(2)}, u32[]{:S(2)}) collective-permute-start(bf16[1,1,1,2,40,2048]{5,4,3,2,1,0:T(8,128)(2,1)S(1)} %split.106), channel_id=1, source_target_pairs={{0,1},{1,0},{2,3},{3,2},{4,5},{5,4},{6,7},{7,6},{8,9},{9,8},{10,11... | collective-permute-start | bytes 983048 | tf_op jit(solution)/shard_map/ppermute | solution.py:25
  259.0 8.7 %collective-permute-start.27 = (bf16[1,1,1,40,1792]{4,3,2,1,0:T(8,128)(2,1)S(1)}, bf16[1,1,1,40,1792]{4,3,2,1,0:T(8,128)(2,1)S(1)}, u32[]{:S(2)}, u32[]{:S(2)}) collective-permute-start(bf16[1,1,1,40,1792]{4,3,2,1,0:T(8,128)(2,1)S(1)} %split.108), channel_id=1, source_target_pairs={{0,16},{2,18},{4,20},{6,22},{8,24},{10,26},{12,28},{14,30},{16,0},... | collective-permute-start | bytes 430088 | tf_op jit(solution)/shard_map/ppermute | solution.py:25
  259.6 22.2 %collective-permute-start.25 = (bf16[1,1,2,1,96,640]{5,4,3,2,1,0:T(8,128)(2,1)S(1)}, bf16[1,1,2,1,96,640]{5,4,3,2,1,0:T(8,128)(2,1)S(1)}, u32[]{:S(2)}, u32[]{:S(2)}) collective-permute-start(bf16[1,1,2,1,96,640]{5,4,3,2,1,0:T(8,128)(2,1)S(1)} %split.104), channel_id=1, source_target_pairs={{0,1},{1,0},{2,3},{3,2},{4,5},{5,4},{6,7},{7,6},{8,9},{9,8},{10,11... | collective-permute-start | bytes 737288 | tf_op jit(solution)/shard_map/ppermute | solution.py:25
  267.8 22.4 %copy-start.4 = (f32[1024,640]{1,0:T(8,128)S(1)}, f32[1024,640]{1,0:T(8,128)}, u32[]{:S(2)}) copy-start(f32[1024,640]{1,0:T(8,128)} %get-tuple-element.119) | copy-start | bytes 7864324
  267.8 15.5 %collective-permute-start.30 = (bf16[40,1792]{1,0:T(8,128)(2,1)S(1)}, bf16[40,1792]{1,0:T(8,128)(2,1)S(1)}, u32[]{:S(2)}, u32[]{:S(2)}) collective-permute-start(bf16[40,1792]{1,0:T(8,128)(2,1)S(1)} %bitcast.55), channel_id=1, source_target_pairs={{0,1},{1,0},{2,3},{3,2},{4,5},{5,4},{6,7},{7,6},{8,9},{9,8},{10,11... | collective-permute-start | bytes 430088 | tf_op jit(solution)/shard_map/ppermute | solution.py:25
  276.8 10.2 %collective-permute-start.29 = (bf16[1,1,1,1,40,2048]{5,4,3,2,1,0:T(8,128)(2,1)S(1)}, bf16[1,1,1,1,40,2048]{5,4,3,2,1,0:T(8,128)(2,1)S(1)}, u32[]{:S(2)}, u32[]{:S(2)}) collective-permute-start(bf16[1,1,1,1,40,2048]{5,4,3,2,1,0:T(8,128)(2,1)S(1)} %split.112), channel_id=1, source_target_pairs={{0,16},{2,18},{4,20},{6,22},{8,24},{10,26},{12,28},{14,30},{16,0},... | collective-permute-start | bytes 491528 | tf_op jit(solution)/shard_map/ppermute | solution.py:25
  281.8 8.3 %collective-permute-start.28 = (bf16[1,1,1,1,96,640]{5,4,3,2,1,0:T(8,128)(2,1)S(1)}, bf16[1,1,1,1,96,640]{5,4,3,2,1,0:T(8,128)(2,1)S(1)}, u32[]{:S(2)}, u32[]{:S(2)}) collective-permute-start(bf16[1,1,1,1,96,640]{5,4,3,2,1,0:T(8,128)(2,1)S(1)} %split.110), channel_id=1, source_target_pairs={{0,16},{2,18},{4,20},{6,22},{8,24},{10,26},{12,28},{14,30},{16,0},... | collective-permute-start | bytes 368648 | tf_op jit(solution)/shard_map/ppermute | solution.py:25
  287.0 5.7 %collective-permute-start.32 = (bf16[40,2048]{1,0:T(8,128)(2,1)S(1)}, bf16[40,2048]{1,0:T(8,128)(2,1)S(1)}, u32[]{:S(2)}, u32[]{:S(2)}) collective-permute-start(bf16[40,2048]{1,0:T(8,128)(2,1)S(1)} %bitcast.53), channel_id=1, source_target_pairs={{0,1},{1,0},{2,3},{3,2},{4,5},{5,4},{6,7},{7,6},{8,9},{9,8},{10,11... | collective-permute-start | bytes 491528 | tf_op jit(solution)/shard_map/ppermute | solution.py:25
  290.1 4.9 %collective-permute-start.31 = (bf16[96,640]{1,0:T(8,128)(2,1)S(1)}, bf16[96,640]{1,0:T(8,128)(2,1)S(1)}, u32[]{:S(2)}, u32[]{:S(2)}) collective-permute-start(bf16[96,640]{1,0:T(8,128)(2,1)S(1)} %fusion.3), channel_id=1, source_target_pairs={{0,1},{1,0},{2,3},{3,2},{4,5},{5,4},{6,7},{7,6},{8,9},{9,8},{10,11... | collective-permute-start | bytes 368648 | tf_op jit(solution)/shard_map/ppermute | solution.py:25
  (3 other events, 3.7 us)

commit v4 on v3

--- a/solution.py
+++ b/solution.py
@@ -55,6 +55,16 @@
 def folded(value, axis, mask, dim):
     kept, sent = jnp.split(value, 2, axis=dim)
     return kept, swap(sent, axis, mask)
+
+
+def first_fold(near, come, axis, mask, dim):
+    (near, near_sent), (come, come_sent) = (jnp.split(part, 2, axis=dim) for part in (near, come))
+    sent = add(near_sent, come_sent)
+    return (near, come), sent, swap(sent, axis, mask)
+
+
+def add_terms(terms, come):
+    return sum(term.astype(jnp.float32) for term in (*terms, come)).astype(jnp.bfloat16)
 
 
 def other_spans(value, axis):
@@ -670,7 +680,12 @@
         if step == len(chip_masks) - 1:
             mine_near = after(mine_near, tall_first, before)
         mine_near = widen(mine_near, "fsdp", mask)
-        first_near = widen(first_near, "fsdp", mask, mine_near)
+        if step == len(chip_masks) - 1:
+            mine_far = swap(mine_near, "fsdp", 1)
+            other_near = swap(mine_near, "ctx", 1)
+            first_near = widen(first_near, "fsdp", mask, mine_far)
+        else:
+            first_near = widen(first_near, "fsdp", mask, mine_near)
         if step == 0:
             tall_near = after(tall_near, mine_near)
         if step < len(chip_masks) - 1:
@@ -679,8 +694,6 @@
             tall_first = tall_near
     first_near = after(first_near, tall_near)
     first_far = swap(first_near, "fsdp", 1)
-    mine_far = swap(mine_near, "fsdp", 1)
-    other_near = swap(mine_near, "ctx", 1)
     tall_late = swap(tall_near, "fsdp", chip_masks[-1])
     total = sequences * span_len
     steps = total // ROWS
@@ -823,14 +836,16 @@
 
     back = attention_back(0, grad_attended, ())
     wide_far_sum, tall_far_sum = after((wide_far_sum, tall_far_sum), back[0])
-    wide = add(wide_grad_near, wide_far_sum)
-    tall = add(tall_grad_near, tall_far_sum)
     bits = (2,) * len(chip_masks)
-    wide = wide.reshape((2,) + bits + wide.shape[2:])
-    tall = tall.reshape(bits + tall.shape[1:])
-    wide_kept, wide_come = folded(wide, "fsdp", near_masks[0], 1)
-    tall_kept, tall_come = folded(tall, "fsdp", near_masks[1], 1)
-    wide, tall, grad_attended = lax.optimization_barrier((wide, tall, grad_attended))
+    wide_shape = (2,) + bits + wide_grad_near.shape[2:]
+    tall_shape = bits + tall_grad_near.shape[1:]
+    wide_kept, wide_sent, wide_come = first_fold(
+        wide_grad_near.reshape(wide_shape), wide_far_sum.reshape(wide_shape), "fsdp", near_masks[0], 1
+    )
+    tall_kept, tall_sent, tall_come = first_fold(
+        tall_grad_near.reshape(tall_shape), tall_far_sum.reshape(tall_shape), "fsdp", near_masks[1], 1
+    )
+    grad_attended = after(grad_attended, wide_sent, tall_sent)
     for sequence in range(1, sequences):
         back = attention_back(sequence, grad_attended, back)
     grad_query, grad_key, grad_value, key_send, value_send = back
@@ -881,16 +896,21 @@
         value_send,
         grad_middle,
     )
-    tall = add(tall_kept, after(tall_come, token_part))
-    wide = add(wide_kept, after(wide_come, token_part))
+    tall = add_terms(tall_kept, after(tall_come, token_part))
+    wide = add_terms(wide_kept, after(wide_come, token_part))
     first_grad_far, before_part = after((first_grad_far, before_part), tall, wide)
     tall_kept, tall_come = folded(tall, "fsdp", near_masks[0], 0)
     wide_kept, wide_come = folded(wide, "fsdp", near_masks[1], 2)
     before_come = shifted(before_part, "ctx", -1)
-    first = add(first_grad_near, swap(first_grad_far, "fsdp", 1))
-    first = first.reshape(bits + first.shape[1:])
-    first_kept, first_come = folded(first, "fsdp", near_masks[0], 0)
-    first = add(first_kept, first_come)
+    first_shape = bits + first_grad_near.shape[1:]
+    first_kept, _, first_come = first_fold(
+        first_grad_near.reshape(first_shape),
+        swap(first_grad_far, "fsdp", 1).reshape(first_shape),
+        "fsdp",
+        near_masks[0],
+        0,
+    )
+    first = add_terms(first_kept, first_come)
     first_kept, first_come = folded(first, "fsdp", near_masks[1], 1)
     wide = add(wide_kept, after(wide_come, first))
     wide_kept, wide_come = folded(wide, "ctx", 1, 0)

time: 300 us -> 310 us (1.033); the launches traced: 297 us -> 303 us
  waiting for transfers between devices: 94.7 us -> 108 us
  local copies, waits for them, and re-layouts: 13.4 us -> 7.95 us
    ppermute x2, waiting for transfers between devices: 1.19 us -> 8.12 us  [shifted(): lax.ppermute(value, axis, [(source, source + steps) for source in range(l...]
    ppermute x31, waiting for transfers between devices: 93.5 us -> 99.5 us  [swap(): lax.ppermute(value, axis, [(source, source ^ mask) for source in range(co...]
    convert_element_type x0 -> x3, other arithmetic: none -> 4.41 us  [add_terms(): sum((term.astype(jnp.float32) for term in (*terms, come)))]
    convert_element_type x13 -> x10, other arithmetic: 10.3 us -> 6.4 us  [add(): (left.astype(jnp.float32) + right.astype(jnp.float32)).astype(jnp.bfloat16)]
  transfers between devices with their start and end apart: 33 -> 33, of which waited for: 21 -> 23; matrix products, arithmetic and copies ran while one was open for 7% -> 6% of each run, Pallas kernels for 20% -> 19%
where the time goes in v4:
time: 310 us; the launch traced here: 303 us
  Pallas kernels  127 us (41%)
  waiting for transfers between devices  108 us (35%)
  starting transfers between devices  35.2 us (11%)
  other arithmetic  24.5 us (8%)
  local copies, waits for them, and re-layouts  7.95 us (3%)
    ppermute x31, waiting for transfers between devices, swap(): lax.ppermute(value, axis, [(source, source ^ mask) for source in range(co...  99.5 us
    pallas_call x1, Pallas kernels, per_device(): pl.pallas_call(functools.partial(middle_kernel, 512, down_rows), grid=(st...  68.3 us
    ppermute x31, starting transfers between devices, swap(): lax.ppermute(value, axis, [(source, source ^ mask) for source in range(co...  30.5 us
    pallas_call x2, Pallas kernels, attention_back(): pl.pallas_call(functools.partial(attention_back_kernel, score_scale), gri...  21 us
    pallas_call x1, Pallas kernels, per_device(): pl.pallas_call(functools.partial(head_back_kernel, head_dim), grid=(steps...  17.9 us
    pallas_call x1, Pallas kernels, per_device(): pl.pallas_call(functools.partial(attention_kernel, score_scale), grid=(se...  10.3 us
    pallas_call x1, Pallas kernels, per_device(): pl.pallas_call(functools.partial(projection_kernel, head_dim, qkv_columns...  9.27 us
    ppermute x2, waiting for transfers between devices, shifted(): lax.ppermute(value, axis, [(source, source + steps) for source in range(l...  8.12 us
  transfers between devices with their start and end apart: 33, of which 23 were waited for; matrix products, arithmetic and copies ran while one was open for 6% of the time, Pallas kernels for 19%

profile of v4, /device:TPU:0, one launch (start us, length us, event | category | flops | bytes accessed | tf_op | source)
XLA Modules:
  0.0 303.4 jit_solution(13708378929289215919)
XLA Ops:
  1.7 4.1 %collective-permute-start.2 = (bf16[1,40,2048]{2,1,0:T(8,128)(2,1)S(1)}, bf16[1,40,2048]{2,1,0:T(8,128)(2,1)S(1)}, u32[]{:S(2)}, u32[]{:S(2)}) collective-permute-start(bf16[1,40,2048]{2,1,0:T(8,128)(2,1)S(1)} %select_bitcast_fusion), channel_id=1, source_target_pairs={{0,16},{2,18},{4,20},{6,22},{8,24},{10,26},{12,28},{14,30},{16,0},... | collective-permute-start | bytes 491528 | tf_op jit(solution)/shard_map/ppermute | solution.py:25
  5.8 3.5 %collective-permute-start = (bf16[2,512,640]{2,1,0:T(8,128)(2,1)}, bf16[2,512,640]{2,1,0:T(8,128)(2,1)S(1)}, u32[]{:S(2)}, u32[]{:S(2)}) collective-permute-start(bf16[2,512,640]{2,1,0:T(8,128)(2,1)} %param.15), channel_id=1, source_target_pairs={{0,1},{2,3},{4,5},{6,7},{8,9},{10,11},{12,13},{14,15},{16,17},{18,... | collective-permute-start | bytes 3932168 | tf_op jit(solution)/shard_map/ppermute | solution.py:81
  11.0 2.5 collective-permute-done.2
  13.8 4.1 %collective-permute-start.4 = (bf16[2,40,2048]{2,1,0:T(8,128)(2,1)S(1)}, bf16[2,40,2048]{2,1,0:T(8,128)(2,1)S(1)}, u32[]{:S(2)}, u32[]{:S(2)}) collective-permute-start(bf16[2,40,2048]{2,1,0:T(8,128)(2,1)S(1)} %pad_maximum_fusion.8), channel_id=1, source_target_pairs={{0,8},{2,10},{4,12},{6,14},{8,0},{10,2},{12,4},{14,6},{16,24},{18,... | collective-permute-start | bytes 983048 | tf_op jit(solution)/shard_map/ppermute | solution.py:25
  18.0 9.1 %collective-permute-done.6 = bf16[1,192,640]{2,1,0:T(8,128)(2,1)S(1)} collective-permute-done((bf16[1,192,640]{2,1,0:T(8,128)(2,1)S(1)}, bf16[1,192,640]{2,1,0:T(8,128)(2,1)S(1)}, u32[]{:S(2)}, u32[]{:S(2)}) %collective-permute-start.6) | collective-permute-done | bytes 245792 | tf_op jit(solution)/shard_map/ppermute | solution.py:25
  27.1 2.0 collective-permute-done.4
  29.2 8.1 %collective-permute-done = bf16[2,512,640]{2,1,0:T(8,128)(2,1)S(1)} collective-permute-done((bf16[2,512,640]{2,1,0:T(8,128)(2,1)}, bf16[2,512,640]{2,1,0:T(8,128)(2,1)S(1)}, u32[]{:S(2)}, u32[]{:S(2)}) %collective-permute-start) | collective-permute-done | bytes 1310752 | tf_op jit(solution)/shard_map/ppermute | solution.py:81
  37.3 1.5 collective-permute-start.7
  40.3 3.0 multiply_sine_fusion
  43.6 7.7 %collective-permute-done.1 = bf16[1,40,1792]{2,1,0:T(8,128)(2,1)S(1)} collective-permute-done((bf16[1,40,1792]{2,1,0:T(8,128)(2,1)S(1)}, bf16[1,40,1792]{2,1,0:T(8,128)(2,1)S(1)}, u32[]{:S(2)}, u32[]{:S(2)}) %collective-permute-start.1) | collective-permute-done | bytes 143392 | tf_op jit(solution)/shard_map/ppermute | solution.py:25
  51.3 1.3 collective-permute-done.7
  53.8 1.6 collective-permute-start.3
  55.9 7.6 %collective-permute-done.3 = bf16[2,40,1792]{2,1,0:T(8,128)(2,1)S(1)} collective-permute-done((bf16[2,40,1792]{2,1,0:T(8,128)(2,1)S(1)}, bf16[2,40,1792]{2,1,0:T(8,128)(2,1)S(1)}, u32[]{:S(2)}, u32[]{:S(2)}) %collective-permute-start.3) | collective-permute-done | bytes 286752 | tf_op jit(solution)/shard_map/ppermute | solution.py:25
  63.6 1.6 collective-permute-start.5
  65.1 8.5 %collective-permute-done.9 = bf16[2,192,640]{2,1,0:T(8,128)(2,1)S(1)} collective-permute-done((bf16[2,192,640]{2,1,0:T(8,128)(2,1)S(1)}, bf16[2,192,640]{2,1,0:T(8,128)(2,1)S(1)}, u32[]{:S(2)}, u32[]{:S(2)}) %collective-permute-start.9) | collective-permute-done | bytes 491552 | tf_op jit(solution)/shard_map/ppermute | solution.py:25
  74.7 3.1 %collective-permute-done.5 = bf16[4,40,1792]{2,1,0:T(8,128)(2,1)S(1)} collective-permute-done((bf16[4,40,1792]{2,1,0:T(8,128)(2,1)S(1)}, bf16[4,40,1792]{2,1,0:T(8,128)(2,1)S(1)}, u32[]{:S(2)}, u32[]{:S(2)}) %collective-permute-start.5) | collective-permute-done | bytes 573472 | tf_op jit(solution)/shard_map/ppermute | solution.py:25
  78.1 1.6 collective-permute-start.11
  79.6 2.4 collective-permute-start.13
  83.1 9.3 %projection.1 = (bf16[1024,1024]{1,0:T(8,128)(2,1)}, bf16[1024,256]{1,0:T(8,128)(2,1)}, bf16[1024,256]{1,0:T(8,128)(2,1)}, bf16[1024,256]{1,0:T(8,128)(2,1)}, bf...) custom-call(bf16[1024,640]{1,0:T(8,128)(2,1)} %bitcast.36, ...), custom_call_target="tpu_custom_call" | custom-call | flops 2621440 | tf_op jit(solution)/shard_map/projection/pallas_call | solution.py:733
  92.3 10.3 %attention.1.att_ref = bf16[1024,1024]{1,0:T(8,128)(2,1)} custom-call(s32[19]{0:T(128)} %pad_add_fusion.info_ref.flag_ref, bf16[1024,1024]{1,0:T(8,128)(2,1)} %get-tuple-element.88.q_ref, bf16[1024,256]{1,0:T(8,128)(2,1)} %get-tuple-element.89.k_ref, bf16[1024,256]{1,0:T(8,128)(2,1)} %get-tuple-element.90.v_ref, bf16[1024,256]{1,0:T(8,128)(2,1)} %get-tuple-element.91.kb_ref, ...), custom_call_target="tpu_custom_call" | custom-call | flops 2808685 | tf_op jit(solution)/shard_map/attention/pallas_call | solution.py:748
  102.6 1.4 pad_maximum_fusion
  104.2 7.2 %collective-permute-done.13.other_near = bf16[8,40,2048]{2,1,0:T(8,128)(2,1)} collective-permute-done((bf16[8,40,2048]{2,1,0:T(8,128)(2,1)}, bf16[8,40,2048]{2,1,0:T(8,128)(2,1)}, u32[]{:S(2)}, u32[]{:S(2)}) %collective-permute-start.13) | collective-permute-done | bytes 1310752 | tf_op jit(solution)/shard_map/ppermute | solution.py:25
  111.4 3.2 %collective-permute-done.14.other_far = bf16[8,40,2048]{2,1,0:T(8,128)(2,1)S(1)} collective-permute-done((bf16[8,40,2048]{2,1,0:T(8,128)(2,1)}, bf16[8,40,2048]{2,1,0:T(8,128)(2,1)S(1)}, u32[]{:S(2)}, u32[]{:S(2)}) %collective-permute-start.14) | collective-permute-done | bytes 1310752 | tf_op jit(solution)/shard_map/ppermute | solution.py:25
  115.8 1.3 copy-done.5
  117.1 68.3 %middle.1 = (bf16[1024,640]{1,0:T(8,128)(2,1)}, f32[1024,640]{1,0:T(8,128)}, bf16[1024,1024]{1,0:T(8,128)(2,1)}, f32[8,640]{1,0:T(8,128)}, bf16[2,8,40,2048]{3,2...) custom-call(bf16[1024,640]{1,0:T(8,128)(2,1)} %bitcast.37, ...), custom_call_target="tpu_custom_call" | custom-call | flops 17203200 | tf_op jit(solution)/shard_map/middle/pallas_call | solution.py:774
  186.0 10.6 %attention_back.2 = (f32[1024,1024]{1,0:T(8,128)}, f32[1024,256]{1,0:T(8,128)}, f32[1024,256]{1,0:T(8,128)}, f32[1024,256]{1,0:T(8,128)}, f32[1024,256]{1,0:T(8,128)}) custom-call(s32[19]{0:T(128)} %pad_add_fusion.info_ref.flag_ref, bf16[1024,1024]{1,0:T(8,128)(2,1)} %get-tuple-element.88.q_ref, bf16[1024,256]{1,0:T(8,128)(2,1)} %get-tuple-element.89.k_ref, ...), custom_call_target="tpu_custom_call" | custom-call | flops 2457600 | tf_op jit(solution)/shard_map/attention_back/pallas_call | solution.py:825
  196.6 3.1 %add_convert_fusion.2 = bf16[2,1,2,2,40,2048]{5,4,3,2,1,0:T(8,128)(2,1)} fusion(bf16[2,2,2,2,40,2048]{5,4,3,2,1,0:T(8,128)(2,1)} %bitcast.19, bf16[2,2,2,2,40,2048]{5,4,3,2,1,0:T(8,128)(2,1)S(1)} %bitcast.43), kind=kLoop, calls=%fused_computation.2 | loop fusion | flops 2621440 | bytes 3932160 | tf_op jit(solution)/shard_map/convert_element_type | solution.py:52
  200.2 2.4 add_convert_fusion.4
  202.6 1.6 collective-permute-start.17
  204.2 10.4 %attention_back.3 = (f32[1024,1024]{1,0:T(8,128)}, f32[1024,256]{1,0:T(8,128)}, f32[1024,256]{1,0:T(8,128)}, f32[1024,256]{1,0:T(8,128)}, f32[1024,256]{1,0:T(8,128)}) custom-call(s32[19]{0:T(128)} %pad_add_fusion.info_ref.flag_ref, ...), custom_call_target="tpu_custom_call", output_to_operand_aliasing={{0}: (7, {}), {1}: (8, {}), {2}: (9, {}), {3}: (10, {}), {4... | custom-call | flops 2457600 | tf_op jit(solution)/shard_map/attention_back/pallas_call | solution.py:825
  214.6 17.9 %head_back.1 = (f32[1024,640]{1,0:T(8,128)}, bf16[1024,640]{1,0:T(8,128)(2,1)}, bf16[8,40,1792]{2,1,0:T(8,128)(2,1)}, bf16[8,40,1792]{2,1,0:T(8,128)(2,1)}) custom-call(bf16[1024,640]{1,0:T(8,128)(2,1)} %bitcast.38, bf16[1024,640]{1,0:T(8,128)(2,1)} %bitcast.41, bf16[640,1536]{1,0:T(8,128)(2,1)} %get-tuple-element.97.w_ref, ...), custom_call_target="tpu_custom_call" | custom-call | flops 5173894 | tf_op jit(solution)/shard_map/head_back/pallas_call | solution.py:852
  232.4 2.2 add_convert_fusion.3
  234.6 2.1 add_convert_fusion.1
  236.9 2.8 collective-permute-done.21
  239.9 1.6 collective-permute-start.22
  242.7 1.3 collective-permute-start.19
  244.0 11.8 %collective-permute-done.22 = bf16[1,2,2,40,1792]{4,3,2,1,0:T(8,128)(2,1)S(1)} collective-permute-done((bf16[1,2,2,40,1792]{4,3,2,1,0:T(8,128)(2,1)S(1)}, bf16[1,2,2,40,1792]{4,3,2,1,0:T(8,128)(2,1)S(1)}, u32[]{:S(2)}, u32[]{:S(2)}) %collective-permute-start.22) | collective-permute-done | bytes 573472 | tf_op jit(solution)/shard_map/ppermute | solution.py:25
  256.0 2.2 collective-permute-done.24
  258.8 1.8 collective-permute-start.26
  260.6 5.2 %collective-permute-done.23 = bf16[1,1,2,40,1792]{4,3,2,1,0:T(8,128)(2,1)S(1)} collective-permute-done((bf16[1,1,2,40,1792]{4,3,2,1,0:T(8,128)(2,1)S(1)}, bf16[1,1,2,40,1792]{4,3,2,1,0:T(8,128)(2,1)S(1)}, u32[]{:S(2)}, u32[]{:S(2)}) %collective-permute-start.23) | collective-permute-done | bytes 286752 | tf_op jit(solution)/shard_map/ppermute | solution.py:25
  266.5 1.8 collective-permute-start.25
  268.3 6.1 %collective-permute-done.27 = bf16[1,1,1,40,1792]{4,3,2,1,0:T(8,128)(2,1)S(1)} collective-permute-done((bf16[1,1,1,40,1792]{4,3,2,1,0:T(8,128)(2,1)S(1)}, bf16[1,1,1,40,1792]{4,3,2,1,0:T(8,128)(2,1)S(1)}, u32[]{:S(2)}, u32[]{:S(2)}) %collective-permute-start.27) | collective-permute-done | bytes 143392 | tf_op jit(solution)/shard_map/ppermute | solution.py:25
  274.4 1.8 collective-permute-start.30
  276.2 7.1 %collective-permute-done.26 = bf16[1,1,1,2,40,2048]{5,4,3,2,1,0:T(8,128)(2,1)S(1)} collective-permute-done((bf16[1,1,1,2,40,2048]{5,4,3,2,1,0:T(8,128)(2,1)S(1)}, bf16[1,1,1,2,40,2048]{5,4,3,2,1,0:T(8,128)(2,1)S(1)}, u32[]{:S(2)}, u32[]{:S(2)}) %collective-permute-start.26) | collective-permute-done | bytes 327712 | tf_op jit(solution)/shard_map/ppermute | solution.py:25
  283.9 4.6 %collective-permute-done.25 = bf16[1,1,2,1,96,640]{5,4,3,2,1,0:T(8,128)(2,1)S(1)} collective-permute-done((bf16[1,1,2,1,96,640]{5,4,3,2,1,0:T(8,128)(2,1)S(1)}, bf16[1,1,2,1,96,640]{5,4,3,2,1,0:T(8,128)(2,1)S(1)}, u32[]{:S(2)}, u32[]{:S(2)}) %collective-permute-start.25) | collective-permute-done | bytes 245792 | tf_op jit(solution)/shard_map/ppermute | solution.py:25
  293.8 3.0 collective-permute-done.28
  296.9 1.4 add_convert_fusion
  300.3 1.4 collective-permute-done.31
  (118 shorter events, 23.8 us)
Async XLA Ops:
  0.6 13.0 %copy-start.16 = (bf16[40]{0:T(256)(128)(2,1)S(1)}, bf16[40]{0:T(256)(128)(2,1)}, u32[]{:S(2)}) copy-start(bf16[40]{0:T(256)(128)(2,1)} %param.29) | copy-start | bytes 244
  0.7 13.0 %copy-start.15 = (bf16[40]{0:T(256)(128)(2,1)S(1)}, bf16[40]{0:T(256)(128)(2,1)}, u32[]{:S(2)}) copy-start(bf16[40]{0:T(256)(128)(2,1)} %param.25) | copy-start | bytes 244
  0.7 13.0 %copy-start.14 = (bf16[40]{0:T(256)(128)(2,1)S(1)}, bf16[40]{0:T(256)(128)(2,1)}, u32[]{:S(2)}) copy-start(bf16[40]{0:T(256)(128)(2,1)} %param.24) | copy-start | bytes 244
  0.7 13.0 %copy-start.13 = (bf16[40]{0:T(256)(128)(2,1)S(1)}, bf16[40]{0:T(256)(128)(2,1)}, u32[]{:S(2)}) copy-start(bf16[40]{0:T(256)(128)(2,1)} %param.17) | copy-start | bytes 244
  0.7 17.3 %copy-start.11 = (bf16[40,256]{1,0:T(8,128)(2,1)S(1)}, bf16[40,256]{1,0:T(8,128)(2,1)}, u32[]{:S(2)}) copy-start(bf16[40,256]{1,0:T(8,128)(2,1)} %param.20) | copy-start | bytes 61444
  0.7 17.2 %copy-start.12 = (bf16[40,256]{1,0:T(8,128)(2,1)S(1)}, bf16[40,256]{1,0:T(8,128)(2,1)}, u32[]{:S(2)}) copy-start(bf16[40,256]{1,0:T(8,128)(2,1)} %param.19) | copy-start | bytes 61444
  0.7 17.2 %copy-start.10 = (bf16[40,1024]{1,0:T(8,128)(2,1)S(1)}, bf16[40,1024]{1,0:T(8,128)(2,1)}, u32[]{:S(2)}) copy-start(bf16[40,1024]{1,0:T(8,128)(2,1)} %param.18) | copy-start | bytes 245764
  1.7 11.8 %collective-permute-start.2 = (bf16[1,40,2048]{2,1,0:T(8,128)(2,1)S(1)}, bf16[1,40,2048]{2,1,0:T(8,128)(2,1)S(1)}, u32[]{:S(2)}, u32[]{:S(2)}) collective-permute-start(bf16[1,40,2048]{2,1,0:T(8,128)(2,1)S(1)} %select_bitcast_fusion), channel_id=1, source_target_pairs={{0,16},{2,18},{4,20},{6,22},{8,24},{10,26},{12,28},{14,30},{16,0},... | collective-permute-start | bytes 491528 | tf_op jit(solution)/shard_map/ppermute | solution.py:25
  5.8 31.4 %collective-permute-start = (bf16[2,512,640]{2,1,0:T(8,128)(2,1)}, bf16[2,512,640]{2,1,0:T(8,128)(2,1)S(1)}, u32[]{:S(2)}, u32[]{:S(2)}) collective-permute-start(bf16[2,512,640]{2,1,0:T(8,128)(2,1)} %param.15), channel_id=1, source_target_pairs={{0,1},{2,3},{4,5},{6,7},{8,9},{10,11},{12,13},{14,15},{16,17},{18,... | collective-permute-start | bytes 3932168 | tf_op jit(solution)/shard_map/ppermute | solution.py:81
  13.6 13.5 %collective-permute-start.6 = (bf16[1,192,640]{2,1,0:T(8,128)(2,1)S(1)}, bf16[1,192,640]{2,1,0:T(8,128)(2,1)S(1)}, u32[]{:S(2)}, u32[]{:S(2)}) collective-permute-start(bf16[1,192,640]{2,1,0:T(8,128)(2,1)S(1)} %maximum_bitcast_fusion), channel_id=1, source_target_pairs={{0,16},{2,18},{4,20},{6,22},{8,24},{10,26},{12,28},{14,30},{16,0},... | collective-permute-start | bytes 737288 | tf_op jit(solution)/shard_map/ppermute | solution.py:25
  13.8 15.2 %collective-permute-start.4 = (bf16[2,40,2048]{2,1,0:T(8,128)(2,1)S(1)}, bf16[2,40,2048]{2,1,0:T(8,128)(2,1)S(1)}, u32[]{:S(2)}, u32[]{:S(2)}) collective-permute-start(bf16[2,40,2048]{2,1,0:T(8,128)(2,1)S(1)} %pad_maximum_fusion.8), channel_id=1, source_target_pairs={{0,8},{2,10},{4,12},{6,14},{8,0},{10,2},{12,4},{14,6},{16,24},{18,... | collective-permute-start | bytes 983048 | tf_op jit(solution)/shard_map/ppermute | solution.py:25
  37.3 16.5 %copy-start.1 = (bf16[2,512,640]{2,1,0:T(8,128)(2,1)}, bf16[2,512,640]{2,1,0:T(8,128)(2,1)S(1)}, u32[]{:S(2)}) copy-start(bf16[2,512,640]{2,1,0:T(8,128)(2,1)S(1)} %collective-permute-done) | copy-start | bytes 3932164
  37.3 15.3 %collective-permute-start.7 = (bf16[4,40,2048]{2,1,0:T(8,128)(2,1)S(1)}, bf16[4,40,2048]{2,1,0:T(8,128)(2,1)S(1)}, u32[]{:S(2)}, u32[]{:S(2)}) collective-permute-start(bf16[4,40,2048]{2,1,0:T(8,128)(2,1)S(1)} %pad_maximum_fusion.4), channel_id=1, source_target_pairs={{0,4},{2,6},{4,0},{6,2},{8,12},{10,14},{12,8},{14,10},{16,20},{18,... | collective-permute-start | bytes 1966088 | tf_op jit(solution)/shard_map/ppermute | solution.py:25
  43.3 8.0 %collective-permute-start.1 = (bf16[1,40,1792]{2,1,0:T(8,128)(2,1)S(1)}, bf16[1,40,1792]{2,1,0:T(8,128)(2,1)S(1)}, u32[]{:S(2)}, u32[]{:S(2)}) collective-permute-start(bf16[1,40,1792]{2,1,0:T(8,128)(2,1)S(1)} %bitcast.45), channel_id=1, source_target_pairs={{0,16},{2,18},{4,20},{6,22},{8,24},{10,26},{12,28},{14,30},{16,0},... | collective-permute-start | bytes 430088 | tf_op jit(solution)/shard_map/ppermute | solution.py:25
  53.8 24.1 %collective-permute-start.8 = (bf16[8,40,2048]{2,1,0:T(8,128)(2,1)}, bf16[8,40,2048]{2,1,0:T(8,128)(2,1)}, u32[]{:S(2)}, u32[]{:S(2)}) collective-permute-start(bf16[8,40,2048]{2,1,0:T(8,128)(2,1)} %pad_maximum_fusion.1.mine_near), channel_id=1, source_target_pairs={{0,2},{2,0},{4,6},{6,4},{8,10},{10,8},{12,14},{14,12},{16,18},{18,... | collective-permute-start | bytes 3932168 | tf_op jit(solution)/shard_map/ppermute | solution.py:25
  53.8 9.7 %collective-permute-start.3 = (bf16[2,40,1792]{2,1,0:T(8,128)(2,1)S(1)}, bf16[2,40,1792]{2,1,0:T(8,128)(2,1)S(1)}, u32[]{:S(2)}, u32[]{:S(2)}) collective-permute-start(bf16[2,40,1792]{2,1,0:T(8,128)(2,1)S(1)} %pad_maximum_fusion.9), channel_id=1, source_target_pairs={{0,8},{2,10},{4,12},{6,14},{8,0},{10,2},{12,4},{14,6},{16,24},{18,... | collective-permute-start | bytes 860168 | tf_op jit(solution)/shard_map/ppermute | solution.py:25
  55.4 18.2 %collective-permute-start.9 = (bf16[2,192,640]{2,1,0:T(8,128)(2,1)S(1)}, bf16[2,192,640]{2,1,0:T(8,128)(2,1)S(1)}, u32[]{:S(2)}, u32[]{:S(2)}) collective-permute-start(bf16[2,192,640]{2,1,0:T(8,128)(2,1)S(1)} %pad_maximum_fusion.6), channel_id=1, source_target_pairs={{0,8},{2,10},{4,12},{6,14},{8,0},{10,2},{12,4},{14,6},{16,24},{18,... | collective-permute-start | bytes 1474568 | tf_op jit(solution)/shard_map/ppermute | solution.py:25
  63.6 14.3 %collective-permute-start.5 = (bf16[4,40,1792]{2,1,0:T(8,128)(2,1)S(1)}, bf16[4,40,1792]{2,1,0:T(8,128)(2,1)S(1)}, u32[]{:S(2)}, u32[]{:S(2)}) collective-permute-start(bf16[4,40,1792]{2,1,0:T(8,128)(2,1)S(1)} %pad_maximum_fusion.5), channel_id=1, source_target_pairs={{0,4},{2,6},{4,0},{6,2},{8,12},{10,14},{12,8},{14,10},{16,20},{18,... | collective-permute-start | bytes 1720328 | tf_op jit(solution)/shard_map/ppermute | solution.py:25
  78.0 5.1 %copy-start.2 = (bf16[8,40,1792]{2,1,0:T(8,128)(2,1)}, bf16[8,40,1792]{2,1,0:T(8,128)(2,1)S(1)}, u32[]{:S(2)}) copy-start(bf16[8,40,1792]{2,1,0:T(8,128)(2,1)S(1)} %pad_maximum_fusion.2.near_ref) | copy-start | bytes 3440644
  78.0 4.0 %collective-permute-start.10 = (bf16[8,40,1792]{2,1,0:T(8,128)(2,1)S(1)}, bf16[8,40,1792]{2,1,0:T(8,128)(2,1)S(1)}, u32[]{:S(2)}, u32[]{:S(2)}) collective-permute-start(bf16[8,40,1792]{2,1,0:T(8,128)(2,1)S(1)} %pad_maximum_fusion.2.near_ref), channel_id=1, source_target_pairs={{0,2},{2,0},{4,6},{6,4},{8,10},{10,8},{12,14},{14,12},{16,18},{18,... | collective-permute-start | bytes 3440648 | tf_op jit(solution)/shard_map/ppermute | solution.py:25
  78.1 24.6 %collective-permute-start.11 = (bf16[4,192,640]{2,1,0:T(8,128)(2,1)}, bf16[4,192,640]{2,1,0:T(8,128)(2,1)}, u32[]{:S(2)}, u32[]{:S(2)}) collective-permute-start(bf16[4,192,640]{2,1,0:T(8,128)(2,1)} %pad_maximum_fusion.3), channel_id=1, source_target_pairs={{0,4},{2,6},{4,0},{6,2},{8,12},{10,14},{12,8},{14,10},{16,20},{18,... | collective-permute-start | bytes 2949128 | tf_op jit(solution)/shard_map/ppermute | solution.py:25
  79.6 31.8 %collective-permute-start.13 = (bf16[8,40,2048]{2,1,0:T(8,128)(2,1)}, bf16[8,40,2048]{2,1,0:T(8,128)(2,1)}, u32[]{:S(2)}, u32[]{:S(2)}) collective-permute-start(bf16[8,40,2048]{2,1,0:T(8,128)(2,1)} %pad_maximum_fusion.1.mine_near), channel_id=1, source_target_pairs={{0,1},{1,0},{2,3},{3,2},{4,5},{5,4},{6,7},{7,6},{8,9},{9,8},{10,11... | collective-permute-start | bytes 3932168 | tf_op jit(solution)/shard_map/ppermute | solution.py:25
  104.1 11.7 %copy-start = (bf16[8,192,640]{2,1,0:T(8,128)(2,1)}, bf16[8,192,640]{2,1,0:T(8,128)(2,1)S(1)}, u32[]{:S(2)}) copy-start(bf16[8,192,640]{2,1,0:T(8,128)(2,1)S(1)} %pad_maximum_fusion) | copy-start | bytes 5898244
  104.1 10.6 %collective-permute-start.12 = (bf16[8,192,640]{2,1,0:T(8,128)(2,1)S(1)}, bf16[8,192,640]{2,1,0:T(8,128)(2,1)S(1)}, u32[]{:S(2)}, u32[]{:S(2)}) collective-permute-start(bf16[8,192,640]{2,1,0:T(8,128)(2,1)S(1)} %pad_maximum_fusion), channel_id=1, source_target_pairs={{0,2},{2,0},{4,6},{6,4},{8,10},{10,8},{12,14},{14,12},{16,18},{18,... | collective-permute-start | bytes 5898248 | tf_op jit(solution)/shard_map/ppermute | solution.py:25
  111.4 3.2 %collective-permute-start.14 = (bf16[8,40,2048]{2,1,0:T(8,128)(2,1)}, bf16[8,40,2048]{2,1,0:T(8,128)(2,1)S(1)}, u32[]{:S(2)}, u32[]{:S(2)}) collective-permute-start(bf16[8,40,2048]{2,1,0:T(8,128)(2,1)} %collective-permute-done.13.other_near), channel_id=1, source_target_pairs={{0,2},{2,0},{4,6},{6,4},{8,10},{10,8},{12,14},{14,12},{16,18},{18,... | collective-permute-start | bytes 3932168 | tf_op jit(solution)/shard_map/ppermute | solution.py:25
  185.4 11.2 %collective-permute-start.15 = (bf16[2,8,40,2048]{3,2,1,0:T(8,128)(2,1)}, bf16[2,8,40,2048]{3,2,1,0:T(8,128)(2,1)}, u32[]{:S(2)}, u32[]{:S(2)}) collective-permute-start(bf16[2,8,40,2048]{3,2,1,0:T(8,128)(2,1)} %get-tuple-element.102), channel_id=1, source_target_pairs={{0,2},{2,0},{4,6},{6,4},{8,10},{10,8},{12,14},{14,12},{16,18},{18,... | collective-permute-start | bytes 7864328 | tf_op jit(solution)/shard_map/ppermute | solution.py:25
  185.7 10.9 %collective-permute-start.16 = (bf16[8,2,96,640]{3,2,1,0:T(8,128)(2,1)}, bf16[8,2,96,640]{3,2,1,0:T(8,128)(2,1)}, u32[]{:S(2)}, u32[]{:S(2)}) collective-permute-start(bf16[8,2,96,640]{3,2,1,0:T(8,128)(2,1)} %get-tuple-element.103), channel_id=1, source_target_pairs={{0,2},{2,0},{4,6},{6,4},{8,10},{10,8},{12,14},{14,12},{16,18},{18,... | collective-permute-start | bytes 5898248 | tf_op jit(solution)/shard_map/ppermute | solution.py:25
  186.0 10.6 %copy-start.4 = (bf16[2,8,40,2048]{3,2,1,0:T(8,128)(2,1)S(1)}, bf16[2,8,40,2048]{3,2,1,0:T(8,128)(2,1)}, u32[]{:S(2)}) copy-start(bf16[2,8,40,2048]{3,2,1,0:T(8,128)(2,1)} %get-tuple-element.101) | copy-start | bytes 7864324
  196.6 3.6 %copy-start.6 = (bf16[8,2,96,640]{3,2,1,0:T(8,128)(2,1)S(1)}, bf16[8,2,96,640]{3,2,1,0:T(8,128)(2,1)}, u32[]{:S(2)}) copy-start(bf16[8,2,96,640]{3,2,1,0:T(8,128)(2,1)} %get-tuple-element.106) | copy-start | bytes 5898244
  199.7 34.9 %collective-permute-start.18 = (bf16[2,1,2,2,40,2048]{5,4,3,2,1,0:T(8,128)(2,1)}, bf16[2,1,2,2,40,2048]{5,4,3,2,1,0:T(8,128)(2,1)S(1)}, u32[]{:S(2)}, u32[]{:S(2)}) collective-permute-start(bf16[2,1,2,2,40,2048]{5,4,3,2,1,0:T(8,128)(2,1)} %add_convert_fusion.2), channel_id=1, source_target_pairs={{0,4},{2,6},{4,0},{6,2},{8,12},{10,14},{12,8},{14,10},{16,20},{18,... | collective-permute-start | bytes 3932168 | tf_op jit(solution)/shard_map/ppermute | solution.py:25
  202.6 29.8 %collective-permute-start.17 = (bf16[2,1,2,2,96,640]{5,4,3,2,1,0:T(8,128)(2,1)}, bf16[2,1,2,2,96,640]{5,4,3,2,1,0:T(8,128)(2,1)}, u32[]{:S(2)}, u32[]{:S(2)}) collective-permute-start(bf16[2,1,2,2,96,640]{5,4,3,2,1,0:T(8,128)(2,1)} %add_convert_fusion.4), channel_id=1, source_target_pairs={{0,8},{2,10},{4,12},{6,14},{8,0},{10,2},{12,4},{14,6},{16,24},{18,... | collective-permute-start | bytes 2949128 | tf_op jit(solution)/shard_map/ppermute | solution.py:25
  234.6 5.0 %copy-start.9 = (bf16[8,40,1792]{2,1,0:T(8,128)(2,1)S(1)}, bf16[8,40,1792]{2,1,0:T(8,128)(2,1)}, u32[]{:S(2)}) copy-start(bf16[8,40,1792]{2,1,0:T(8,128)(2,1)} %get-tuple-element.125) | copy-start | bytes 3440644
  236.8 2.9 collective-permute-start.21
  239.9 2.8 copy-start.17
  239.9 15.9 %collective-permute-start.22 = (bf16[1,2,2,40,1792]{4,3,2,1,0:T(8,128)(2,1)S(1)}, bf16[1,2,2,40,1792]{4,3,2,1,0:T(8,128)(2,1)S(1)}, u32[]{:S(2)}, u32[]{:S(2)}) collective-permute-start(bf16[1,2,2,40,1792]{4,3,2,1,0:T(8,128)(2,1)S(1)} %bitcast.56), channel_id=1, source_target_pairs={{0,4},{2,6},{4,0},{6,2},{8,12},{10,14},{12,8},{14,10},{16,20},{18,... | collective-permute-start | bytes 1720328 | tf_op jit(solution)/shard_map/ppermute | solution.py:25
  241.6 16.6 %collective-permute-start.24 = (bf16[2,1,1,2,40,2048]{5,4,3,2,1,0:T(8,128)(2,1)S(1)}, bf16[2,1,1,2,40,2048]{5,4,3,2,1,0:T(8,128)(2,1)S(1)}, u32[]{:S(2)}, u32[]{:S(2)}) collective-permute-start(bf16[2,1,1,2,40,2048]{5,4,3,2,1,0:T(8,128)(2,1)S(1)} %split.127), channel_id=1, source_target_pairs={{0,8},{2,10},{4,12},{6,14},{8,0},{10,2},{12,4},{14,6},{16,24},{18,... | collective-permute-start | bytes 1966088 | tf_op jit(solution)/shard_map/ppermute | solution.py:25
  242.1 23.8 %collective-permute-start.20 = (bf16[1,1,2,2,96,640]{5,4,3,2,1,0:T(8,128)(2,1)S(1)}, bf16[1,1,2,2,96,640]{5,4,3,2,1,0:T(8,128)(2,1)S(1)}, u32[]{:S(2)}, u32[]{:S(2)}) collective-permute-start(bf16[1,1,2,2,96,640]{5,4,3,2,1,0:T(8,128)(2,1)S(1)} %split.121), channel_id=1, source_target_pairs={{0,4},{2,6},{4,0},{6,2},{8,12},{10,14},{12,8},{14,10},{16,20},{18,... | collective-permute-start | bytes 1474568 | tf_op jit(solution)/shard_map/ppermute | solution.py:25
  242.7 54.2 %collective-permute-start.19 = (bf16[1024,640]{1,0:T(8,128)(2,1)S(1)}, bf16[1024,640]{1,0:T(8,128)(2,1)S(1)}, u32[]{:S(2)}, u32[]{:S(2)}) collective-permute-start(bf16[1024,640]{1,0:T(8,128)(2,1)S(1)} %copy-done.17), channel_id=1, source_target_pairs={{1,0},{3,2},{5,4},{7,6},{9,8},{11,10},{13,12},{15,14},{17,16},{19,... | collective-permute-start | bytes 3932168 | tf_op jit(solution)/shard_map/ppermute | solution.py:81
  258.1 7.7 %collective-permute-start.23 = (bf16[1,1,2,40,1792]{4,3,2,1,0:T(8,128)(2,1)S(1)}, bf16[1,1,2,40,1792]{4,3,2,1,0:T(8,128)(2,1)S(1)}, u32[]{:S(2)}, u32[]{:S(2)}) collective-permute-start(bf16[1,1,2,40,1792]{4,3,2,1,0:T(8,128)(2,1)S(1)} %split.125), channel_id=1, source_target_pairs={{0,8},{2,10},{4,12},{6,14},{8,0},{10,2},{12,4},{14,6},{16,24},{18,... | collective-permute-start | bytes 860168 | tf_op jit(solution)/shard_map/ppermute | solution.py:25
  258.8 24.5 %collective-permute-start.26 = (bf16[1,1,1,2,40,2048]{5,4,3,2,1,0:T(8,128)(2,1)S(1)}, bf16[1,1,1,2,40,2048]{5,4,3,2,1,0:T(8,128)(2,1)S(1)}, u32[]{:S(2)}, u32[]{:S(2)}) collective-permute-start(bf16[1,1,1,2,40,2048]{5,4,3,2,1,0:T(8,128)(2,1)S(1)} %split.131), channel_id=1, source_target_pairs={{0,1},{1,0},{2,3},{3,2},{4,5},{5,4},{6,7},{7,6},{8,9},{9,8},{10,11... | collective-permute-start | bytes 983048 | tf_op jit(solution)/shard_map/ppermute | solution.py:25
  266.0 8.4 %collective-permute-start.27 = (bf16[1,1,1,40,1792]{4,3,2,1,0:T(8,128)(2,1)S(1)}, bf16[1,1,1,40,1792]{4,3,2,1,0:T(8,128)(2,1)S(1)}, u32[]{:S(2)}, u32[]{:S(2)}) collective-permute-start(bf16[1,1,1,40,1792]{4,3,2,1,0:T(8,128)(2,1)S(1)} %split.133), channel_id=1, source_target_pairs={{0,16},{2,18},{4,20},{6,22},{8,24},{10,26},{12,28},{14,30},{16,0},... | collective-permute-start | bytes 430088 | tf_op jit(solution)/shard_map/ppermute | solution.py:25
  266.5 21.9 %collective-permute-start.25 = (bf16[1,1,2,1,96,640]{5,4,3,2,1,0:T(8,128)(2,1)S(1)}, bf16[1,1,2,1,96,640]{5,4,3,2,1,0:T(8,128)(2,1)S(1)}, u32[]{:S(2)}, u32[]{:S(2)}) collective-permute-start(bf16[1,1,2,1,96,640]{5,4,3,2,1,0:T(8,128)(2,1)S(1)} %split.129), channel_id=1, source_target_pairs={{0,1},{1,0},{2,3},{3,2},{4,5},{5,4},{6,7},{7,6},{8,9},{9,8},{10,11... | collective-permute-start | bytes 737288 | tf_op jit(solution)/shard_map/ppermute | solution.py:25
  274.4 15.5 %collective-permute-start.30 = (bf16[40,1792]{1,0:T(8,128)(2,1)S(1)}, bf16[40,1792]{1,0:T(8,128)(2,1)S(1)}, u32[]{:S(2)}, u32[]{:S(2)}) collective-permute-start(bf16[40,1792]{1,0:T(8,128)(2,1)S(1)} %bitcast.55), channel_id=1, source_target_pairs={{0,1},{1,0},{2,3},{3,2},{4,5},{5,4},{6,7},{7,6},{8,9},{9,8},{10,11... | collective-permute-start | bytes 430088 | tf_op jit(solution)/shard_map/ppermute | solution.py:25
  283.5 10.2 %collective-permute-start.29 = (bf16[1,1,1,1,40,2048]{5,4,3,2,1,0:T(8,128)(2,1)S(1)}, bf16[1,1,1,1,40,2048]{5,4,3,2,1,0:T(8,128)(2,1)S(1)}, u32[]{:S(2)}, u32[]{:S(2)}) collective-permute-start(bf16[1,1,1,1,40,2048]{5,4,3,2,1,0:T(8,128)(2,1)S(1)} %split.137), channel_id=1, source_target_pairs={{0,16},{2,18},{4,20},{6,22},{8,24},{10,26},{12,28},{14,30},{16,0},... | collective-permute-start | bytes 491528 | tf_op jit(solution)/shard_map/ppermute | solution.py:25
  288.4 8.5 %copy-start.3 = (f32[1024,640]{1,0:T(8,128)S(1)}, f32[1024,640]{1,0:T(8,128)}, u32[]{:S(2)}) copy-start(f32[1024,640]{1,0:T(8,128)} %get-tuple-element.119) | copy-start | bytes 7864324
  288.5 8.3 %collective-permute-start.28 = (bf16[1,1,1,1,96,640]{5,4,3,2,1,0:T(8,128)(2,1)S(1)}, bf16[1,1,1,1,96,640]{5,4,3,2,1,0:T(8,128)(2,1)S(1)}, u32[]{:S(2)}, u32[]{:S(2)}) collective-permute-start(bf16[1,1,1,1,96,640]{5,4,3,2,1,0:T(8,128)(2,1)S(1)} %split.135), channel_id=1, source_target_pairs={{0,16},{2,18},{4,20},{6,22},{8,24},{10,26},{12,28},{14,30},{16,0},... | collective-permute-start | bytes 368648 | tf_op jit(solution)/shard_map/ppermute | solution.py:25
  293.7 5.7 %collective-permute-start.32 = (bf16[40,2048]{1,0:T(8,128)(2,1)S(1)}, bf16[40,2048]{1,0:T(8,128)(2,1)S(1)}, u32[]{:S(2)}, u32[]{:S(2)}) collective-permute-start(bf16[40,2048]{1,0:T(8,128)(2,1)S(1)} %bitcast.54), channel_id=1, source_target_pairs={{0,1},{1,0},{2,3},{3,2},{4,5},{5,4},{6,7},{7,6},{8,9},{9,8},{10,11... | collective-permute-start | bytes 491528 | tf_op jit(solution)/shard_map/ppermute | solution.py:25
  296.8 4.9 %collective-permute-start.31 = (bf16[96,640]{1,0:T(8,128)(2,1)S(1)}, bf16[96,640]{1,0:T(8,128)(2,1)S(1)}, u32[]{:S(2)}, u32[]{:S(2)}) collective-permute-start(bf16[96,640]{1,0:T(8,128)(2,1)S(1)} %fusion.2), channel_id=1, source_target_pairs={{0,1},{1,0},{2,3},{3,2},{4,5},{5,4},{6,7},{7,6},{8,9},{9,8},{10,11... | collective-permute-start | bytes 368648 | tf_op jit(solution)/shard_map/ppermute | solution.py:25
  (4 other events, 5.6 us)
